TPU v7x, 768 devices: a whole 4x8x12 slice. The times are simulated.
768 devices in a mesh: rep: 16 (over x_lo, y), shard: 48 (over x_hi, z, core).
Axes of the slice: x: 4 (x_hi: 2, x_lo: 2; x = x_hi * 2 + x_lo), y: 8, z: 12, core: 2. Of those that a mesh axis runs over, the one named last changes fastest.
Arguments:
- bag_ids: int32 [49152, 20], P(('rep', 'shard')), may hold values from 0 to 24575
- table: float32 [24576, 256], P('shard'), may hold values from -1.2 to 1.2
- accum: float32 [24576], P('shard'), may hold values from 0.01 to 0.1
- cross_weight: float32 [256, 256], replicated, may hold values from -0.375 to 0.375
- cross_bias: float32 [256], replicated, may hold values from -4 to 4
- upstream: float32 [49152, 256], P(('rep', 'shard')), may hold values from -6 to 6
Outputs:
- crossed: float32 [49152, 256], P(('rep', 'shard'))
- new_table: float32 [24576, 256], P('shard')
- new_accum: float32 [24576], P('shard')
All inputs are finite; a program needn't handle non-finite values.
Results may differ from a plain program's by a relative error of at most 0.00014.
Values sent between devices are 32-bit elements; how exact they have to be, the bound alone decides.
No kernel may reach another device: no remote copies, remote signals or barrier semaphores. Data moves between devices by JAX's collectives and lax.ppermute only.
A program may use at most 64 MiB of HBM per device.

v0:
```python
import jax
import jax.numpy as jnp
from jax import lax
from jax.sharding import PartitionSpec as P


def adagrad_rows(rows, sums, grads):
    fresh = sums + jnp.mean(grads * grads, axis=1)
    return (rows - 0.5 * grads / jnp.sqrt(fresh)[:, None], fresh)


def count_block(spill_ids, count, rows_owned):
    sample_pos = lax.broadcasted_iota(jnp.int32, spill_ids.shape, 0)
    flat_index = (sample_pos * (rows_owned + 1) + spill_ids).reshape(-1)
    ones_flat = jnp.ones(flat_index.shape, jnp.float32)
    counted = jax.ops.segment_sum(ones_flat, flat_index, num_segments=count * (rows_owned + 1))
    return counted.reshape(count, rows_owned + 1)[:, :rows_owned]


def body(bag_ids, table, accum, cross_weight, cross_bias, upstream):
    per_device = bag_ids.shape[0]
    rows_owned = table.shape[0]
    first_row = lax.axis_index("shard") * rows_owned
    group_ids = lax.all_gather(bag_ids, "shard", axis=0, tiled=True)
    local_ids = group_ids - first_row
    owned = (local_ids >= 0) & (local_ids < rows_owned)
    spill_ids = jnp.where(owned, local_ids, rows_owned)
    counts = count_block(spill_ids, lax.axis_size("shard") * per_device, rows_owned)
    pooled = lax.psum_scatter(
        jnp.dot(counts, table, precision=lax.Precision.HIGHEST),
        "shard",
        scatter_dimension=0,
        tiled=True,
    )
    mixed = jnp.dot(pooled, cross_weight, precision=lax.Precision.HIGHEST) + cross_bias
    crossed = pooled * mixed + pooled
    back = (
        upstream * mixed
        + jnp.dot(upstream * pooled, cross_weight.T, precision=lax.Precision.HIGHEST)
        + upstream
    )
    piece = lax.all_gather(back, "shard", axis=0, tiled=True)
    counts = count_block(spill_ids, piece.shape[0], rows_owned)
    added = lax.dot_general(
        counts, piece, (((0,), (0,)), ((), ())), precision=lax.Precision.HIGHEST
    )
    totals = lax.psum(added, "rep")
    new_table, new_accum = adagrad_rows(table, accum, totals)
    return (crossed, new_table, new_accum)


def solution(mesh):
    placed = (
        P(("rep", "shard"), None),
        P("shard", None),
        P("shard"),
        P(),
        P(),
        P(("rep", "shard"), None),
    )
    return jax.shard_map(
        body,
        mesh=mesh,
        in_specs=placed,
        out_specs=(P(("rep", "shard"), None), P("shard", None), P("shard")),
        check_vma=False,
    )
```

profile of v0, /device:TPU:4, one launch (start us, length us, event | category | flops | bytes accessed | tf_op | source)
XLA Modules:
  0.0 979.3 jit_solution(10714853281412989330)
XLA Ops:
  7.2 0.0 copy-start
  7.2 0.0 reduce-scatter.2.cloned.1.call-start
  7.2 68.3 %all-gather = s32[48,64,20]{1,2,0:T(8,128)S(1)} all-gather(s32[1,64,20]{1,2,0:T(8,128)} %bitcast.8), channel_id=1, replica_groups=mesh['rep'=16,'shard'=48] {'shard'}, dimensions={0}, use_global_device_ids=true | all-gather | bytes 250880 | tf_op jit(solution)/shard_map/all_gather | solution.py:24
  75.5 0.1 copy_subtract_fusion
  75.6 0.2 reshape.25
  75.8 0.1 select_add_fusion
  75.9 0.5 copy.14
  76.4 1.4 reshape.15
  77.8 419.0 %scatter_custom_fusion = f32[1575936]{0:T(1024)} fusion(s32[61440]{0:T(1024)S(1)} %reshape.15, f32[61440]{0:T(1024)S(1)} %broadcast.17, f32[]{:T(128)} %constant.8.clone.1), kind=kCustom, calls=%fused_computation.5 | custom fusion | flops 61440 | bytes 6303748 | tf_op jit(solution)/shard_map/scatter-add | solution.py:16
  496.8 0.0 copy-start.1
  496.8 9.6 reshape.12
  506.4 0.0 copy-done.1
  506.4 8.3 fusion.2
  514.8 0.0 reduce-scatter.2.cloned.1.call-update
  514.8 0.0 all-gather.3.cloned.1.call-start
  514.9 173.3 %reduce-scatter.2.cloned.1.call-done = f32[64,256]{1,0:T(8,128)} async-done(((f32[3072,256]{1,0:T(8,128)}), f32[64,256]{1,0:T(8,128)}) %reduce-scatter.2.cloned.1.call-update) | async-done | bytes 65552 | tf_op jit(solution)/shard_map/reduce_scatter | solution.py:29
  688.1 0.0 copy-done
  688.1 0.0 copy-done.4
  688.1 1.8 multiply_add_fusion
  689.9 0.0 copy-done.2
  689.9 1.8 fusion.6
  691.8 0.0 all-gather.3.cloned.1.call-update
  691.8 0.0 copy-start.3
  691.8 0.2 all-reduce.2.cloned.1.call-start
  692.0 118.7 %all-gather.3.cloned.1.call-done = f32[3072,256]{1,0:T(8,128)} async-done(((f32[64,256]{1,0:T(8,128)}), f32[3072,256]{1,0:T(8,128)}) %all-gather.3.cloned.1.call-update) | async-done | bytes 3145744 | tf_op jit(solution)/shard_map/all_gather | solution.py:42
  810.7 13.8 %fusion = f32[512,256]{1,0:T(8,128)} fusion(f32[3072,256]{1,0:T(8,128)} %all-gather.3.cloned.1.call-done, f32[3072,513]{1,0:T(8,128)} %reshape.12), kind=kOutput, calls=%fused_computation.1 | convolution fusion | flops 4831838208 | bytes 9961472 | tf_op jit(solution)/shard_map/dot_general | solution.py:44
  824.5 0.0 all-reduce.2.cloned.1.call-update
  824.6 144.4 %all-reduce.2.cloned.1.call-done = f32[512,256]{1,0:T(8,128)} async-done(((f32[512,256]{1,0:T(8,128)}), f32[512,256]{1,0:T(8,128)}) %all-reduce.2.cloned.1.call-update) | async-done | bytes 524304 | tf_op jit(solution)/shard_map/psum | solution.py:47
  969.0 1.2 multiply_reduce_fusion
  970.2 0.0 copy-done.3
  970.2 0.6 fusion.8
  970.8 2.0 divide_subtract_fusion
  (4 shorter events, 0.0 us)
Async XLA Ops:
  7.2 681.0 %copy-start = (f32[256,256]{1,0:T(8,128)S(1)}, f32[256,256]{1,0:T(8,128)}, u32[]{:S(2)}) copy-start(f32[256,256]{1,0:T(8,128)} %param.9) | copy-start | bytes 786436
  7.2 680.9 %reduce-scatter.2.cloned.1.call-start = ((), (), s32[]{:S(2)}) async-start(), calls=%async_computation.1 | async-start | bytes 3211264 | tf_op jit(solution)/shard_map/reduce_scatter | solution.py:29
  496.8 9.6 copy-start.1
  506.4 181.7 %copy-start.4 = (f32[256]{0:T(256)S(1)}, f32[256]{0:T(256)}, u32[]{:S(2)}) copy-start(f32[256]{0:T(256)} %param.10) | copy-start | bytes 3076
  506.4 183.5 %copy-start.2 = (f32[64,256]{1,0:T(8,128)S(1)}, f32[64,256]{1,0:T(8,128)}, u32[]{:S(2)}) copy-start(f32[64,256]{1,0:T(8,128)} %param.11) | copy-start | bytes 196612
  514.8 295.9 %all-gather.3.cloned.1.call-start = ((), (), s32[]{:S(2)}) async-start(), calls=%async_computation.2 | async-start | bytes 3211264 | tf_op jit(solution)/shard_map/all_gather | solution.py:42
  691.8 278.4 %copy-start.3 = (f32[512]{0:T(512)S(1)}, f32[512]{0:T(512)}, u32[]{:S(2)}) copy-start(f32[512]{0:T(512)} %param.8) | copy-start | bytes 6148
  691.8 277.2 %all-reduce.2.cloned.1.call-start = ((), (), s32[]{:S(2)}) async-start(), calls=%async_computation.3 | async-start | bytes 1048576 | tf_op jit(solution)/shard_map/psum | solution.py:47
Sparse Core Ops, SparseCore 0:
  514.9 173.1 reduce-scatter.1
  692.4 118.3 all-gather.2
  824.7 144.2 all-reduce.1
where the time goes:
time: 980 us; the launch traced here: 979 us
  waiting for transfers between devices  436 us (44%)
  other arithmetic  423 us (43%)
  blocking collectives  68.3 us (7%)
  matrix products  25.8 us (3%)
  between operations  13.8 us (1%)
  local copies, waits for them, and re-layouts  11.7 us (1%)
    scatter-add x1, other arithmetic, count_block(): jax.ops.segment_sum(ones_flat, flat_index, num_segments=count * (rows_own...  419 us
    reduce_scatter x1, waiting for transfers between devices, body(): lax.psum_scatter(jnp.dot(counts, table, precision=lax.Precision.HIGHEST),...  173 us
    psum x1, waiting for transfers between devices, body(): totals = lax.psum(added, 'rep')  144 us
    all_gather x1, waiting for transfers between devices, body(): piece = lax.all_gather(back, 'shard', axis=0, tiled=True)  119 us
    all_gather x1, blocking collectives, body(): group_ids = lax.all_gather(bag_ids, 'shard', axis=0, tiled=True)  68.3 us
  transfers between devices with their start and end apart: 3, of which 3 were waited for; matrix products, arithmetic and copies ran while one was open for 0% of the time, Pallas kernels for 0%

commit v1 on v0

v1 whole, which is shorter than its diff:
```python
import jax
import jax.numpy as jnp
from jax import lax
from jax.experimental import pallas as pl
from jax.experimental.pallas import tpu as pltpu
from jax.sharding import Mesh
from jax.sharding import PartitionSpec as P

AXES = ("xl", "y", "xh", "z", "c")
SIZES = (2, 8, 2, 12, 2)
NZ = 12
LANES = 128
VMEM_LIMIT = 48 * 1024 * 1024


def split_halves(x):
    high = x.astype(jnp.bfloat16)
    return high, (x - high.astype(jnp.float32)).astype(jnp.bfloat16)


def count_kernel(base_ref, ids_ref, out_ref):
    bag = ids_ref.shape[1]
    rows = out_ref.shape[0] // 4
    ids = jnp.concatenate([ids_ref[0], ids_ref[1]], axis=1)
    word = ids & (LANES - 1)
    values = []
    for q in range(4):
        local = ids - base_ref[q]
        inside = (local >= 0) & (local < rows)
        values.append(jnp.where(inside, jnp.int32(1) << ((local & (rows - 1)) >> 7) * 8, 0))
    part = 32
    for first in range(0, LANES, part):
        lines = lax.broadcasted_iota(jnp.int32, (part, LANES), 0) + first
        sums = [jnp.zeros((part, LANES), jnp.int32) for _ in range(4)]
        for j in range(bag):
            hit = word[j : j + 1] == lines
            for q in range(4):
                sums[q] = sums[q] + jnp.where(hit, values[q][j : j + 1], 0)
        for q in range(4):
            for f in range(rows // LANES):
                count = (sums[q] >> (8 * f)) & 255
                at = q * rows + f * LANES + first
                out_ref[at : at + part, :] = count.astype(jnp.float32).astype(jnp.bfloat16)


def count_rows(base, ids, rows):
    blocks, bag, per = ids.shape
    return pl.pallas_call(
        count_kernel,
        out_shape=jax.ShapeDtypeStruct((4 * rows, blocks * per), jnp.bfloat16),
        grid_spec=pltpu.PrefetchScalarGridSpec(
            num_scalar_prefetch=1,
            grid=(blocks // 2,),
            in_specs=[pl.BlockSpec((2, bag, per), lambda i, b: (i, 0, 0))],
            out_specs=pl.BlockSpec((4 * rows, 2 * per), lambda i, b: (0, i)),
        ),
        compiler_params=pltpu.CompilerParams(vmem_limit_bytes=VMEM_LIMIT),
        name="count_rows",
    )(base, ids)


def pool_kernel(xh_ref, counts_ref, own_ref, own_c_ref, far_ref, far_c_ref, out_ref, halves):
    rows, width = own_ref.shape

    @pl.when(pl.program_id(0) == 0)
    def _():
        xh = xh_ref[0]
        for at, ref in (
            (2 * xh, own_ref),
            (2 * xh + 1, own_c_ref),
            (2 - 2 * xh, far_ref),
            (3 - 2 * xh, far_c_ref),
        ):
            high, low = split_halves(ref[...])
            halves[at, :, :width] = high
            halves[at, :, width:] = low

    total = None
    for p in range(4):
        term = lax.dot_general(
            counts_ref[p * rows : (p + 1) * rows, :],
            halves[p],
            (((0,), (0,)), ((), ())),
            preferred_element_type=jnp.float32,
        )
        total = term if total is None else total + term
    out_ref[...] = total[:, :width] + total[:, width:]


def pool(xh, counts, tables, tile=256):
    rows, width = tables[0].shape
    samples = counts.shape[1]
    whole = pl.BlockSpec((rows, width), lambda i, b: (0, 0))
    return pl.pallas_call(
        pool_kernel,
        out_shape=jax.ShapeDtypeStruct((samples, width), jnp.float32),
        grid_spec=pltpu.PrefetchScalarGridSpec(
            num_scalar_prefetch=1,
            grid=(samples // tile,),
            in_specs=[pl.BlockSpec((4 * rows, tile), lambda i, b: (0, i))] + [whole] * 4,
            out_specs=pl.BlockSpec((tile, width), lambda i, b: (i, 0)),
            scratch_shapes=[pltpu.VMEM((4, rows, 2 * width), jnp.bfloat16)],
        ),
        compiler_params=pltpu.CompilerParams(vmem_limit_bytes=VMEM_LIMIT),
        name="pool",
    )(xh, counts, *tables)


def dot3(a, b, dims):
    a_high, a_low = split_halves(a)
    b_high, b_low = split_halves(b)

    def dot(u, v):
        return lax.dot_general(u, v, (dims, ((), ())), preferred_element_type=jnp.float32)

    return dot(a_high, b_high) + (dot(a_high, b_low) + dot(a_low, b_high))


def cross_kernel(parts_ref, weight_ref, bias_ref, upstream_ref, crossed_ref, back_ref):
    pooled = parts_ref[0]
    for k in range(1, parts_ref.shape[0]):
        pooled = pooled + parts_ref[k]
    weight, upstream = weight_ref[...], upstream_ref[...]
    mixed = dot3(pooled, weight, ((1,), (0,))) + bias_ref[...]
    crossed_ref[...] = pooled * mixed + pooled
    back_ref[...] = upstream * mixed + dot3(upstream * pooled, weight, ((1,), (1,))) + upstream


def cross(parts, weight, bias, upstream):
    out = jax.ShapeDtypeStruct(upstream.shape, jnp.float32)
    return pl.pallas_call(
        cross_kernel,
        out_shape=(out, out),
        compiler_params=pltpu.CompilerParams(vmem_limit_bytes=VMEM_LIMIT),
        name="cross",
    )(parts, weight, bias.reshape(1, -1), upstream)


def row_kernel(counts_ref, back_ref, out_ref, halves):
    width = back_ref.shape[1]

    @pl.when(pl.program_id(0) == 0)
    def _():
        high, low = split_halves(back_ref[...])
        halves[:, :width] = high
        halves[:, width:] = low

    both = jnp.dot(counts_ref[...], halves[...], preferred_element_type=jnp.float32)
    out_ref[0] = both[:, :width] + both[:, width:]


def row_sums(counts, back, rows, core):
    samples, width = back.shape
    return pl.pallas_call(
        row_kernel,
        out_shape=jax.ShapeDtypeStruct((2, rows, width), jnp.float32),
        grid=(2,),
        in_specs=[
            pl.BlockSpec((rows, samples), lambda i: (2 * i + core, 0)),
            pl.BlockSpec((samples, width), lambda i: (0, 0)),
        ],
        out_specs=pl.BlockSpec((1, rows, width), lambda i: (i, 0, 0)),
        scratch_shapes=[pltpu.VMEM((samples, 2 * width), jnp.bfloat16)],
        compiler_params=pltpu.CompilerParams(vmem_limit_bytes=VMEM_LIMIT),
        name="row_sums",
    )(counts, back)


def adagrad_rows(rows, sums, grads):
    fresh = sums + jnp.mean(grads * grads, axis=1)
    return (rows - 0.5 * grads / jnp.sqrt(fresh)[:, None], fresh)


def other_core(x):
    return lax.ppermute(x, "c", [(0, 1), (1, 0)])


def body(bag_ids, table, accum, cross_weight, cross_bias, upstream):
    per, bag = bag_ids.shape
    rows, width = table.shape
    xh, z, c = (lax.axis_index(a) for a in ("xh", "z", "c"))
    base = jnp.stack(
        [(h * (NZ * 2) + z * 2 + (c if d == 0 else 1 - c)) * rows for h in (0, 1) for d in (0, 1)]
    ).astype(jnp.int32)

    ids = lax.all_to_all(
        jnp.broadcast_to(bag_ids.T[None], (NZ, bag, per)), "z", 0, 0, tiled=True
    )
    far = lax.ppermute(table, ("xl", "xh"), [(0, 3), (3, 0), (1, 2), (2, 1)])
    tables = (table, other_core(table), far, other_core(far))
    counts = count_rows(base, ids, rows)
    partial = pool(xh.astype(jnp.int32).reshape(1), counts, tables)
    parts = lax.all_to_all(partial.reshape(NZ, per, width), "z", 0, 0, tiled=True)
    crossed, back = cross(parts, cross_weight, cross_bias, upstream)

    gathered = lax.all_gather(back, "z", axis=0, tiled=True)
    theirs = row_sums(counts, gathered, rows, 1)
    mine = row_sums(counts, gathered, rows, 0)
    mine = mine + other_core(theirs)
    blocks = mine.reshape(32, rows // 16, width)
    blocks = lax.all_to_all(blocks, ("xh", "xl", "y"), 0, 0, tiled=True)
    total = jnp.sum(blocks, axis=0)
    totals = lax.all_to_all(
        jnp.broadcast_to(total[None], (16,) + total.shape), ("xl", "y"), 0, 0, tiled=True
    ).reshape(rows, width)
    new_table, new_accum = adagrad_rows(table, accum, totals)
    return (crossed, new_table, new_accum)


def solution(mesh):
    fine = Mesh(mesh.devices.reshape(SIZES), AXES)
    samples = P(AXES, None)
    shard = ("xh", "z", "c")
    return jax.shard_map(
        body,
        mesh=fine,
        in_specs=(samples, P(shard, None), P(shard), P(), P(), samples),
        out_specs=(samples, P(shard, None), P(shard)),
        check_vma=False,
    )
```

time: 980 us -> 183 us (0.19)
  the two profiles are of different devices: /device:TPU:4 before, /device:TPU:10 now
where the time goes in v1:
time: 183 us
  blocking collectives  119 us (65%)
  starting transfers between devices  24.4 us (13%)
  waiting for transfers between devices  23 us (13%)
  Pallas kernels  11.1 us (6%)
  other arithmetic  2.73 us (1%)
  local copies, waits for them, and re-layouts  2.21 us (1%)
    all_to_all x1, blocking collectives, body(): blocks = lax.all_to_all(blocks, ('xh', 'xl', 'y'), 0, 0, tiled=True)  38.8 us
    all_to_all x1, blocking collectives, body(): lax.all_to_all(partial.reshape(NZ, per, width), 'z', 0, 0, tiled=True)  34.3 us
    all_gather x1, blocking collectives, body(): gathered = lax.all_gather(back, 'z', axis=0, tiled=True)  26.3 us
    all_to_all x1, blocking collectives, body(): lax.all_to_all(jnp.broadcast_to(total[None], (16,) + total.shape), ('xl',...  19.3 us
    all_to_all x1, starting transfers between devices, body(): lax.all_to_all(jnp.broadcast_to(bag_ids.T[None], (NZ, bag, per)), 'z', 0,...  15.2 us
    all_to_all x1, waiting for transfers between devices, body(): lax.all_to_all(jnp.broadcast_to(bag_ids.T[None], (NZ, bag, per)), 'z', 0,...  11.2 us
    ppermute x1, waiting for transfers between devices, body(): far = lax.ppermute(table, ('xl', 'xh'), [(0, 3), (3, 0), (1, 2), (2, 1)])  10.4 us
    ppermute x3, starting transfers between devices, other_core(): return lax.ppermute(x, 'c', [(0, 1), (1, 0)])  5.75 us
  transfers between devices with their start and end apart: 5, of which 3 were waited for; matrix products, arithmetic and copies ran while one was open for 2% of the time, Pallas kernels for 3%

profile of v1, /device:TPU:10, one launch (start us, length us, event | category | flops | bytes accessed | tf_op | source)
XLA Modules:
  0.0 182.9 jit_solution(5233505355544975714)
XLA Ops:
  0.6 3.5 %collective-permute-start.1 = (f32[512,256]{1,0:T(8,128)}, f32[512,256]{1,0:T(8,128)S(1)}, u32[]{:S(2)}, u32[]{:S(2)}) collective-permute-start(f32[512,256]{1,0:T(8,128)} %own_ref.1), channel_id=1, source_target_pairs={{0,408},{408,0},{24,384},{384,24},{1,409},{409,1},{25,385},{385,25... | collective-permute-start | bytes 1572872 | tf_op jit(solution)/shard_map/ppermute | solution.py:189
  4.2 1.9 %collective-permute-start = (f32[512,256]{1,0:T(8,128)}, f32[512,256]{1,0:T(8,128)S(1)}, u32[]{:S(2)}, u32[]{:S(2)}) collective-permute-start(f32[512,256]{1,0:T(8,128)} %own_ref.1), channel_id=1, source_target_pairs={{0,1},{1,0},{2,3},{3,2},{4,5},{5,4},{6,7},{7,6},{8,9},{9,8},{10,11... | collective-permute-start | bytes 1572872 | tf_op jit(solution)/shard_map/ppermute | solution.py:175
  6.1 10.4 %collective-permute-done.1.far_ref = f32[512,256]{1,0:T(8,128)S(1)} collective-permute-done((f32[512,256]{1,0:T(8,128)}, f32[512,256]{1,0:T(8,128)S(1)}, u32[]{:S(2)}, u32[]{:S(2)}) %collective-permute-start.1) | collective-permute-done | bytes 524320 | tf_op jit(solution)/shard_map/ppermute | solution.py:189
  16.5 1.9 %collective-permute-start.2 = (f32[512,256]{1,0:T(8,128)S(1)}, f32[512,256]{1,0:T(8,128)S(1)}, u32[]{:S(2)}, u32[]{:S(2)}) collective-permute-start(f32[512,256]{1,0:T(8,128)S(1)} %collective-permute-done.1.far_ref), channel_id=1, source_target_pairs={{0,1},{1,0},{2,3},{3,2},{4,5},{5,4},{6,7},{7,6},{8,9},{9,8},{10,11... | collective-permute-start | bytes 1572872 | tf_op jit(solution)/shard_map/ppermute | solution.py:175
  18.5 0.7 broadcast_in_dim.4
  19.2 0.7 reshape.31
  19.9 15.2 %all-to-all-start = ((s32[12,1,1280]{2,1,0:T(1,128)}), s32[12,1,1280]{2,1,0:T(1,128)S(1)}, u32[]{:S(2)}, u32[]{:S(2)}) async-start(s32[12,1,1280]{2,1,0:T(1,128)} %reshape.31), calls=%async_computation | async-start | bytes 122880 | tf_op jit(solution)/shard_map/all_to_all | solution.py:186
  35.1 0.1 pad_add_fusion.base_ref
  35.2 11.2 %all-to-all-done = s32[12,1,1280]{2,1,0:T(1,128)S(1)} async-done(((s32[12,1,1280]{2,1,0:T(1,128)}), s32[12,1,1280]{2,1,0:T(1,128)S(1)}, u32[]{:S(2)}, u32[]{:S(2)}) %all-to-all-start) | async-done | bytes 61472 | tf_op jit(solution)/shard_map/all_to_all | solution.py:186
  46.4 0.5 broadcast.8
  46.9 0.8 reduce.1
  47.7 0.1 reshape.32.ids_ref
  47.8 4.7 %count_rows.1.counts_ref = bf16[2048,768]{1,0:T(8,128)(2,1)S(1)} custom-call(s32[4]{0:T(128)S(1)} %pad_add_fusion.base_ref, s32[12,20,64]{2,1,0:T(8,128)S(1)} %reshape.32.ids_ref), custom_call_target="tpu_custom_call" | custom-call | tf_op jit(solution)/shard_map/count_rows/pallas_call | solution.py:48
  52.5 0.0 copy-start.1
  52.5 0.0 copy-start.2
  52.5 0.0 copy-start.3
  52.5 2.9 %pool.1 = f32[768,256]{1,0:T(8,128)S(1)} custom-call(s32[1]{0:T(128)} %bitcast.xh_ref, bf16[2048,768]{1,0:T(8,128)(2,1)S(1)} %count_rows.1.counts_ref, f32[512,256]{1,0:T(8,128)S(1)} %copy-done, f32[512,256]{1,0:T(8,128)S(1)} %collective-permute-done.own_c_ref, f32[512,256]{1,0:T(8,128)S(1)} %collective-permute-done.1.far_ref, ...), custom_call_target="tpu_custom_call" | custom-call | tf_op jit(solution)/shard_map/pool/pallas_call | solution.py:94
  55.5 34.3 %all_to_all.20.parts_ref = f32[12,64,256]{2,1,0:T(8,128)S(1)} all-to-all(f32[12,64,256]{2,1,0:T(8,128)S(1)} %bitcast.13), channel_id=1, replica_groups=mesh['xl'=2,'y'=8,'xh'=2,'z'=12,'c'=2] {'z'}, dimensions={0} | all-to-all | bytes 1572864 | tf_op jit(solution)/shard_map/all_to_all | solution.py:193
  89.7 0.9 cross.1
  90.6 26.3 %all_gather.3.back_ref = f32[768,256]{1,0:T(8,128)S(1)} all-gather(f32[64,256]{1,0:T(8,128)S(1)} %get-tuple-element.6), channel_id=1, replica_groups=mesh['xl'=2,'y'=8,'xh'=2,'z'=12,'c'=2] {'z'}, dimensions={0}, use_global_device_ids=true | all-gather | bytes 851968 | tf_op jit(solution)/shard_map/all_gather | solution.py:196
  116.9 1.3 row_sums.3
  118.2 1.9 %collective-permute-start.3 = (f32[2,512,256]{2,1,0:T(8,128)S(1)}, f32[2,512,256]{2,1,0:T(8,128)S(1)}, u32[]{:S(2)}, u32[]{:S(2)}) collective-permute-start(f32[2,512,256]{2,1,0:T(8,128)S(1)} %row_sums.3), channel_id=1, source_target_pairs={{0,1},{1,0},{2,3},{3,2},{4,5},{5,4},{6,7},{7,6},{8,9},{9,8},{10,11... | collective-permute-start | bytes 3145736 | tf_op jit(solution)/shard_map/ppermute | solution.py:175
  120.1 1.3 row_sums.2
  121.5 1.3 collective-permute-done.3
  122.8 0.1 add.27
  122.9 38.8 %all_to_all.21 = f32[32,32,256]{2,1,0:T(8,128)S(1)} all-to-all(f32[32,32,256]{2,1,0:T(8,128)S(1)} %bitcast.15), channel_id=1, replica_groups=mesh['xl'=2,'y'=8,'xh'=2,'z'=12,'c'=2] {'xh','xl','y'}, dimensions={0} | all-to-all | bytes 2097152 | tf_op jit(solution)/shard_map/all_to_all | solution.py:201
  161.8 0.1 reduce_sum.18
  161.9 19.3 %all_to_all.22 = f32[16,32,256]{2,1,0:T(8,128)S(1)} all-to-all(f32[16,32,256]{2,1,0:T(8,128)S(1)} %broadcast_in_dim.5), channel_id=1, replica_groups=mesh['xl'=2,'y'=8,'xh'=2,'z'=12,'c'=2] {'xl','y'}, dimensions={0} | all-to-all | bytes 1048576 | tf_op jit(solution)/shard_map/all_to_all | solution.py:203
  181.2 0.1 multiply_reduce_fusion
  181.3 0.1 div.18
  181.4 0.6 fusion.1
  182.0 0.9 fusion
  (11 shorter events, 0.1 us)
Async XLA Ops:
  0.6 51.9 %copy-start = (f32[512,256]{1,0:T(8,128)S(1)}, f32[512,256]{1,0:T(8,128)}, u32[]{:S(2)}) copy-start(f32[512,256]{1,0:T(8,128)} %own_ref.1) | copy-start | bytes 1572868
  0.6 15.9 %collective-permute-start.1 = (f32[512,256]{1,0:T(8,128)}, f32[512,256]{1,0:T(8,128)S(1)}, u32[]{:S(2)}, u32[]{:S(2)}) collective-permute-start(f32[512,256]{1,0:T(8,128)} %own_ref.1), channel_id=1, source_target_pairs={{0,408},{408,0},{24,384},{384,24},{1,409},{409,1},{25,385},{385,25... | collective-permute-start | bytes 1572872 | tf_op jit(solution)/shard_map/ppermute | solution.py:189
  4.2 48.3 %collective-permute-start = (f32[512,256]{1,0:T(8,128)}, f32[512,256]{1,0:T(8,128)S(1)}, u32[]{:S(2)}, u32[]{:S(2)}) collective-permute-start(f32[512,256]{1,0:T(8,128)} %own_ref.1), channel_id=1, source_target_pairs={{0,1},{1,0},{2,3},{3,2},{4,5},{5,4},{6,7},{7,6},{8,9},{9,8},{10,11... | collective-permute-start | bytes 1572872 | tf_op jit(solution)/shard_map/ppermute | solution.py:175
  16.5 35.9 %collective-permute-start.2 = (f32[512,256]{1,0:T(8,128)S(1)}, f32[512,256]{1,0:T(8,128)S(1)}, u32[]{:S(2)}, u32[]{:S(2)}) collective-permute-start(f32[512,256]{1,0:T(8,128)S(1)} %collective-permute-done.1.far_ref), channel_id=1, source_target_pairs={{0,1},{1,0},{2,3},{3,2},{4,5},{5,4},{6,7},{7,6},{8,9},{9,8},{10,11... | collective-permute-start | bytes 1572872 | tf_op jit(solution)/shard_map/ppermute | solution.py:175
  19.9 26.5 %all-to-all-start = ((s32[12,1,1280]{2,1,0:T(1,128)}), s32[12,1,1280]{2,1,0:T(1,128)S(1)}, u32[]{:S(2)}, u32[]{:S(2)}) async-start(s32[12,1,1280]{2,1,0:T(1,128)} %reshape.31), calls=%async_computation | async-start | bytes 122880 | tf_op jit(solution)/shard_map/all_to_all | solution.py:186
  52.5 37.2 %copy-start.1 = (f32[256,256]{1,0:T(8,128)S(1)}, f32[256,256]{1,0:T(8,128)}, u32[]{:S(2)}) copy-start(f32[256,256]{1,0:T(8,128)} %weight_ref.1) | copy-start | bytes 786436
  52.5 37.2 %copy-start.2 = (f32[64,256]{1,0:T(8,128)S(1)}, f32[64,256]{1,0:T(8,128)}, u32[]{:S(2)}) copy-start(f32[64,256]{1,0:T(8,128)} %upstream_ref.1) | copy-start | bytes 196612
  52.5 37.2 %copy-start.3 = (f32[256]{0:T(256)S(1)}, f32[256]{0:T(256)}, u32[]{:S(2)}) copy-start(f32[256]{0:T(256)} %param.10) | copy-start | bytes 3076
  118.2 4.6 %collective-permute-start.3 = (f32[2,512,256]{2,1,0:T(8,128)S(1)}, f32[2,512,256]{2,1,0:T(8,128)S(1)}, u32[]{:S(2)}, u32[]{:S(2)}) collective-permute-start(f32[2,512,256]{2,1,0:T(8,128)S(1)} %row_sums.3), channel_id=1, source_target_pairs={{0,1},{1,0},{2,3},{3,2},{4,5},{5,4},{6,7},{7,6},{8,9},{9,8},{10,11... | collective-permute-start | bytes 3145736 | tf_op jit(solution)/shard_map/ppermute | solution.py:175
  122.9 58.5 %copy-start.4 = (f32[512]{0:T(512)S(1)}, f32[512]{0:T(512)}, u32[]{:S(2)}) copy-start(f32[512]{0:T(512)} %param.8) | copy-start | bytes 6148

commit v2 on v1

v2 whole, which is shorter than its diff:
```python
import functools

import jax
import jax.numpy as jnp
from jax import lax
from jax.experimental import pallas as pl
from jax.experimental.pallas import tpu as pltpu
from jax.sharding import Mesh
from jax.sharding import PartitionSpec as P

AXES = ("xl", "y", "xh", "z", "c")
SIZES = (2, 8, 2, 12, 2)
NZ = 12
LANES = 128
PARAMS = pltpu.CompilerParams(vmem_limit_bytes=16 * 1024 * 1024)
SCALARS = pl.BlockSpec(memory_space=pltpu.SMEM)
WHOLE = pl.BlockSpec(memory_space=pltpu.VMEM)


def split_halves(x):
    high = x.astype(jnp.bfloat16)
    return high, (x - high.astype(jnp.float32)).astype(jnp.bfloat16)


def count_kernel(bag, per, base_ref, ids_ref, out_ref):
    rows = out_ref.shape[0] // 4
    part = 32

    def two_blocks(i, _):
        ids = jnp.concatenate([ids_ref[2 * i, :, :per], ids_ref[2 * i + 1, :, :per]], axis=1)
        columns = pl.ds(pl.multiple_of(i * LANES, LANES), LANES)
        word = ids & (LANES - 1)
        values = []
        for q in range(4):
            local = ids - base_ref[q]
            inside = (local >= 0) & (local < rows)
            values.append(jnp.where(inside, jnp.int32(1) << ((local & (rows - 1)) >> 7) * 8, 0))
        for first in range(0, LANES, part):
            lines = lax.broadcasted_iota(jnp.int32, (part, LANES), 0) + first
            sums = [jnp.zeros((part, LANES), jnp.int32) for _ in range(4)]
            for j in range(bag):
                hit = word[j : j + 1] == lines
                for q in range(4):
                    sums[q] = sums[q] + jnp.where(hit, values[q][j : j + 1], 0)
            for q in range(4):
                for f in range(rows // LANES):
                    count = (sums[q] >> (8 * f)) & 255
                    at = q * rows + f * LANES + first
                    out_ref[at : at + part, columns] = count.astype(jnp.float32).astype(jnp.bfloat16)
        return 0

    lax.fori_loop(0, ids_ref.shape[0] // 2, two_blocks, 0)


def count_rows(places, ids, bag, per, rows):
    return pl.pallas_call(
        functools.partial(count_kernel, bag, per),
        out_shape=jax.ShapeDtypeStruct((4 * rows, ids.shape[0] * per), jnp.bfloat16),
        in_specs=[SCALARS, WHOLE],
        out_specs=WHOLE,
        compiler_params=PARAMS,
        name="count_rows",
    )(places, ids)


def pool_kernel(tile, places_ref, counts_ref, own_ref, own_c_ref, far_ref, far_c_ref, out_ref, halves):
    rows, width = own_ref.shape
    for place, ref in ((4, own_ref), (5, own_c_ref), (6, far_ref), (7, far_c_ref)):
        high, low = split_halves(ref[...])
        at = places_ref[place]
        halves[at, :, :width] = high
        halves[at, :, width:] = low

    def some_samples(i, _):
        some = pl.ds(pl.multiple_of(i * tile, tile), tile)
        total = None
        for p in range(4):
            term = lax.dot_general(
                counts_ref[p * rows : (p + 1) * rows, some],
                halves[p],
                (((0,), (0,)), ((), ())),
                preferred_element_type=jnp.float32,
            )
            total = term if total is None else total + term
        out_ref[some, :] = total[:, :width] + total[:, width:]
        return 0

    lax.fori_loop(0, counts_ref.shape[1] // tile, some_samples, 0)


def pool(places, counts, tables, tile=256):
    rows, width = tables[0].shape
    return pl.pallas_call(
        functools.partial(pool_kernel, tile),
        out_shape=jax.ShapeDtypeStruct((counts.shape[1], width), jnp.float32),
        in_specs=[SCALARS] + [WHOLE] * 5,
        out_specs=WHOLE,
        scratch_shapes=[pltpu.VMEM((4, rows, 2 * width), jnp.bfloat16)],
        compiler_params=PARAMS,
        name="pool",
    )(places, counts, *tables)


def dot3(a, b, dims):
    a_high, a_low = split_halves(a)
    b_high, b_low = split_halves(b)

    def dot(u, v):
        return lax.dot_general(u, v, (dims, ((), ())), preferred_element_type=jnp.float32)

    return dot(a_high, b_high) + (dot(a_high, b_low) + dot(a_low, b_high))


def cross_kernel(parts_ref, weight_ref, bias_ref, upstream_ref, crossed_ref, back_ref):
    pooled = parts_ref[0]
    for k in range(1, parts_ref.shape[0]):
        pooled = pooled + parts_ref[k]
    weight, upstream = weight_ref[...], upstream_ref[...]
    mixed = dot3(pooled, weight, ((1,), (0,))) + bias_ref[...]
    crossed_ref[...] = pooled * mixed + pooled
    back_ref[...] = upstream * mixed + dot3(upstream * pooled, weight, ((1,), (1,))) + upstream


def cross(parts, weight, bias, upstream):
    out = jax.ShapeDtypeStruct(upstream.shape, jnp.float32)
    return pl.pallas_call(
        cross_kernel,
        out_shape=(out, out),
        compiler_params=PARAMS,
        name="cross",
    )(parts, weight, bias.reshape(1, -1), upstream)


def row_kernel(first, places_ref, counts_ref, back_ref, a_ref, b_ref, halves):
    rows, width = a_ref.shape
    high, low = split_halves(back_ref[...])
    halves[:, :width] = high
    halves[:, width:] = low
    for k, out_ref in enumerate((a_ref, b_ref)):
        lines = pl.ds(pl.multiple_of(places_ref[first + k] * rows, rows), rows)
        both = jnp.dot(counts_ref[lines, :], halves[...], preferred_element_type=jnp.float32)
        out_ref[...] = both[:, :width] + both[:, width:]


def row_sums(first, places, counts, back, rows):
    samples, width = back.shape
    out = jax.ShapeDtypeStruct((rows, width), jnp.float32)
    return pl.pallas_call(
        functools.partial(row_kernel, first),
        out_shape=(out, out),
        in_specs=[SCALARS, WHOLE, WHOLE],
        out_specs=(WHOLE, WHOLE),
        scratch_shapes=[pltpu.VMEM((samples, 2 * width), jnp.bfloat16)],
        compiler_params=PARAMS,
        name="row_sums",
    )(places, counts, back)


def adagrad_rows(rows, sums, grads):
    fresh = sums + jnp.mean(grads * grads, axis=1)
    return (rows - 0.5 * grads / jnp.sqrt(fresh)[:, None], fresh)


def other_core(x):
    return lax.ppermute(x, "c", [(0, 1), (1, 0)])


def x_neighbour(x):
    return lax.ppermute(x, ("xl", "xh"), [(0, 3), (3, 0), (1, 2), (2, 1)])


def body(bag_ids, table, accum, cross_weight, cross_bias, upstream):
    per, bag = bag_ids.shape
    rows, width = table.shape
    xh, z, c = (lax.axis_index(a) for a in ("xh", "z", "c"))
    places = [(h * (NZ * 2) + z * 2 + d) * rows for h in (0, 1) for d in (c, 1 - c)]
    places = jnp.stack(places + [2 * xh, 2 * xh + 1, 2 - 2 * xh, 3 - 2 * xh]).astype(jnp.int32)

    padded = jnp.pad(bag_ids.T, ((0, -bag % 8), (0, LANES - per)))
    ids = lax.all_to_all(jnp.broadcast_to(padded[None], (NZ,) + padded.shape), "z", 0, 0, tiled=True)
    far = x_neighbour(table)
    own_c = other_core(table)
    far, ids, places = lax.optimization_barrier((far, ids, places))
    tables = (table, own_c, far, other_core(far))
    counts = count_rows(places, ids, bag, per, rows)
    partial = pool(places, counts, tables)
    parts = lax.all_to_all(partial.reshape(NZ, per, width), "z", 0, 0, tiled=True)
    crossed, back = cross(parts, cross_weight, cross_bias, upstream)

    gathered = lax.all_gather(back, "z", axis=0, tiled=True)
    mine, theirs = row_sums(6, places, counts, gathered, rows)
    away = x_neighbour(mine + other_core(theirs))
    mine, theirs = row_sums(4, places, counts, gathered, rows)
    here = mine + other_core(theirs) + away
    blocks = lax.all_to_all(here.reshape(16, rows // 16, width), ("xl", "y"), 0, 0, tiled=True)
    total = jnp.sum(blocks, axis=0)
    totals = lax.all_to_all(
        jnp.broadcast_to(total[None], (16,) + total.shape), ("xl", "y"), 0, 0, tiled=True
    ).reshape(rows, width)
    new_table, new_accum = adagrad_rows(table, accum, totals)
    return (crossed, new_table, new_accum)


def solution(mesh):
    fine = Mesh(mesh.devices.reshape(SIZES), AXES)
    samples = P(AXES, None)
    shard = ("xh", "z", "c")
    return jax.shard_map(
        body,
        mesh=fine,
        in_specs=(samples, P(shard, None), P(shard), P(), P(), samples),
        out_specs=(samples, P(shard, None), P(shard)),
        check_vma=False,
    )
```

time: 183 us -> 175 us (0.956)
  blocking collectives: 119 us -> 106 us
  starting transfers between devices: 24.4 us -> 29.3 us
    all_to_all x1, blocking collectives: 38.8 us -> 24.5 us  [body(): lax.all_to_all(here.reshape(16, rows // 16, width), ('xl', 'y'), 0, 0, ti...]
    ppermute x1 -> x2, waiting for transfers between devices: 10.4 us -> 13.3 us  [x_neighbour(): return lax.ppermute(x, ('xl', 'xh'), [(0, 3), (3, 0), (1, 2), (2, 1)])]
    ppermute x1 -> x2, starting transfers between devices: 3.53 us -> 5.98 us  [x_neighbour(): return lax.ppermute(x, ('xl', 'xh'), [(0, 3), (3, 0), (1, 2), (2, 1)])]
    ppermute x3 -> x4, starting transfers between devices: 5.75 us -> 8.16 us  [other_core(): return lax.ppermute(x, 'c', [(0, 1), (1, 0)])]
  transfers between devices with their start and end apart: 5 -> 7, of which waited for: 3 -> 2; matrix products, arithmetic and copies ran while one was open for 2% -> 1% of each run, Pallas kernels for 3% -> 3%
where the time goes in v2:
time: 175 us; the launch traced here: 174 us
  blocking collectives  106 us (61%)
  starting transfers between devices  29.3 us (17%)
  waiting for transfers between devices  23.8 us (14%)
  Pallas kernels  11.3 us (6%)
  other arithmetic  1.87 us (1%)
    all_to_all x1, blocking collectives, body(): lax.all_to_all(partial.reshape(NZ, per, width), 'z', 0, 0, tiled=True)  35.3 us
    all_gather x1, blocking collectives, body(): gathered = lax.all_gather(back, 'z', axis=0, tiled=True)  27 us
    all_to_all x1, blocking collectives, body(): lax.all_to_all(here.reshape(16, rows // 16, width), ('xl', 'y'), 0, 0, ti...  24.5 us
    all_to_all x1, blocking collectives, body(): lax.all_to_all(jnp.broadcast_to(total[None], (16,) + total.shape), ('xl',...  18.8 us
    all_to_all x1, starting transfers between devices, body(): lax.all_to_all(jnp.broadcast_to(padded[None], (NZ,) + padded.shape), 'z',...  15.2 us
    ppermute x2, waiting for transfers between devices, x_neighbour(): return lax.ppermute(x, ('xl', 'xh'), [(0, 3), (3, 0), (1, 2), (2, 1)])  13.3 us
    all_to_all x1, waiting for transfers between devices, body(): lax.all_to_all(jnp.broadcast_to(padded[None], (NZ,) + padded.shape), 'z',...  10.5 us
    ppermute x4, starting transfers between devices, other_core(): return lax.ppermute(x, 'c', [(0, 1), (1, 0)])  8.16 us
  transfers between devices with their start and end apart: 7, of which 2 were waited for; matrix products, arithmetic and copies ran while one was open for 1% of the time, Pallas kernels for 3%

profile of v2, /device:TPU:10, one launch (start us, length us, event | category | flops | bytes accessed | tf_op | source)
XLA Modules:
  0.0 174.3 jit_solution(4977030334413129020)
XLA Ops:
  0.6 0.0 copy-start
  0.6 3.5 %collective-permute-start = (f32[512,256]{1,0:T(8,128)}, f32[512,256]{1,0:T(8,128)S(1)}, u32[]{:S(2)}, u32[]{:S(2)}) collective-permute-start(f32[512,256]{1,0:T(8,128)} %own_ref.1), channel_id=1, source_target_pairs={{0,408},{408,0},{24,384},{384,24},{1,409},{409,1},{25,385},{385,25... | collective-permute-start | bytes 1572872 | tf_op jit(solution)/shard_map/ppermute | solution.py:169
  4.2 0.7 pad.4
  4.9 0.7 broadcast_in_dim.4
  5.6 15.2 %all-to-all-start = ((s32[12,24,128]{2,1,0:T(8,128)}), s32[12,24,128]{2,1,0:T(8,128)S(1)}, u32[]{:S(2)}, u32[]{:S(2)}) async-start(s32[12,24,128]{2,1,0:T(8,128)} %broadcast_in_dim.4), calls=%async_computation | async-start | bytes 294912 | tf_op jit(solution)/shard_map/all_to_all | solution.py:180
  20.7 1.9 %collective-permute-start.1 = (f32[512,256]{1,0:T(8,128)}, f32[512,256]{1,0:T(8,128)S(1)}, u32[]{:S(2)}, u32[]{:S(2)}) collective-permute-start(f32[512,256]{1,0:T(8,128)} %own_ref.1), channel_id=1, source_target_pairs={{0,1},{1,0},{2,3},{3,2},{4,5},{5,4},{6,7},{7,6},{8,9},{9,8},{10,11... | collective-permute-start | bytes 1572872 | tf_op jit(solution)/shard_map/ppermute | solution.py:165
  22.7 0.1 stack.35.base_ref.places_ref
  22.8 10.5 %all-to-all-done.ids_ref = s32[12,24,128]{2,1,0:T(8,128)S(1)} async-done(((s32[12,24,128]{2,1,0:T(8,128)}), s32[12,24,128]{2,1,0:T(8,128)S(1)}, u32[]{:S(2)}, u32[]{:S(2)}) %all-to-all-start) | async-done | bytes 147488 | tf_op jit(solution)/shard_map/all_to_all | solution.py:180
  33.3 0.0 collective-permute-done.far_ref
  33.3 1.9 %collective-permute-start.2 = (f32[512,256]{1,0:T(8,128)S(1)}, f32[512,256]{1,0:T(8,128)S(1)}, u32[]{:S(2)}, u32[]{:S(2)}) collective-permute-start(f32[512,256]{1,0:T(8,128)S(1)} %collective-permute-done.far_ref), channel_id=1, source_target_pairs={{0,1},{1,0},{2,3},{3,2},{4,5},{5,4},{6,7},{7,6},{8,9},{9,8},{10,11... | collective-permute-start | bytes 1572872 | tf_op jit(solution)/shard_map/ppermute | solution.py:165
  35.2 4.2 %count_rows.1.counts_ref = bf16[2048,768]{1,0:T(8,128)(2,1)S(1)} custom-call(s32[8]{0:T(128)S(1)} %stack.35.base_ref.places_ref, s32[12,24,128]{2,1,0:T(8,128)S(1)} %all-to-all-done.ids_ref), custom_call_target="tpu_custom_call" | custom-call | tf_op jit(solution)/shard_map/count_rows/pallas_call | solution.py:56
  39.4 0.0 copy-start.1
  39.4 0.0 copy-start.2
  39.4 0.0 copy-start.3
  39.5 3.2 %pool.1 = f32[768,256]{1,0:T(8,128)S(1)} custom-call(s32[8]{0:T(128)S(1)} %stack.35.base_ref.places_ref, bf16[2048,768]{1,0:T(8,128)(2,1)S(1)} %count_rows.1.counts_ref, f32[512,256]{1,0:T(8,128)S(1)} %copy-done, f32[512,256]{1,0:T(8,128)S(1)} %collective-permute-done.1.own_c_ref, f32[512,256]{1,0:T(8,128)S(1)} %collective-permute-done.far_ref, ...), custom_call_target="tpu_custom_call" | custom-call | tf_op jit(solution)/shard_map/pool/pallas_call | solution.py:93
  42.7 35.3 %all_to_all.20.parts_ref = f32[12,64,256]{2,1,0:T(8,128)S(1)} all-to-all(f32[12,64,256]{2,1,0:T(8,128)S(1)} %bitcast.16), channel_id=1, replica_groups=mesh['xl'=2,'y'=8,'xh'=2,'z'=12,'c'=2] {'z'}, dimensions={0} | all-to-all | bytes 1572864 | tf_op jit(solution)/shard_map/all_to_all | solution.py:187
  78.0 0.9 cross.1
  78.8 27.0 %all_gather.3.back_ref = f32[768,256]{1,0:T(8,128)S(1)} all-gather(f32[64,256]{1,0:T(8,128)S(1)} %get-tuple-element.16), channel_id=1, replica_groups=mesh['xl'=2,'y'=8,'xh'=2,'z'=12,'c'=2] {'z'}, dimensions={0}, use_global_device_ids=true | all-gather | bytes 851968 | tf_op jit(solution)/shard_map/all_gather | solution.py:190
  105.8 1.5 row_sums.3
  107.3 1.9 %collective-permute-start.4 = (f32[512,256]{1,0:T(8,128)S(1)}, f32[512,256]{1,0:T(8,128)S(1)}, u32[]{:S(2)}, u32[]{:S(2)}) collective-permute-start(f32[512,256]{1,0:T(8,128)S(1)} %get-tuple-element.20), channel_id=1, source_target_pairs={{0,1},{1,0},{2,3},{3,2},{4,5},{5,4},{6,7},{7,6},{8,9},{9,8},{10,11... | collective-permute-start | bytes 1572872 | tf_op jit(solution)/shard_map/ppermute | solution.py:165
  109.3 1.5 row_sums.2
  110.8 2.4 %collective-permute-start.3 = (f32[512,256]{1,0:T(8,128)S(1)}, f32[512,256]{1,0:T(8,128)S(1)}, u32[]{:S(2)}, u32[]{:S(2)}) collective-permute-start(f32[512,256]{1,0:T(8,128)S(1)} %get-tuple-element.18), channel_id=1, source_target_pairs={{0,1},{1,0},{2,3},{3,2},{4,5},{5,4},{6,7},{7,6},{8,9},{9,8},{10,11... | collective-permute-start | bytes 1572872 | tf_op jit(solution)/shard_map/ppermute | solution.py:165
  113.2 0.1 add.40
  113.3 2.4 %collective-permute-start.5 = (f32[512,256]{1,0:T(8,128)S(1)}, f32[512,256]{1,0:T(8,128)S(1)}, u32[]{:S(2)}, u32[]{:S(2)}) collective-permute-start(f32[512,256]{1,0:T(8,128)S(1)} %add.40), channel_id=1, source_target_pairs={{0,408},{408,0},{24,384},{384,24},{1,409},{409,1},{25,385},{385,25... | collective-permute-start | bytes 1572872 | tf_op jit(solution)/shard_map/ppermute | solution.py:169
  115.8 13.3 %collective-permute-done.5 = f32[512,256]{1,0:T(8,128)S(1)} collective-permute-done((f32[512,256]{1,0:T(8,128)S(1)}, f32[512,256]{1,0:T(8,128)S(1)}, u32[]{:S(2)}, u32[]{:S(2)}) %collective-permute-start.5) | collective-permute-done | bytes 524320 | tf_op jit(solution)/shard_map/ppermute | solution.py:169
  129.0 0.1 add_add_fusion
  129.1 24.5 %all_to_all.21 = f32[16,32,256]{2,1,0:T(8,128)S(1)} all-to-all(f32[16,32,256]{2,1,0:T(8,128)S(1)} %bitcast.18), channel_id=1, replica_groups=mesh['xl'=2,'y'=8,'xh'=2,'z'=12,'c'=2] {'xl','y'}, dimensions={0} | all-to-all | bytes 1048576 | tf_op jit(solution)/shard_map/all_to_all | solution.py:195
  153.7 18.8 %all_to_all.22 = f32[16,32,256]{2,1,0:T(8,128)S(1)} all-to-all(f32[16,32,256]{2,1,0:T(8,128)S(1)} %broadcast_in_dim.5), channel_id=1, replica_groups=mesh['xl'=2,'y'=8,'xh'=2,'z'=12,'c'=2] {'xl','y'}, dimensions={0} | all-to-all | bytes 1048576 | tf_op jit(solution)/shard_map/all_to_all | solution.py:197
  172.5 0.1 multiply_reduce_fusion
  172.7 0.1 div.18
  172.8 0.6 fusion.1
  173.4 0.9 fusion
  (13 shorter events, 0.1 us)
Async XLA Ops:
  0.6 38.8 %copy-start = (f32[512,256]{1,0:T(8,128)S(1)}, f32[512,256]{1,0:T(8,128)}, u32[]{:S(2)}) copy-start(f32[512,256]{1,0:T(8,128)} %own_ref.1) | copy-start | bytes 1572868
  0.6 32.7 %collective-permute-start = (f32[512,256]{1,0:T(8,128)}, f32[512,256]{1,0:T(8,128)S(1)}, u32[]{:S(2)}, u32[]{:S(2)}) collective-permute-start(f32[512,256]{1,0:T(8,128)} %own_ref.1), channel_id=1, source_target_pairs={{0,408},{408,0},{24,384},{384,24},{1,409},{409,1},{25,385},{385,25... | collective-permute-start | bytes 1572872 | tf_op jit(solution)/shard_map/ppermute | solution.py:169
  5.6 27.7 %all-to-all-start = ((s32[12,24,128]{2,1,0:T(8,128)}), s32[12,24,128]{2,1,0:T(8,128)S(1)}, u32[]{:S(2)}, u32[]{:S(2)}) async-start(s32[12,24,128]{2,1,0:T(8,128)} %broadcast_in_dim.4), calls=%async_computation | async-start | bytes 294912 | tf_op jit(solution)/shard_map/all_to_all | solution.py:180
  20.7 18.7 %collective-permute-start.1 = (f32[512,256]{1,0:T(8,128)}, f32[512,256]{1,0:T(8,128)S(1)}, u32[]{:S(2)}, u32[]{:S(2)}) collective-permute-start(f32[512,256]{1,0:T(8,128)} %own_ref.1), channel_id=1, source_target_pairs={{0,1},{1,0},{2,3},{3,2},{4,5},{5,4},{6,7},{7,6},{8,9},{9,8},{10,11... | collective-permute-start | bytes 1572872 | tf_op jit(solution)/shard_map/ppermute | solution.py:165
  33.3 6.2 %collective-permute-start.2 = (f32[512,256]{1,0:T(8,128)S(1)}, f32[512,256]{1,0:T(8,128)S(1)}, u32[]{:S(2)}, u32[]{:S(2)}) collective-permute-start(f32[512,256]{1,0:T(8,128)S(1)} %collective-permute-done.far_ref), channel_id=1, source_target_pairs={{0,1},{1,0},{2,3},{3,2},{4,5},{5,4},{6,7},{7,6},{8,9},{9,8},{10,11... | collective-permute-start | bytes 1572872 | tf_op jit(solution)/shard_map/ppermute | solution.py:165
  39.4 38.5 %copy-start.1 = (f32[256,256]{1,0:T(8,128)S(1)}, f32[256,256]{1,0:T(8,128)}, u32[]{:S(2)}) copy-start(f32[256,256]{1,0:T(8,128)} %weight_ref.1) | copy-start | bytes 786436
  39.4 38.5 %copy-start.2 = (f32[64,256]{1,0:T(8,128)S(1)}, f32[64,256]{1,0:T(8,128)}, u32[]{:S(2)}) copy-start(f32[64,256]{1,0:T(8,128)} %upstream_ref.1) | copy-start | bytes 196612
  39.4 38.5 %copy-start.3 = (f32[256]{0:T(256)S(1)}, f32[256]{0:T(256)}, u32[]{:S(2)}) copy-start(f32[256]{0:T(256)} %param.10) | copy-start | bytes 3076
  107.3 5.9 %collective-permute-start.4 = (f32[512,256]{1,0:T(8,128)S(1)}, f32[512,256]{1,0:T(8,128)S(1)}, u32[]{:S(2)}, u32[]{:S(2)}) collective-permute-start(f32[512,256]{1,0:T(8,128)S(1)} %get-tuple-element.20), channel_id=1, source_target_pairs={{0,1},{1,0},{2,3},{3,2},{4,5},{5,4},{6,7},{7,6},{8,9},{9,8},{10,11... | collective-permute-start | bytes 1572872 | tf_op jit(solution)/shard_map/ppermute | solution.py:165
  110.8 5.0 %collective-permute-start.3 = (f32[512,256]{1,0:T(8,128)S(1)}, f32[512,256]{1,0:T(8,128)S(1)}, u32[]{:S(2)}, u32[]{:S(2)}) collective-permute-start(f32[512,256]{1,0:T(8,128)S(1)} %get-tuple-element.18), channel_id=1, source_target_pairs={{0,1},{1,0},{2,3},{3,2},{4,5},{5,4},{6,7},{7,6},{8,9},{9,8},{10,11... | collective-permute-start | bytes 1572872 | tf_op jit(solution)/shard_map/ppermute | solution.py:165
  113.3 15.7 %collective-permute-start.5 = (f32[512,256]{1,0:T(8,128)S(1)}, f32[512,256]{1,0:T(8,128)S(1)}, u32[]{:S(2)}, u32[]{:S(2)}) collective-permute-start(f32[512,256]{1,0:T(8,128)S(1)} %add.40), channel_id=1, source_target_pairs={{0,408},{408,0},{24,384},{384,24},{1,409},{409,1},{25,385},{385,25... | collective-permute-start | bytes 1572872 | tf_op jit(solution)/shard_map/ppermute | solution.py:169
  129.0 43.8 %copy-start.4 = (f32[512]{0:T(512)S(1)}, f32[512]{0:T(512)}, u32[]{:S(2)}) copy-start(f32[512]{0:T(512)} %param.8) | copy-start | bytes 6148

commit v3 on v2

v3 whole, which is shorter than its diff:
```python
import functools

import jax
import jax.numpy as jnp
from jax import lax
from jax.experimental import pallas as pl
from jax.experimental.pallas import tpu as pltpu
from jax.sharding import Mesh
from jax.sharding import PartitionSpec as P

AXES = ("xl", "y", "xh", "z", "c")
SIZES = (2, 8, 2, 12, 2)
NZ = 12
LANES = 128
FIELDS, BITS = 6, 5
PARAMS = pltpu.CompilerParams(vmem_limit_bytes=16 * 1024 * 1024)
SCALARS = pl.BlockSpec(memory_space=pltpu.SMEM)
WHOLE = pl.BlockSpec(memory_space=pltpu.VMEM)


def split_halves(x):
    high = x.astype(jnp.bfloat16)
    return high, (x - high.astype(jnp.float32)).astype(jnp.bfloat16)


def spread_kernel(ids_ref, out_ref):
    bag, per = ids_ref.shape
    half = bag // 2
    ids = jnp.concatenate([ids_ref[:half], ids_ref[half:]], axis=1)
    ids = jnp.concatenate([ids, jnp.zeros((out_ref.shape[1] - half, 2 * per), jnp.int32)], axis=0)
    for k in range(out_ref.shape[0]):
        out_ref[k] = ids


def spread(ids, copies):
    bag, per = ids.shape
    return pl.pallas_call(
        spread_kernel,
        out_shape=jax.ShapeDtypeStruct((copies, -(-bag // 16) * 8, 2 * per), jnp.int32),
        in_specs=[WHOLE],
        out_specs=WHOLE,
        compiler_params=PARAMS,
        name="spread",
    )(ids)


def count_kernel(bag, per, base_ref, ids_ref, out_ref):
    assert bag < 1 << BITS
    rows = out_ref.shape[0] // 4
    pieces = 4 * rows // LANES
    words = -(-pieces // FIELDS)
    part = 32

    def two_blocks(i, _):
        one, two = ids_ref[2 * i, : bag // 2], ids_ref[2 * i + 1, : bag // 2]
        ids = jnp.concatenate(
            [
                jnp.concatenate([one[:, :per], two[:, :per]], axis=1),
                jnp.concatenate([one[:, per:], two[:, per:]], axis=1),
            ],
            axis=0,
        )
        columns = pl.ds(pl.multiple_of(i * LANES, LANES), LANES)
        line = ids & (LANES - 1)
        piece = jnp.full(ids.shape, -1, jnp.int32)
        for q in range(4):
            local = ids - base_ref[q]
            piece = jnp.where((local >= 0) & (local < rows), (q * rows + local) >> 7, piece)
        values = []
        for t in range(words):
            field = piece - t * FIELDS
            inside = (field >= 0) & (field < FIELDS) & (piece >= 0)
            values.append(jnp.where(inside, jnp.int32(1) << jnp.where(inside, field, 0) * BITS, 0))
        for first in range(0, LANES, part):
            lines = lax.broadcasted_iota(jnp.int32, (part, LANES), 0) + first
            sums = [jnp.zeros((part, LANES), jnp.int32) for _ in range(words)]
            for j in range(bag):
                hit = line[j : j + 1] == lines
                for t in range(words):
                    sums[t] = sums[t] + jnp.where(hit, values[t][j : j + 1], 0)
            for p in range(pieces):
                count = (sums[p // FIELDS] >> (BITS * (p % FIELDS))) & ((1 << BITS) - 1)
                at = p * LANES + first
                out_ref[at : at + part, columns] = count.astype(jnp.float32).astype(jnp.bfloat16)
        return 0

    lax.fori_loop(0, ids_ref.shape[0] // 2, two_blocks, 0)


def count_rows(places, ids, bag, per, rows):
    return pl.pallas_call(
        functools.partial(count_kernel, bag, per),
        out_shape=jax.ShapeDtypeStruct((4 * rows, ids.shape[0] * per), jnp.bfloat16),
        in_specs=[SCALARS, WHOLE],
        out_specs=WHOLE,
        compiler_params=PARAMS,
        name="count_rows",
    )(places, ids)


def pool_kernel(tile, places_ref, counts_ref, own_ref, own_c_ref, far_ref, far_c_ref, out_ref, halves):
    rows, width = own_ref.shape
    for place, ref in ((4, own_ref), (5, own_c_ref), (6, far_ref), (7, far_c_ref)):
        high, low = split_halves(ref[...])
        at = places_ref[place]
        halves[at, :, :width] = high
        halves[at, :, width:] = low

    def some_samples(i, _):
        some = pl.ds(pl.multiple_of(i * tile, tile), tile)
        total = None
        for p in range(4):
            term = lax.dot_general(
                counts_ref[p * rows : (p + 1) * rows, some],
                halves[p],
                (((0,), (0,)), ((), ())),
                preferred_element_type=jnp.float32,
            )
            total = term if total is None else total + term
        out_ref[some, :] = total[:, :width] + total[:, width:]
        return 0

    lax.fori_loop(0, counts_ref.shape[1] // tile, some_samples, 0)


def pool(places, counts, tables, tile=256):
    rows, width = tables[0].shape
    return pl.pallas_call(
        functools.partial(pool_kernel, tile),
        out_shape=jax.ShapeDtypeStruct((counts.shape[1], width), jnp.float32),
        in_specs=[SCALARS] + [WHOLE] * 5,
        out_specs=WHOLE,
        scratch_shapes=[pltpu.VMEM((4, rows, 2 * width), jnp.bfloat16)],
        compiler_params=PARAMS,
        name="pool",
    )(places, counts, *tables)


def dot3(a, b, dims):
    a_high, a_low = split_halves(a)
    b_high, b_low = split_halves(b)

    def dot(u, v):
        return lax.dot_general(u, v, (dims, ((), ())), preferred_element_type=jnp.float32)

    return dot(a_high, b_high) + (dot(a_high, b_low) + dot(a_low, b_high))


def cross_kernel(places_ref, parts_ref, weight_ref, bias_ref, upstream_ref, crossed_ref, keep_ref, give_ref):
    pooled = parts_ref[0]
    for k in range(1, parts_ref.shape[0]):
        pooled = pooled + parts_ref[k]
    weight, upstream = weight_ref[...], upstream_ref[...]
    mixed = dot3(pooled, weight, ((1,), (0,))) + bias_ref[...]
    crossed_ref[...] = pooled * mixed + pooled
    back = upstream * mixed + dot3(upstream * pooled, weight, ((1,), (1,))) + upstream
    half = keep_ref.shape[1]
    first = places_ref[8] == 0
    keep_ref[...] = jnp.where(first, back[:, :half], back[:, half:])
    give_ref[...] = jnp.where(first, back[:, half:], back[:, :half])


def cross(places, parts, weight, bias, upstream):
    samples, width = upstream.shape
    half = jax.ShapeDtypeStruct((samples, width // 2), jnp.float32)
    return pl.pallas_call(
        cross_kernel,
        out_shape=(jax.ShapeDtypeStruct(upstream.shape, jnp.float32), half, half),
        in_specs=[SCALARS] + [WHOLE] * 4,
        out_specs=(WHOLE, WHOLE, WHOLE),
        compiler_params=PARAMS,
        name="cross",
    )(places, parts, weight, bias.reshape(1, -1), upstream)


def row_kernel(core, near_ref, far_ref, back_ref, out_ref, halves):
    blocks, per, width = back_ref.shape
    per = per // 2
    for b in range(blocks):
        high, low = split_halves(back_ref[b])
        for k in range(2):
            halves[k, b * per : (b + 1) * per, :width] = high[k * per : (k + 1) * per]
            halves[k, b * per : (b + 1) * per, width:] = low[k * per : (k + 1) * per]
    parts, _, lines, _ = out_ref.shape
    rows = parts * lines
    for h in range(2):
        chunk = slice((2 * h + core) * rows, (2 * h + core + 1) * rows)
        both = jnp.dot(near_ref[chunk, :], halves[0], preferred_element_type=jnp.float32)
        both = both + jnp.dot(far_ref[chunk, :], halves[1], preferred_element_type=jnp.float32)
        out_ref[:, h] = (both[:, :width] + both[:, width:]).reshape(parts, lines, width)


def row_sums(core, near, far, back, rows, parts):
    width = back.shape[2]
    return pl.pallas_call(
        functools.partial(row_kernel, core),
        out_shape=jax.ShapeDtypeStruct((parts, 2, rows // parts, width), jnp.float32),
        in_specs=[WHOLE] * 3,
        out_specs=WHOLE,
        scratch_shapes=[pltpu.VMEM((2, near.shape[1], 2 * width), jnp.bfloat16)],
        compiler_params=PARAMS,
        name="row_sums",
    )(near, far, back)


def adagrad_rows(rows, sums, grads):
    fresh = sums + jnp.sum(grads * grads, axis=(0, 2)) / rows.shape[1]
    scale = 0.5 / jnp.sqrt(fresh)[:, None]
    return (rows - jnp.concatenate([grads[0], grads[1]], axis=1) * scale, fresh)


def other_core(x):
    return lax.ppermute(x, "c", [(0, 1), (1, 0)])


def x_neighbour(x):
    return lax.ppermute(x, ("xl", "xh"), [(0, 3), (3, 0), (1, 2), (2, 1)])


def body(bag_ids, table, accum, cross_weight, cross_bias, upstream):
    per, bag = bag_ids.shape
    rows, width = table.shape
    xh, z, c = (lax.axis_index(a) for a in ("xh", "z", "c"))
    places = [(h * (NZ * 2) + z * 2 + d) * rows for h in (0, 1) for d in (c, 1 - c)]
    places = jnp.stack(places + [2 * xh, 2 * xh + 1, 2 - 2 * xh, 3 - 2 * xh, xh]).astype(jnp.int32)

    copies, sent = lax.optimization_barrier((spread(bag_ids.T, NZ), table))
    ids = lax.all_to_all(copies, "z", 0, 0, tiled=True)
    far = x_neighbour(sent)
    own_c = other_core(sent)
    far, ids, places = lax.optimization_barrier((far, ids, places))
    tables = (table, own_c, far, other_core(far))
    far_ids = x_neighbour(ids)
    counts = count_rows(places, ids, bag, per, rows)
    partial = pool(places, counts, tables)
    partial, far_ids = lax.optimization_barrier((partial, far_ids))
    parts = lax.all_to_all(partial.reshape(NZ, per, width), "z", 0, 0, tiled=True)
    crossed, keep, give = cross(places, parts, cross_weight, cross_bias, upstream)
    far_ids, give = lax.optimization_barrier((far_ids, give))
    far_counts = count_rows(places, far_ids, bag, per, rows)

    halves = jnp.concatenate([keep, x_neighbour(give)], axis=0)
    gathered = lax.all_gather(halves, "z", axis=0, tiled=False)
    theirs = other_core(row_sums(1, counts, far_counts, gathered, rows, 16))
    mine = row_sums(0, counts, far_counts, gathered, rows, 16) + theirs
    total = jnp.sum(lax.all_to_all(mine, ("xl", "y"), 0, 0, tiled=False), axis=0)
    copies = jnp.broadcast_to(total[:, None], (2, 16) + total.shape[1:])
    totals = lax.all_to_all(
        copies.reshape((32,) + total.shape[1:]), ("xh", "xl", "y"), 0, 0, tiled=True
    ).reshape(2, rows, width // 2)
    new_table, new_accum = adagrad_rows(table, accum, totals)
    return (crossed, new_table, new_accum)


def solution(mesh):
    fine = Mesh(mesh.devices.reshape(SIZES), AXES)
    samples = P(AXES, None)
    shard = ("xh", "z", "c")
    return jax.shard_map(
        body,
        mesh=fine,
        in_specs=(samples, P(shard, None), P(shard), P(), P(), samples),
        out_specs=(samples, P(shard, None), P(shard)),
        check_vma=False,
    )
```

time: 175 us -> 170 us (0.971)
  the two profiles are of different devices: /device:TPU:10 before, /device:TPU:8 now
where the time goes in v3:
time: 170 us
  blocking collectives  108 us (64%)
  starting transfers between devices  32.5 us (19%)
  Pallas kernels  15.1 us (9%)
  waiting for transfers between devices  10.4 us (6%)
  other arithmetic  1.87 us (1%)
    all_to_all x1, blocking collectives, body(): lax.all_to_all(partial.reshape(NZ, per, width), 'z', 0, 0, tiled=True)  35.3 us
    all_gather x1, blocking collectives, body(): gathered = lax.all_gather(halves, 'z', axis=0, tiled=False)  26.9 us
    all_to_all x1, blocking collectives, body(): lax.all_to_all(mine, ('xl', 'y'), 0, 0, tiled=False)  23 us
    all_to_all x1, blocking collectives, body(): lax.all_to_all(copies.reshape((32,) + total.shape[1:]), ('xh', 'xl', 'y')...  22.8 us
    all_to_all x1, starting transfers between devices, body(): ids = lax.all_to_all(copies, 'z', 0, 0, tiled=True)  15.2 us
    ppermute x3, starting transfers between devices, x_neighbour(): return lax.ppermute(x, ('xl', 'xh'), [(0, 3), (3, 0), (1, 2), (2, 1)])  11.6 us
    all_to_all x1, waiting for transfers between devices, body(): ids = lax.all_to_all(copies, 'z', 0, 0, tiled=True)  9.65 us
    pallas_call x2, Pallas kernels, count_rows(): pl.pallas_call(functools.partial(count_kernel, bag, per), out_shape=jax.S...  7.62 us
  transfers between devices with their start and end apart: 7, of which 2 were waited for; matrix products, arithmetic and copies ran while one was open for 0% of the time, Pallas kernels for 7%

profile of v3, /device:TPU:8, one launch (start us, length us, event | category | flops | bytes accessed | tf_op | source)
XLA Modules:
  0.0 169.8 jit_solution(9552340164576355222)
XLA Ops:
  0.6 0.0 copy-start
  0.7 0.8 copy-done.3
  1.4 0.7 spread.1
  2.1 4.7 %collective-permute-start = (f32[512,256]{1,0:T(8,128)}, f32[512,256]{1,0:T(8,128)S(1)}, u32[]{:S(2)}, u32[]{:S(2)}) collective-permute-start(f32[512,256]{1,0:T(8,128)} %own_ref.1), channel_id=1, source_target_pairs={{0,408},{408,0},{24,384},{384,24},{1,409},{409,1},{25,385},{385,25... | collective-permute-start | bytes 1572872 | tf_op jit(solution)/shard_map/ppermute | solution.py:217
  6.8 15.2 %all-to-all-start = ((s32[12,16,128]{2,1,0:T(8,128)}), s32[12,16,128]{2,1,0:T(8,128)S(1)}, u32[]{:S(2)}, u32[]{:S(2)}) async-start(s32[12,16,128]{2,1,0:T(8,128)} %spread.1), calls=%async_computation | async-start | bytes 196608 | tf_op jit(solution)/shard_map/all_to_all | solution.py:228
  22.0 1.9 %collective-permute-start.1 = (f32[512,256]{1,0:T(8,128)}, f32[512,256]{1,0:T(8,128)S(1)}, u32[]{:S(2)}, u32[]{:S(2)}) collective-permute-start(f32[512,256]{1,0:T(8,128)} %own_ref.1), channel_id=1, source_target_pairs={{0,1},{1,0},{2,3},{3,2},{4,5},{5,4},{6,7},{7,6},{8,9},{9,8},{10,11... | collective-permute-start | bytes 1572872 | tf_op jit(solution)/shard_map/ppermute | solution.py:213
  23.9 0.1 stack.39.base_ref.places_ref
  24.0 9.6 %all-to-all-done.ids_ref = s32[12,16,128]{2,1,0:T(8,128)S(1)} async-done(((s32[12,16,128]{2,1,0:T(8,128)}), s32[12,16,128]{2,1,0:T(8,128)S(1)}, u32[]{:S(2)}, u32[]{:S(2)}) %all-to-all-start) | async-done | bytes 98336 | tf_op jit(solution)/shard_map/all_to_all | solution.py:228
  33.6 1.9 %collective-permute-start.2 = (f32[512,256]{1,0:T(8,128)S(1)}, f32[512,256]{1,0:T(8,128)S(1)}, u32[]{:S(2)}, u32[]{:S(2)}) collective-permute-start(f32[512,256]{1,0:T(8,128)S(1)} %collective-permute-done.far_ref), channel_id=1, source_target_pairs={{0,1},{1,0},{2,3},{3,2},{4,5},{5,4},{6,7},{7,6},{8,9},{9,8},{10,11... | collective-permute-start | bytes 1572872 | tf_op jit(solution)/shard_map/ppermute | solution.py:213
  35.6 2.4 %collective-permute-start.3 = (s32[12,16,128]{2,1,0:T(8,128)S(1)}, s32[12,16,128]{2,1,0:T(8,128)S(1)}, u32[]{:S(2)}, u32[]{:S(2)}) collective-permute-start(s32[12,16,128]{2,1,0:T(8,128)S(1)} %all-to-all-done.ids_ref), channel_id=1, source_target_pairs={{0,408},{408,0},{24,384},{384,24},{1,409},{409,1},{25,385},{385,25... | collective-permute-start | bytes 294920 | tf_op jit(solution)/shard_map/ppermute | solution.py:217
  38.0 3.8 %count_rows.2.counts_ref.near_ref = bf16[2048,768]{1,0:T(8,128)(2,1)S(1)} custom-call(s32[9]{0:T(128)S(1)} %stack.39.base_ref.places_ref, s32[12,16,128]{2,1,0:T(8,128)S(1)} %all-to-all-done.ids_ref), custom_call_target="tpu_custom_call" | custom-call | tf_op jit(solution)/shard_map/count_rows/pallas_call | solution.py:91
  41.8 0.0 copy-start.1
  41.8 0.0 copy-start.2
  41.8 0.0 copy-start.4
  41.8 3.2 %pool.1 = f32[768,256]{1,0:T(8,128)S(1)} custom-call(s32[9]{0:T(128)S(1)} %stack.39.base_ref.places_ref, bf16[2048,768]{1,0:T(8,128)(2,1)S(1)} %count_rows.2.counts_ref.near_ref, f32[512,256]{1,0:T(8,128)S(1)} %copy-done, f32[512,256]{1,0:T(8,128)S(1)} %collective-permute-done.1.own_c_ref, f32[512,256]{1,0:T(8,128)S(1)} %collective-permute-done.far_ref, ...), custom_call_target="tpu_custom_call" | custom-call | tf_op jit(solution)/shard_map/pool/pallas_call | solution.py:128
  45.1 35.3 %all_to_all.20.parts_ref = f32[12,64,256]{2,1,0:T(8,128)S(1)} all-to-all(f32[12,64,256]{2,1,0:T(8,128)S(1)} %bitcast.18), channel_id=1, replica_groups=mesh['xl'=2,'y'=8,'xh'=2,'z'=12,'c'=2] {'z'}, dimensions={0} | all-to-all | bytes 1572864 | tf_op jit(solution)/shard_map/all_to_all | solution.py:237
  80.4 1.4 cross.1
  81.8 4.6 %collective-permute-start.4 = (f32[64,128]{1,0:T(8,128)S(1)}, f32[64,128]{1,0:T(8,128)S(1)}, u32[]{:S(2)}, u32[]{:S(2)}) collective-permute-start(f32[64,128]{1,0:T(8,128)S(1)} %get-tuple-element.26), channel_id=1, source_target_pairs={{0,408},{408,0},{24,384},{384,24},{1,409},{409,1},{25,385},{385,25... | collective-permute-start | bytes 98312 | tf_op jit(solution)/shard_map/ppermute | solution.py:217
  86.4 3.8 %count_rows.3.far_ref = bf16[2048,768]{1,0:T(8,128)(2,1)S(1)} custom-call(s32[9]{0:T(128)S(1)} %stack.39.base_ref.places_ref, s32[12,16,128]{2,1,0:T(8,128)S(1)} %collective-permute-done.3.ids_ref), custom_call_target="tpu_custom_call" | custom-call | tf_op jit(solution)/shard_map/count_rows/pallas_call | solution.py:91
  90.2 26.9 %all-gather = f32[1536,128]{1,0:T(8,128)S(1)} all-gather(f32[128,128]{1,0:T(8,128)S(1)} %pad_maximum_fusion), channel_id=2, replica_groups=mesh['xl'=2,'y'=8,'xh'=2,'z'=12,'c'=2] {'z'}, dimensions={0}, use_global_device_ids=true | all-gather | bytes 851968 | tf_op jit(solution)/shard_map/all_gather | solution.py:243
  117.1 1.1 row_sums.3
  118.2 1.9 %collective-permute-start.5 = (f32[16,2,32,128]{3,2,1,0:T(8,128)S(1)}, f32[16,2,32,128]{3,2,1,0:T(8,128)S(1)}, u32[]{:S(2)}, u32[]{:S(2)}) collective-permute-start(f32[16,2,32,128]{3,2,1,0:T(8,128)S(1)} %row_sums.3), channel_id=1, source_target_pairs={{0,1},{1,0},{2,3},{3,2},{4,5},{5,4},{6,7},{7,6},{8,9},{9,8},{10,11... | collective-permute-start | bytes 1572872 | tf_op jit(solution)/shard_map/ppermute | solution.py:213
  120.1 1.1 row_sums.2
  121.2 0.8 collective-permute-done.5
  122.0 0.1 add.31
  122.1 23.0 %all_to_all.21 = f32[16,2,32,128]{3,2,1,0:T(8,128)S(1)} all-to-all(f32[16,2,32,128]{3,2,1,0:T(8,128)S(1)} %add.31), channel_id=1, replica_groups=mesh['xl'=2,'y'=8,'xh'=2,'z'=12,'c'=2] {'xl','y'}, dimensions={0} | all-to-all | bytes 1048576 | tf_op jit(solution)/shard_map/all_to_all | solution.py:246
  145.1 0.1 broadcast_in_dim.2
  145.1 22.8 %all_to_all.22 = f32[32,32,128]{2,1,0:T(8,128)S(1)} all-to-all(f32[32,32,128]{2,1,0:T(8,128)S(1)} %bitcast.21), channel_id=1, replica_groups=mesh['xl'=2,'y'=8,'xh'=2,'z'=12,'c'=2] {'xh','xl','y'}, dimensions={0} | all-to-all | bytes 1048576 | tf_op jit(solution)/shard_map/all_to_all | solution.py:248
  167.9 0.2 multiply_reduce_fusion
  168.1 0.1 reduce_sum.27
  168.2 0.6 rsqrt_multiply_fusion
  168.8 0.9 fusion
  (16 shorter events, 0.1 us)
Async XLA Ops:
  0.6 41.2 %copy-start = (f32[512,256]{1,0:T(8,128)S(1)}, f32[512,256]{1,0:T(8,128)}, u32[]{:S(2)}) copy-start(f32[512,256]{1,0:T(8,128)} %own_ref.1) | copy-start | bytes 1572868
  0.6 0.8 copy-start.3
  2.1 31.5 %collective-permute-start = (f32[512,256]{1,0:T(8,128)}, f32[512,256]{1,0:T(8,128)S(1)}, u32[]{:S(2)}, u32[]{:S(2)}) collective-permute-start(f32[512,256]{1,0:T(8,128)} %own_ref.1), channel_id=1, source_target_pairs={{0,408},{408,0},{24,384},{384,24},{1,409},{409,1},{25,385},{385,25... | collective-permute-start | bytes 1572872 | tf_op jit(solution)/shard_map/ppermute | solution.py:217
  6.8 26.9 %all-to-all-start = ((s32[12,16,128]{2,1,0:T(8,128)}), s32[12,16,128]{2,1,0:T(8,128)S(1)}, u32[]{:S(2)}, u32[]{:S(2)}) async-start(s32[12,16,128]{2,1,0:T(8,128)} %spread.1), calls=%async_computation | async-start | bytes 196608 | tf_op jit(solution)/shard_map/all_to_all | solution.py:228
  22.0 19.9 %collective-permute-start.1 = (f32[512,256]{1,0:T(8,128)}, f32[512,256]{1,0:T(8,128)S(1)}, u32[]{:S(2)}, u32[]{:S(2)}) collective-permute-start(f32[512,256]{1,0:T(8,128)} %own_ref.1), channel_id=1, source_target_pairs={{0,1},{1,0},{2,3},{3,2},{4,5},{5,4},{6,7},{7,6},{8,9},{9,8},{10,11... | collective-permute-start | bytes 1572872 | tf_op jit(solution)/shard_map/ppermute | solution.py:213
  33.6 8.2 %collective-permute-start.2 = (f32[512,256]{1,0:T(8,128)S(1)}, f32[512,256]{1,0:T(8,128)S(1)}, u32[]{:S(2)}, u32[]{:S(2)}) collective-permute-start(f32[512,256]{1,0:T(8,128)S(1)} %collective-permute-done.far_ref), channel_id=1, source_target_pairs={{0,1},{1,0},{2,3},{3,2},{4,5},{5,4},{6,7},{7,6},{8,9},{9,8},{10,11... | collective-permute-start | bytes 1572872 | tf_op jit(solution)/shard_map/ppermute | solution.py:213
  35.6 9.5 %collective-permute-start.3 = (s32[12,16,128]{2,1,0:T(8,128)S(1)}, s32[12,16,128]{2,1,0:T(8,128)S(1)}, u32[]{:S(2)}, u32[]{:S(2)}) collective-permute-start(s32[12,16,128]{2,1,0:T(8,128)S(1)} %all-to-all-done.ids_ref), channel_id=1, source_target_pairs={{0,408},{408,0},{24,384},{384,24},{1,409},{409,1},{25,385},{385,25... | collective-permute-start | bytes 294920 | tf_op jit(solution)/shard_map/ppermute | solution.py:217
  41.8 38.6 %copy-start.1 = (f32[256,256]{1,0:T(8,128)S(1)}, f32[256,256]{1,0:T(8,128)}, u32[]{:S(2)}) copy-start(f32[256,256]{1,0:T(8,128)} %weight_ref.1) | copy-start | bytes 786436
  41.8 38.6 %copy-start.2 = (f32[64,256]{1,0:T(8,128)S(1)}, f32[64,256]{1,0:T(8,128)}, u32[]{:S(2)}) copy-start(f32[64,256]{1,0:T(8,128)} %upstream_ref.1) | copy-start | bytes 196612
  41.8 38.6 %copy-start.4 = (f32[256]{0:T(256)S(1)}, f32[256]{0:T(256)}, u32[]{:S(2)}) copy-start(f32[256]{0:T(256)} %param.10) | copy-start | bytes 3076
  81.8 8.4 %collective-permute-start.4 = (f32[64,128]{1,0:T(8,128)S(1)}, f32[64,128]{1,0:T(8,128)S(1)}, u32[]{:S(2)}, u32[]{:S(2)}) collective-permute-start(f32[64,128]{1,0:T(8,128)S(1)} %get-tuple-element.26), channel_id=1, source_target_pairs={{0,408},{408,0},{24,384},{384,24},{1,409},{409,1},{25,385},{385,25... | collective-permute-start | bytes 98312 | tf_op jit(solution)/shard_map/ppermute | solution.py:217
  118.2 3.8 %collective-permute-start.5 = (f32[16,2,32,128]{3,2,1,0:T(8,128)S(1)}, f32[16,2,32,128]{3,2,1,0:T(8,128)S(1)}, u32[]{:S(2)}, u32[]{:S(2)}) collective-permute-start(f32[16,2,32,128]{3,2,1,0:T(8,128)S(1)} %row_sums.3), channel_id=1, source_target_pairs={{0,1},{1,0},{2,3},{3,2},{4,5},{5,4},{6,7},{7,6},{8,9},{9,8},{10,11... | collective-permute-start | bytes 1572872 | tf_op jit(solution)/shard_map/ppermute | solution.py:213
  121.2 47.0 %copy-start.5 = (f32[512]{0:T(512)S(1)}, f32[512]{0:T(512)}, u32[]{:S(2)}) copy-start(f32[512]{0:T(512)} %param.8) | copy-start | bytes 6148

commit v4 on v3

--- a/solution.py
+++ b/solution.py
@@ -181,20 +181,19 @@
         for k in range(2):
             halves[k, b * per : (b + 1) * per, :width] = high[k * per : (k + 1) * per]
             halves[k, b * per : (b + 1) * per, width:] = low[k * per : (k + 1) * per]
-    parts, _, lines, _ = out_ref.shape
-    rows = parts * lines
+    rows = out_ref.shape[1]
     for h in range(2):
         chunk = slice((2 * h + core) * rows, (2 * h + core + 1) * rows)
         both = jnp.dot(near_ref[chunk, :], halves[0], preferred_element_type=jnp.float32)
         both = both + jnp.dot(far_ref[chunk, :], halves[1], preferred_element_type=jnp.float32)
-        out_ref[:, h] = (both[:, :width] + both[:, width:]).reshape(parts, lines, width)
-
-
-def row_sums(core, near, far, back, rows, parts):
+        out_ref[h] = both[:, :width] + both[:, width:]
+
+
+def row_sums(core, near, far, back, rows):
     width = back.shape[2]
     return pl.pallas_call(
         functools.partial(row_kernel, core),
-        out_shape=jax.ShapeDtypeStruct((parts, 2, rows // parts, width), jnp.float32),
+        out_shape=jax.ShapeDtypeStruct((2, rows, width), jnp.float32),
         in_specs=[WHOLE] * 3,
         out_specs=WHOLE,
         scratch_shapes=[pltpu.VMEM((2, near.shape[1], 2 * width), jnp.bfloat16)],
@@ -203,10 +202,56 @@
     )(near, far, back)
 
 
-def adagrad_rows(rows, sums, grads):
-    fresh = sums + jnp.sum(grads * grads, axis=(0, 2)) / rows.shape[1]
-    scale = 0.5 / jnp.sqrt(fresh)[:, None]
-    return (rows - jnp.concatenate([grads[0], grads[1]], axis=1) * scale, fresh)
+def merge_kernel(parts_ref, out_ref):
+    n, width = parts_ref.shape[0] // 2, parts_ref.shape[2]
+    for h in range(2):
+        total = parts_ref[h * n]
+        for k in range(1, n):
+            total = total + parts_ref[h * n + k]
+        for k in range(out_ref.shape[0]):
+            out_ref[k, :, h * width : (h + 1) * width] = total
+
+
+def merge(parts, copies):
+    _, lines, width = parts.shape
+    return pl.pallas_call(
+        merge_kernel,
+        out_shape=jax.ShapeDtypeStruct((copies, lines, 2 * width), jnp.float32),
+        in_specs=[WHOLE],
+        out_specs=WHOLE,
+        compiler_params=PARAMS,
+        name="merge",
+    )(parts)
+
+
+def adagrad_kernel(rows_ref, sums_ref, grads_ref, new_rows_ref, new_sums_ref):
+    grads = grads_ref[...]
+    lines, width = grads.shape
+    at = (lines, lines)
+    diagonal = lax.broadcasted_iota(jnp.int32, at, 0) == lax.broadcasted_iota(jnp.int32, at, 1)
+    sums = jnp.sum(jnp.where(diagonal, sums_ref[0], 0.0), axis=1, keepdims=True)
+    fresh = sums + jnp.sum(grads * grads, axis=1, keepdims=True) / width
+    new_rows_ref[...] = rows_ref[...] - 0.5 * grads / jnp.sqrt(fresh)
+    new_sums_ref[0] = jnp.sum(jnp.where(diagonal, fresh, 0.0), axis=0, keepdims=True)
+
+
+def adagrad(rows, sums, grads):
+    count, width = rows.shape
+    block = pl.BlockSpec((LANES, width), lambda i: (i, 0))
+    line = pl.BlockSpec((1, 1, LANES), lambda i: (i, 0, 0))
+    new_rows, new_sums = pl.pallas_call(
+        adagrad_kernel,
+        out_shape=(
+            jax.ShapeDtypeStruct(rows.shape, jnp.float32),
+            jax.ShapeDtypeStruct((count // LANES, 1, LANES), jnp.float32),
+        ),
+        grid=(count // LANES,),
+        in_specs=[block, line, block],
+        out_specs=(block, line),
+        compiler_params=PARAMS,
+        name="adagrad",
+    )(rows, sums.reshape(-1, 1, LANES), grads)
+    return new_rows, new_sums.reshape(-1)
 
 
 def other_core(x):
@@ -241,14 +286,12 @@
 
     halves = jnp.concatenate([keep, x_neighbour(give)], axis=0)
     gathered = lax.all_gather(halves, "z", axis=0, tiled=False)
-    theirs = other_core(row_sums(1, counts, far_counts, gathered, rows, 16))
-    mine = row_sums(0, counts, far_counts, gathered, rows, 16) + theirs
-    total = jnp.sum(lax.all_to_all(mine, ("xl", "y"), 0, 0, tiled=False), axis=0)
-    copies = jnp.broadcast_to(total[:, None], (2, 16) + total.shape[1:])
-    totals = lax.all_to_all(
-        copies.reshape((32,) + total.shape[1:]), ("xh", "xl", "y"), 0, 0, tiled=True
-    ).reshape(2, rows, width // 2)
-    new_table, new_accum = adagrad_rows(table, accum, totals)
+    theirs = other_core(row_sums(1, counts, far_counts, gathered, rows))
+    mine = row_sums(0, counts, far_counts, gathered, rows) + theirs
+    part = rows // 16
+    got = lax.all_to_all(mine.reshape(32, part, width // 2), ("xh", "xl", "y"), 0, 0, tiled=True)
+    totals = lax.all_to_all(merge(got, 16), ("xl", "y"), 0, 0, tiled=True).reshape(rows, width)
+    new_table, new_accum = adagrad(table, accum, totals)
     return (crossed, new_table, new_accum)
 
 

time: 170 us -> 168 us (0.988)
  the two profiles are of different devices: /device:TPU:8 before, /device:TPU:10 now
where the time goes in v4:
time: 168 us
  blocking collectives  109 us (65%)
  starting transfers between devices  30.1 us (18%)
  Pallas kernels  16.9 us (10%)
  waiting for transfers between devices  10.4 us (6%)
    all_to_all x1, blocking collectives, body(): lax.all_to_all(partial.reshape(NZ, per, width), 'z', 0, 0, tiled=True)  35.2 us
    all_to_all x1, blocking collectives, body(): lax.all_to_all(mine.reshape(32, part, width // 2), ('xh', 'xl', 'y'), 0,...  27.2 us
    all_gather x1, blocking collectives, body(): gathered = lax.all_gather(halves, 'z', axis=0, tiled=False)  26.9 us
    all_to_all x1, blocking collectives, body(): lax.all_to_all(merge(got, 16), ('xl', 'y'), 0, 0, tiled=True)  19.3 us
    all_to_all x1, starting transfers between devices, body(): ids = lax.all_to_all(copies, 'z', 0, 0, tiled=True)  15.2 us
    all_to_all x1, waiting for transfers between devices, body(): ids = lax.all_to_all(copies, 'z', 0, 0, tiled=True)  9.65 us
    ppermute x3, starting transfers between devices, x_neighbour(): return lax.ppermute(x, ('xl', 'xh'), [(0, 3), (3, 0), (1, 2), (2, 1)])  9.22 us
    pallas_call x2, Pallas kernels, count_rows(): pl.pallas_call(functools.partial(count_kernel, bag, per), out_shape=jax.S...  7.62 us
  transfers between devices with their start and end apart: 7, of which 2 were waited for; matrix products, arithmetic and copies ran while one was open for 0% of the time, Pallas kernels for 7%

profile of v4, /device:TPU:10, one launch (start us, length us, event | category | flops | bytes accessed | tf_op | source)
XLA Modules:
  0.0 167.9 jit_solution(3549250421248382680)
XLA Ops:
  0.6 0.0 copy-start
  0.7 0.8 copy-done.3
  1.4 0.7 spread.1
  2.1 3.4 %collective-permute-start = (f32[512,256]{1,0:T(8,128)}, f32[512,256]{1,0:T(8,128)S(1)}, u32[]{:S(2)}, u32[]{:S(2)}) collective-permute-start(f32[512,256]{1,0:T(8,128)} %rows_ref.1), channel_id=1, source_target_pairs={{0,408},{408,0},{24,384},{384,24},{1,409},{409,1},{25,385},{385,25... | collective-permute-start | bytes 1572872 | tf_op jit(solution)/shard_map/ppermute | solution.py:262
  5.5 15.2 %all-to-all-start = ((s32[12,16,128]{2,1,0:T(8,128)}), s32[12,16,128]{2,1,0:T(8,128)S(1)}, u32[]{:S(2)}, u32[]{:S(2)}) async-start(s32[12,16,128]{2,1,0:T(8,128)} %spread.1), calls=%async_computation | async-start | bytes 196608 | tf_op jit(solution)/shard_map/all_to_all | solution.py:273
  20.7 1.9 %collective-permute-start.1 = (f32[512,256]{1,0:T(8,128)}, f32[512,256]{1,0:T(8,128)S(1)}, u32[]{:S(2)}, u32[]{:S(2)}) collective-permute-start(f32[512,256]{1,0:T(8,128)} %rows_ref.1), channel_id=1, source_target_pairs={{0,1},{1,0},{2,3},{3,2},{4,5},{5,4},{6,7},{7,6},{8,9},{9,8},{10,11... | collective-permute-start | bytes 1572872 | tf_op jit(solution)/shard_map/ppermute | solution.py:258
  22.6 0.1 stack.39.base_ref.places_ref
  22.7 9.6 %all-to-all-done.ids_ref = s32[12,16,128]{2,1,0:T(8,128)S(1)} async-done(((s32[12,16,128]{2,1,0:T(8,128)}), s32[12,16,128]{2,1,0:T(8,128)S(1)}, u32[]{:S(2)}, u32[]{:S(2)}) %all-to-all-start) | async-done | bytes 98336 | tf_op jit(solution)/shard_map/all_to_all | solution.py:273
  32.4 0.0 collective-permute-done.far_ref
  32.4 1.9 %collective-permute-start.2 = (f32[512,256]{1,0:T(8,128)S(1)}, f32[512,256]{1,0:T(8,128)S(1)}, u32[]{:S(2)}, u32[]{:S(2)}) collective-permute-start(f32[512,256]{1,0:T(8,128)S(1)} %collective-permute-done.far_ref), channel_id=1, source_target_pairs={{0,1},{1,0},{2,3},{3,2},{4,5},{5,4},{6,7},{7,6},{8,9},{9,8},{10,11... | collective-permute-start | bytes 1572872 | tf_op jit(solution)/shard_map/ppermute | solution.py:258
  34.3 2.4 %collective-permute-start.3 = (s32[12,16,128]{2,1,0:T(8,128)S(1)}, s32[12,16,128]{2,1,0:T(8,128)S(1)}, u32[]{:S(2)}, u32[]{:S(2)}) collective-permute-start(s32[12,16,128]{2,1,0:T(8,128)S(1)} %all-to-all-done.ids_ref), channel_id=1, source_target_pairs={{0,408},{408,0},{24,384},{384,24},{1,409},{409,1},{25,385},{385,25... | collective-permute-start | bytes 294920 | tf_op jit(solution)/shard_map/ppermute | solution.py:262
  36.8 3.8 %count_rows.2.counts_ref.near_ref = bf16[2048,768]{1,0:T(8,128)(2,1)S(1)} custom-call(s32[9]{0:T(128)S(1)} %stack.39.base_ref.places_ref, s32[12,16,128]{2,1,0:T(8,128)S(1)} %all-to-all-done.ids_ref), custom_call_target="tpu_custom_call" | custom-call | tf_op jit(solution)/shard_map/count_rows/pallas_call | solution.py:91
  40.6 0.0 copy-start.1
  40.6 0.0 copy-start.2
  40.6 0.0 copy-start.5
  40.6 0.0 collective-permute-done.1.own_c_ref
  40.6 3.2 %pool.1 = f32[768,256]{1,0:T(8,128)S(1)} custom-call(s32[9]{0:T(128)S(1)} %stack.39.base_ref.places_ref, bf16[2048,768]{1,0:T(8,128)(2,1)S(1)} %count_rows.2.counts_ref.near_ref, f32[512,256]{1,0:T(8,128)S(1)} %copy-done, f32[512,256]{1,0:T(8,128)S(1)} %collective-permute-done.1.own_c_ref, f32[512,256]{1,0:T(8,128)S(1)} %collective-permute-done.far_ref, ...), custom_call_target="tpu_custom_call" | custom-call | tf_op jit(solution)/shard_map/pool/pallas_call | solution.py:128
  43.8 35.2 %all_to_all.20.parts_ref = f32[12,64,256]{2,1,0:T(8,128)S(1)} all-to-all(f32[12,64,256]{2,1,0:T(8,128)S(1)} %bitcast.19), channel_id=1, replica_groups=mesh['xl'=2,'y'=8,'xh'=2,'z'=12,'c'=2] {'z'}, dimensions={0} | all-to-all | bytes 1572864 | tf_op jit(solution)/shard_map/all_to_all | solution.py:282
  79.1 1.4 cross.1
  80.5 3.4 %collective-permute-start.4 = (f32[64,128]{1,0:T(8,128)S(1)}, f32[64,128]{1,0:T(8,128)S(1)}, u32[]{:S(2)}, u32[]{:S(2)}) collective-permute-start(f32[64,128]{1,0:T(8,128)S(1)} %get-tuple-element.28), channel_id=1, source_target_pairs={{0,408},{408,0},{24,384},{384,24},{1,409},{409,1},{25,385},{385,25... | collective-permute-start | bytes 98312 | tf_op jit(solution)/shard_map/ppermute | solution.py:262
  83.9 3.8 %count_rows.3.far_ref = bf16[2048,768]{1,0:T(8,128)(2,1)S(1)} custom-call(s32[9]{0:T(128)S(1)} %stack.39.base_ref.places_ref, s32[12,16,128]{2,1,0:T(8,128)S(1)} %collective-permute-done.3.ids_ref), custom_call_target="tpu_custom_call" | custom-call | tf_op jit(solution)/shard_map/count_rows/pallas_call | solution.py:91
  87.8 26.9 %all-gather = f32[1536,128]{1,0:T(8,128)S(1)} all-gather(f32[128,128]{1,0:T(8,128)S(1)} %pad_maximum_fusion), channel_id=2, replica_groups=mesh['xl'=2,'y'=8,'xh'=2,'z'=12,'c'=2] {'z'}, dimensions={0}, use_global_device_ids=true | all-gather | bytes 851968 | tf_op jit(solution)/shard_map/all_gather | solution.py:288
  114.6 1.1 row_sums.3
  115.7 1.9 %collective-permute-start.5 = (f32[2,512,128]{2,1,0:T(8,128)S(1)}, f32[2,512,128]{2,1,0:T(8,128)S(1)}, u32[]{:S(2)}, u32[]{:S(2)}) collective-permute-start(f32[2,512,128]{2,1,0:T(8,128)S(1)} %row_sums.3), channel_id=1, source_target_pairs={{0,1},{1,0},{2,3},{3,2},{4,5},{5,4},{6,7},{7,6},{8,9},{9,8},{10,11... | collective-permute-start | bytes 1572872 | tf_op jit(solution)/shard_map/ppermute | solution.py:258
  117.6 1.1 row_sums.2
  118.7 0.0 copy-start.4
  118.7 0.8 collective-permute-done.5
  119.5 0.1 add.28
  119.6 27.2 %all_to_all.21.parts_ref = f32[32,32,128]{2,1,0:T(8,128)S(1)} all-to-all(f32[32,32,128]{2,1,0:T(8,128)S(1)} %bitcast.24), channel_id=1, replica_groups=mesh['xl'=2,'y'=8,'xh'=2,'z'=12,'c'=2] {'xh','xl','y'}, dimensions={0} | all-to-all | bytes 1048576 | tf_op jit(solution)/shard_map/all_to_all | solution.py:292
  146.8 0.1 merge.1
  146.9 19.3 %all_to_all.22 = f32[16,32,256]{2,1,0:T(8,128)S(1)} all-to-all(f32[16,32,256]{2,1,0:T(8,128)S(1)} %merge.1), channel_id=1, replica_groups=mesh['xl'=2,'y'=8,'xh'=2,'z'=12,'c'=2] {'xl','y'}, dimensions={0} | all-to-all | bytes 1048576 | tf_op jit(solution)/shard_map/all_to_all | solution.py:293
  166.2 1.7 %adagrad.1 = (f32[512,256]{1,0:T(8,128)}, f32[4,1,128]{2,1,0:T(1,128)}) custom-call(f32[512,256]{1,0:T(8,128)S(1)} %copy-done, f32[4,1,128]{2,1,0:T(1,128)S(1)} %bitcast.22, f32[512,256]{1,0:T(8,128)S(1)} %bitcast.20), custom_call_target="tpu_custom_call" | custom-call | tf_op jit(solution)/shard_map/adagrad/pallas_call | solution.py:242
  (10 shorter events, 0.0 us)
Async XLA Ops:
  0.6 40.0 %copy-start = (f32[512,256]{1,0:T(8,128)S(1)}, f32[512,256]{1,0:T(8,128)}, u32[]{:S(2)}) copy-start(f32[512,256]{1,0:T(8,128)} %rows_ref.1) | copy-start | bytes 1572868
  0.6 0.8 copy-start.3
  2.1 30.3 %collective-permute-start = (f32[512,256]{1,0:T(8,128)}, f32[512,256]{1,0:T(8,128)S(1)}, u32[]{:S(2)}, u32[]{:S(2)}) collective-permute-start(f32[512,256]{1,0:T(8,128)} %rows_ref.1), channel_id=1, source_target_pairs={{0,408},{408,0},{24,384},{384,24},{1,409},{409,1},{25,385},{385,25... | collective-permute-start | bytes 1572872 | tf_op jit(solution)/shard_map/ppermute | solution.py:262
  5.5 26.9 %all-to-all-start = ((s32[12,16,128]{2,1,0:T(8,128)}), s32[12,16,128]{2,1,0:T(8,128)S(1)}, u32[]{:S(2)}, u32[]{:S(2)}) async-start(s32[12,16,128]{2,1,0:T(8,128)} %spread.1), calls=%async_computation | async-start | bytes 196608 | tf_op jit(solution)/shard_map/all_to_all | solution.py:273
  20.7 19.9 %collective-permute-start.1 = (f32[512,256]{1,0:T(8,128)}, f32[512,256]{1,0:T(8,128)S(1)}, u32[]{:S(2)}, u32[]{:S(2)}) collective-permute-start(f32[512,256]{1,0:T(8,128)} %rows_ref.1), channel_id=1, source_target_pairs={{0,1},{1,0},{2,3},{3,2},{4,5},{5,4},{6,7},{7,6},{8,9},{9,8},{10,11... | collective-permute-start | bytes 1572872 | tf_op jit(solution)/shard_map/ppermute | solution.py:258
  32.4 8.2 %collective-permute-start.2 = (f32[512,256]{1,0:T(8,128)S(1)}, f32[512,256]{1,0:T(8,128)S(1)}, u32[]{:S(2)}, u32[]{:S(2)}) collective-permute-start(f32[512,256]{1,0:T(8,128)S(1)} %collective-permute-done.far_ref), channel_id=1, source_target_pairs={{0,1},{1,0},{2,3},{3,2},{4,5},{5,4},{6,7},{7,6},{8,9},{9,8},{10,11... | collective-permute-start | bytes 1572872 | tf_op jit(solution)/shard_map/ppermute | solution.py:258
  34.3 9.5 %collective-permute-start.3 = (s32[12,16,128]{2,1,0:T(8,128)S(1)}, s32[12,16,128]{2,1,0:T(8,128)S(1)}, u32[]{:S(2)}, u32[]{:S(2)}) collective-permute-start(s32[12,16,128]{2,1,0:T(8,128)S(1)} %all-to-all-done.ids_ref), channel_id=1, source_target_pairs={{0,408},{408,0},{24,384},{384,24},{1,409},{409,1},{25,385},{385,25... | collective-permute-start | bytes 294920 | tf_op jit(solution)/shard_map/ppermute | solution.py:262
  40.6 38.5 %copy-start.1 = (f32[256,256]{1,0:T(8,128)S(1)}, f32[256,256]{1,0:T(8,128)}, u32[]{:S(2)}) copy-start(f32[256,256]{1,0:T(8,128)} %weight_ref.1) | copy-start | bytes 786436
  40.6 38.5 %copy-start.2 = (f32[64,256]{1,0:T(8,128)S(1)}, f32[64,256]{1,0:T(8,128)}, u32[]{:S(2)}) copy-start(f32[64,256]{1,0:T(8,128)} %upstream_ref.1) | copy-start | bytes 196612
  40.6 38.5 %copy-start.5 = (f32[256]{0:T(256)S(1)}, f32[256]{0:T(256)}, u32[]{:S(2)}) copy-start(f32[256]{0:T(256)} %param.10) | copy-start | bytes 3076
  80.5 7.2 %collective-permute-start.4 = (f32[64,128]{1,0:T(8,128)S(1)}, f32[64,128]{1,0:T(8,128)S(1)}, u32[]{:S(2)}, u32[]{:S(2)}) collective-permute-start(f32[64,128]{1,0:T(8,128)S(1)} %get-tuple-element.28), channel_id=1, source_target_pairs={{0,408},{408,0},{24,384},{384,24},{1,409},{409,1},{25,385},{385,25... | collective-permute-start | bytes 98312 | tf_op jit(solution)/shard_map/ppermute | solution.py:262
  115.7 3.8 %collective-permute-start.5 = (f32[2,512,128]{2,1,0:T(8,128)S(1)}, f32[2,512,128]{2,1,0:T(8,128)S(1)}, u32[]{:S(2)}, u32[]{:S(2)}) collective-permute-start(f32[2,512,128]{2,1,0:T(8,128)S(1)} %row_sums.3), channel_id=1, source_target_pairs={{0,1},{1,0},{2,3},{3,2},{4,5},{5,4},{6,7},{7,6},{8,9},{9,8},{10,11... | collective-permute-start | bytes 1572872 | tf_op jit(solution)/shard_map/ppermute | solution.py:258
  118.7 47.5 %copy-start.4 = (f32[512]{0:T(512)S(1)}, f32[512]{0:T(512)}, u32[]{:S(2)}) copy-start(f32[512]{0:T(512)} %param.8) | copy-start | bytes 6148

commit v5 on v4

--- a/solution.py
+++ b/solution.py
@@ -203,20 +203,17 @@
 
 
 def merge_kernel(parts_ref, out_ref):
-    n, width = parts_ref.shape[0] // 2, parts_ref.shape[2]
-    for h in range(2):
-        total = parts_ref[h * n]
-        for k in range(1, n):
-            total = total + parts_ref[h * n + k]
-        for k in range(out_ref.shape[0]):
-            out_ref[k, :, h * width : (h + 1) * width] = total
+    total = parts_ref[0]
+    for k in range(1, parts_ref.shape[0]):
+        total = total + parts_ref[k]
+    for k in range(out_ref.shape[0]):
+        out_ref[k] = total
 
 
 def merge(parts, copies):
-    _, lines, width = parts.shape
     return pl.pallas_call(
         merge_kernel,
-        out_shape=jax.ShapeDtypeStruct((copies, lines, 2 * width), jnp.float32),
+        out_shape=jax.ShapeDtypeStruct((copies,) + parts.shape[1:], jnp.float32),
         in_specs=[WHOLE],
         out_specs=WHOLE,
         compiler_params=PARAMS,
@@ -225,13 +222,16 @@
 
 
 def adagrad_kernel(rows_ref, sums_ref, grads_ref, new_rows_ref, new_sums_ref):
-    grads = grads_ref[...]
-    lines, width = grads.shape
+    lines, width = rows_ref.shape
+    half = width // 2
     at = (lines, lines)
     diagonal = lax.broadcasted_iota(jnp.int32, at, 0) == lax.broadcasted_iota(jnp.int32, at, 1)
     sums = jnp.sum(jnp.where(diagonal, sums_ref[0], 0.0), axis=1, keepdims=True)
-    fresh = sums + jnp.sum(grads * grads, axis=1, keepdims=True) / width
-    new_rows_ref[...] = rows_ref[...] - 0.5 * grads / jnp.sqrt(fresh)
+    one, two = grads_ref[0], grads_ref[1]
+    fresh = sums + jnp.sum(one * one + two * two, axis=1, keepdims=True) / width
+    root = jnp.sqrt(fresh)
+    new_rows_ref[:, :half] = rows_ref[:, :half] - 0.5 * one / root
+    new_rows_ref[:, half:] = rows_ref[:, half:] - 0.5 * two / root
     new_sums_ref[0] = jnp.sum(jnp.where(diagonal, fresh, 0.0), axis=0, keepdims=True)
 
 
@@ -246,7 +246,7 @@
             jax.ShapeDtypeStruct((count // LANES, 1, LANES), jnp.float32),
         ),
         grid=(count // LANES,),
-        in_specs=[block, line, block],
+        in_specs=[block, line, pl.BlockSpec((2, LANES, width // 2), lambda i: (0, i, 0))],
         out_specs=(block, line),
         compiler_params=PARAMS,
         name="adagrad",
@@ -258,6 +258,10 @@
     return lax.ppermute(x, "c", [(0, 1), (1, 0)])
 
 
+def xl_mate(x):
+    return lax.ppermute(x, "xl", [(0, 1), (1, 0)])
+
+
 def x_neighbour(x):
     return lax.ppermute(x, ("xl", "xh"), [(0, 3), (3, 0), (1, 2), (2, 1)])
 
@@ -265,9 +269,9 @@
 def body(bag_ids, table, accum, cross_weight, cross_bias, upstream):
     per, bag = bag_ids.shape
     rows, width = table.shape
-    xh, z, c = (lax.axis_index(a) for a in ("xh", "z", "c"))
+    xl, xh, z, c = (lax.axis_index(a) for a in ("xl", "xh", "z", "c"))
     places = [(h * (NZ * 2) + z * 2 + d) * rows for h in (0, 1) for d in (c, 1 - c)]
-    places = jnp.stack(places + [2 * xh, 2 * xh + 1, 2 - 2 * xh, 3 - 2 * xh, xh]).astype(jnp.int32)
+    places = jnp.stack(places + [2 * xh, 2 * xh + 1, 2 - 2 * xh, 3 - 2 * xh, xl]).astype(jnp.int32)
 
     copies, sent = lax.optimization_barrier((spread(bag_ids.T, NZ), table))
     ids = lax.all_to_all(copies, "z", 0, 0, tiled=True)
@@ -275,23 +279,22 @@
     own_c = other_core(sent)
     far, ids, places = lax.optimization_barrier((far, ids, places))
     tables = (table, own_c, far, other_core(far))
-    far_ids = x_neighbour(ids)
+    mate_ids = xl_mate(ids)
     counts = count_rows(places, ids, bag, per, rows)
     partial = pool(places, counts, tables)
-    partial, far_ids = lax.optimization_barrier((partial, far_ids))
+    partial, mate_ids = lax.optimization_barrier((partial, mate_ids))
     parts = lax.all_to_all(partial.reshape(NZ, per, width), "z", 0, 0, tiled=True)
     crossed, keep, give = cross(places, parts, cross_weight, cross_bias, upstream)
-    far_ids, give = lax.optimization_barrier((far_ids, give))
-    far_counts = count_rows(places, far_ids, bag, per, rows)
-
-    halves = jnp.concatenate([keep, x_neighbour(give)], axis=0)
+    mate_ids, give = lax.optimization_barrier((mate_ids, give))
+    mate_counts = count_rows(places, mate_ids, bag, per, rows)
+
+    halves = jnp.concatenate([keep, xl_mate(give)], axis=0)
     gathered = lax.all_gather(halves, "z", axis=0, tiled=False)
-    theirs = other_core(row_sums(1, counts, far_counts, gathered, rows))
-    mine = row_sums(0, counts, far_counts, gathered, rows) + theirs
-    part = rows // 16
-    got = lax.all_to_all(mine.reshape(32, part, width // 2), ("xh", "xl", "y"), 0, 0, tiled=True)
-    totals = lax.all_to_all(merge(got, 16), ("xl", "y"), 0, 0, tiled=True).reshape(rows, width)
-    new_table, new_accum = adagrad(table, accum, totals)
+    theirs = other_core(row_sums(1, counts, mate_counts, gathered, rows))
+    mine = row_sums(0, counts, mate_counts, gathered, rows) + theirs
+    parts = lax.all_to_all(mine.reshape(16, rows // 8, width // 2), ("xh", "y"), 0, 0, tiled=True)
+    totals = lax.all_to_all(merge(parts, 16), ("xl", "y"), 0, 0, tiled=True)
+    new_table, new_accum = adagrad(table, accum, totals.reshape(2, rows, width // 2))
     return (crossed, new_table, new_accum)
 
 

time: 168 us -> 167 us (level)
  blocking collectives: 109 us -> 107 us
    ppermute x3 -> x1, starting transfers between devices: 9.22 us -> 3.39 us  [x_neighbour(): return lax.ppermute(x, ('xl', 'xh'), [(0, 3), (3, 0), (1, 2), (2, 1)])]
    ppermute x0 -> x2, starting transfers between devices: none -> 5.82 us  [xl_mate(): return lax.ppermute(x, 'xl', [(0, 1), (1, 0)])]
where the time goes in v5:
time: 167 us
  blocking collectives  107 us (64%)
  starting transfers between devices  30.1 us (18%)
  Pallas kernels  16.9 us (10%)
  waiting for transfers between devices  10.4 us (6%)
    all_to_all x1, blocking collectives, body(): lax.all_to_all(partial.reshape(NZ, per, width), 'z', 0, 0, tiled=True)  35.2 us
    all_gather x1, blocking collectives, body(): gathered = lax.all_gather(halves, 'z', axis=0, tiled=False)  26.9 us
    all_to_all x1, blocking collectives, body(): lax.all_to_all(mine.reshape(16, rows // 8, width // 2), ('xh', 'y'), 0, 0...  24.3 us
    all_to_all x1, blocking collectives, body(): totals = lax.all_to_all(merge(parts, 16), ('xl', 'y'), 0, 0, tiled=True)  20.8 us
    all_to_all x1, starting transfers between devices, body(): ids = lax.all_to_all(copies, 'z', 0, 0, tiled=True)  15.2 us
    all_to_all x1, waiting for transfers between devices, body(): ids = lax.all_to_all(copies, 'z', 0, 0, tiled=True)  9.64 us
    pallas_call x2, Pallas kernels, count_rows(): pl.pallas_call(functools.partial(count_kernel, bag, per), out_shape=jax.S...  7.62 us
    ppermute x2, starting transfers between devices, xl_mate(): return lax.ppermute(x, 'xl', [(0, 1), (1, 0)])  5.82 us
  transfers between devices with their start and end apart: 7, of which 2 were waited for; matrix products, arithmetic and copies ran while one was open for 0% of the time, Pallas kernels for 7%

profile of v5, /device:TPU:10, one launch (start us, length us, event | category | flops | bytes accessed | tf_op | source)
XLA Modules:
  0.0 166.5 jit_solution(1837856029452366999)
XLA Ops:
  0.6 0.0 copy-start
  0.7 0.8 copy-done.3
  1.4 0.7 spread.1
  2.1 3.4 %collective-permute-start = (f32[512,256]{1,0:T(8,128)}, f32[512,256]{1,0:T(8,128)S(1)}, u32[]{:S(2)}, u32[]{:S(2)}) collective-permute-start(f32[512,256]{1,0:T(8,128)} %rows_ref.1), channel_id=1, source_target_pairs={{0,408},{408,0},{24,384},{384,24},{1,409},{409,1},{25,385},{385,25... | collective-permute-start | bytes 1572872 | tf_op jit(solution)/shard_map/ppermute | solution.py:266
  5.5 15.2 %all-to-all-start = ((s32[12,16,128]{2,1,0:T(8,128)}), s32[12,16,128]{2,1,0:T(8,128)S(1)}, u32[]{:S(2)}, u32[]{:S(2)}) async-start(s32[12,16,128]{2,1,0:T(8,128)} %spread.1), calls=%async_computation | async-start | bytes 196608 | tf_op jit(solution)/shard_map/all_to_all | solution.py:277
  20.7 1.9 %collective-permute-start.1 = (f32[512,256]{1,0:T(8,128)}, f32[512,256]{1,0:T(8,128)S(1)}, u32[]{:S(2)}, u32[]{:S(2)}) collective-permute-start(f32[512,256]{1,0:T(8,128)} %rows_ref.1), channel_id=1, source_target_pairs={{0,1},{1,0},{2,3},{3,2},{4,5},{5,4},{6,7},{7,6},{8,9},{9,8},{10,11... | collective-permute-start | bytes 1572872 | tf_op jit(solution)/shard_map/ppermute | solution.py:258
  22.6 0.1 stack.39.base_ref.places_ref
  22.7 9.6 %all-to-all-done.ids_ref = s32[12,16,128]{2,1,0:T(8,128)S(1)} async-done(((s32[12,16,128]{2,1,0:T(8,128)}), s32[12,16,128]{2,1,0:T(8,128)S(1)}, u32[]{:S(2)}, u32[]{:S(2)}) %all-to-all-start) | async-done | bytes 98336 | tf_op jit(solution)/shard_map/all_to_all | solution.py:277
  32.4 0.0 collective-permute-done.far_ref
  32.4 1.9 %collective-permute-start.2 = (f32[512,256]{1,0:T(8,128)S(1)}, f32[512,256]{1,0:T(8,128)S(1)}, u32[]{:S(2)}, u32[]{:S(2)}) collective-permute-start(f32[512,256]{1,0:T(8,128)S(1)} %collective-permute-done.far_ref), channel_id=1, source_target_pairs={{0,1},{1,0},{2,3},{3,2},{4,5},{5,4},{6,7},{7,6},{8,9},{9,8},{10,11... | collective-permute-start | bytes 1572872 | tf_op jit(solution)/shard_map/ppermute | solution.py:258
  34.3 3.7 %collective-permute-start.3 = (s32[12,16,128]{2,1,0:T(8,128)S(1)}, s32[12,16,128]{2,1,0:T(8,128)S(1)}, u32[]{:S(2)}, u32[]{:S(2)}) collective-permute-start(s32[12,16,128]{2,1,0:T(8,128)S(1)} %all-to-all-done.ids_ref), channel_id=1, source_target_pairs={{0,384},{384,0},{1,385},{385,1},{2,386},{386,2},{3,387},{387,3},{4... | collective-permute-start | bytes 294920 | tf_op jit(solution)/shard_map/ppermute | solution.py:262
  38.0 3.8 %count_rows.2.counts_ref.near_ref = bf16[2048,768]{1,0:T(8,128)(2,1)S(1)} custom-call(s32[9]{0:T(128)S(1)} %stack.39.base_ref.places_ref, s32[12,16,128]{2,1,0:T(8,128)S(1)} %all-to-all-done.ids_ref), custom_call_target="tpu_custom_call" | custom-call | tf_op jit(solution)/shard_map/count_rows/pallas_call | solution.py:91
  41.8 0.0 copy-start.1
  41.8 0.0 copy-start.2
  41.9 0.0 copy-start.5
  41.9 0.0 collective-permute-done.2.far_c_ref
  41.9 3.2 %pool.1 = f32[768,256]{1,0:T(8,128)S(1)} custom-call(s32[9]{0:T(128)S(1)} %stack.39.base_ref.places_ref, bf16[2048,768]{1,0:T(8,128)(2,1)S(1)} %count_rows.2.counts_ref.near_ref, f32[512,256]{1,0:T(8,128)S(1)} %copy-done, f32[512,256]{1,0:T(8,128)S(1)} %collective-permute-done.1.own_c_ref, f32[512,256]{1,0:T(8,128)S(1)} %collective-permute-done.far_ref, ...), custom_call_target="tpu_custom_call" | custom-call | tf_op jit(solution)/shard_map/pool/pallas_call | solution.py:128
  45.1 35.2 %all_to_all.20.parts_ref = f32[12,64,256]{2,1,0:T(8,128)S(1)} all-to-all(f32[12,64,256]{2,1,0:T(8,128)S(1)} %bitcast.19), channel_id=1, replica_groups=mesh['xl'=2,'y'=8,'xh'=2,'z'=12,'c'=2] {'z'}, dimensions={0} | all-to-all | bytes 1572864 | tf_op jit(solution)/shard_map/all_to_all | solution.py:286
  80.3 1.4 cross.1
  81.8 2.1 %collective-permute-start.4 = (f32[64,128]{1,0:T(8,128)S(1)}, f32[64,128]{1,0:T(8,128)S(1)}, u32[]{:S(2)}, u32[]{:S(2)}) collective-permute-start(f32[64,128]{1,0:T(8,128)S(1)} %get-tuple-element.28), channel_id=1, source_target_pairs={{0,384},{384,0},{1,385},{385,1},{2,386},{386,2},{3,387},{387,3},{4... | collective-permute-start | bytes 98312 | tf_op jit(solution)/shard_map/ppermute | solution.py:262
  83.9 3.8 %count_rows.3.far_ref = bf16[2048,768]{1,0:T(8,128)(2,1)S(1)} custom-call(s32[9]{0:T(128)S(1)} %stack.39.base_ref.places_ref, s32[12,16,128]{2,1,0:T(8,128)S(1)} %collective-permute-done.3.ids_ref), custom_call_target="tpu_custom_call" | custom-call | tf_op jit(solution)/shard_map/count_rows/pallas_call | solution.py:91
  87.7 26.9 %all-gather = f32[1536,128]{1,0:T(8,128)S(1)} all-gather(f32[128,128]{1,0:T(8,128)S(1)} %pad_maximum_fusion), channel_id=2, replica_groups=mesh['xl'=2,'y'=8,'xh'=2,'z'=12,'c'=2] {'z'}, dimensions={0}, use_global_device_ids=true | all-gather | bytes 851968 | tf_op jit(solution)/shard_map/all_gather | solution.py:292
  114.7 1.1 row_sums.3
  115.8 1.9 %collective-permute-start.5 = (f32[2,512,128]{2,1,0:T(8,128)S(1)}, f32[2,512,128]{2,1,0:T(8,128)S(1)}, u32[]{:S(2)}, u32[]{:S(2)}) collective-permute-start(f32[2,512,128]{2,1,0:T(8,128)S(1)} %row_sums.3), channel_id=1, source_target_pairs={{0,1},{1,0},{2,3},{3,2},{4,5},{5,4},{6,7},{7,6},{8,9},{9,8},{10,11... | collective-permute-start | bytes 1572872 | tf_op jit(solution)/shard_map/ppermute | solution.py:258
  117.7 1.1 row_sums.2
  118.8 0.0 copy-start.4
  118.8 0.8 collective-permute-done.5
  119.6 0.1 add.28
  119.6 24.3 %all_to_all.21.parts_ref = f32[16,64,128]{2,1,0:T(8,128)S(1)} all-to-all(f32[16,64,128]{2,1,0:T(8,128)S(1)} %bitcast.24), channel_id=1, replica_groups=mesh['xl'=2,'y'=8,'xh'=2,'z'=12,'c'=2] {'xh','y'}, dimensions={0} | all-to-all | bytes 1048576 | tf_op jit(solution)/shard_map/all_to_all | solution.py:295
  143.9 0.1 merge.1
  144.0 20.8 %all_to_all.22 = f32[16,64,128]{2,1,0:T(8,128)S(1)} all-to-all(f32[16,64,128]{2,1,0:T(8,128)S(1)} %merge.1), channel_id=1, replica_groups=mesh['xl'=2,'y'=8,'xh'=2,'z'=12,'c'=2] {'xl','y'}, dimensions={0} | all-to-all | bytes 1048576 | tf_op jit(solution)/shard_map/all_to_all | solution.py:296
  164.8 1.8 %adagrad.1 = (f32[512,256]{1,0:T(8,128)}, f32[4,1,128]{2,1,0:T(1,128)}) custom-call(f32[512,256]{1,0:T(8,128)S(1)} %copy-done, f32[4,1,128]{2,1,0:T(1,128)S(1)} %bitcast.22, f32[2,512,128]{2,1,0:T(8,128)S(1)} %bitcast.20), custom_call_target="tpu_custom_call" | custom-call | tf_op jit(solution)/shard_map/adagrad/pallas_call | solution.py:242
  (10 shorter events, 0.0 us)
Async XLA Ops:
  0.6 41.3 %copy-start = (f32[512,256]{1,0:T(8,128)S(1)}, f32[512,256]{1,0:T(8,128)}, u32[]{:S(2)}) copy-start(f32[512,256]{1,0:T(8,128)} %rows_ref.1) | copy-start | bytes 1572868
  0.6 0.8 copy-start.3
  2.1 30.3 %collective-permute-start = (f32[512,256]{1,0:T(8,128)}, f32[512,256]{1,0:T(8,128)S(1)}, u32[]{:S(2)}, u32[]{:S(2)}) collective-permute-start(f32[512,256]{1,0:T(8,128)} %rows_ref.1), channel_id=1, source_target_pairs={{0,408},{408,0},{24,384},{384,24},{1,409},{409,1},{25,385},{385,25... | collective-permute-start | bytes 1572872 | tf_op jit(solution)/shard_map/ppermute | solution.py:266
  5.5 26.9 %all-to-all-start = ((s32[12,16,128]{2,1,0:T(8,128)}), s32[12,16,128]{2,1,0:T(8,128)S(1)}, u32[]{:S(2)}, u32[]{:S(2)}) async-start(s32[12,16,128]{2,1,0:T(8,128)} %spread.1), calls=%async_computation | async-start | bytes 196608 | tf_op jit(solution)/shard_map/all_to_all | solution.py:277
  20.7 21.2 %collective-permute-start.1 = (f32[512,256]{1,0:T(8,128)}, f32[512,256]{1,0:T(8,128)S(1)}, u32[]{:S(2)}, u32[]{:S(2)}) collective-permute-start(f32[512,256]{1,0:T(8,128)} %rows_ref.1), channel_id=1, source_target_pairs={{0,1},{1,0},{2,3},{3,2},{4,5},{5,4},{6,7},{7,6},{8,9},{9,8},{10,11... | collective-permute-start | bytes 1572872 | tf_op jit(solution)/shard_map/ppermute | solution.py:258
  32.4 9.5 %collective-permute-start.2 = (f32[512,256]{1,0:T(8,128)S(1)}, f32[512,256]{1,0:T(8,128)S(1)}, u32[]{:S(2)}, u32[]{:S(2)}) collective-permute-start(f32[512,256]{1,0:T(8,128)S(1)} %collective-permute-done.far_ref), channel_id=1, source_target_pairs={{0,1},{1,0},{2,3},{3,2},{4,5},{5,4},{6,7},{7,6},{8,9},{9,8},{10,11... | collective-permute-start | bytes 1572872 | tf_op jit(solution)/shard_map/ppermute | solution.py:258
  34.3 10.8 %collective-permute-start.3 = (s32[12,16,128]{2,1,0:T(8,128)S(1)}, s32[12,16,128]{2,1,0:T(8,128)S(1)}, u32[]{:S(2)}, u32[]{:S(2)}) collective-permute-start(s32[12,16,128]{2,1,0:T(8,128)S(1)} %all-to-all-done.ids_ref), channel_id=1, source_target_pairs={{0,384},{384,0},{1,385},{385,1},{2,386},{386,2},{3,387},{387,3},{4... | collective-permute-start | bytes 294920 | tf_op jit(solution)/shard_map/ppermute | solution.py:262
  41.8 38.5 %copy-start.1 = (f32[256,256]{1,0:T(8,128)S(1)}, f32[256,256]{1,0:T(8,128)}, u32[]{:S(2)}) copy-start(f32[256,256]{1,0:T(8,128)} %weight_ref.1) | copy-start | bytes 786436
  41.8 38.5 %copy-start.2 = (f32[64,256]{1,0:T(8,128)S(1)}, f32[64,256]{1,0:T(8,128)}, u32[]{:S(2)}) copy-start(f32[64,256]{1,0:T(8,128)} %upstream_ref.1) | copy-start | bytes 196612
  41.9 38.5 %copy-start.5 = (f32[256]{0:T(256)S(1)}, f32[256]{0:T(256)}, u32[]{:S(2)}) copy-start(f32[256]{0:T(256)} %param.10) | copy-start | bytes 3076
  81.8 5.9 %collective-permute-start.4 = (f32[64,128]{1,0:T(8,128)S(1)}, f32[64,128]{1,0:T(8,128)S(1)}, u32[]{:S(2)}, u32[]{:S(2)}) collective-permute-start(f32[64,128]{1,0:T(8,128)S(1)} %get-tuple-element.28), channel_id=1, source_target_pairs={{0,384},{384,0},{1,385},{385,1},{2,386},{386,2},{3,387},{387,3},{4... | collective-permute-start | bytes 98312 | tf_op jit(solution)/shard_map/ppermute | solution.py:262
  115.8 3.8 %collective-permute-start.5 = (f32[2,512,128]{2,1,0:T(8,128)S(1)}, f32[2,512,128]{2,1,0:T(8,128)S(1)}, u32[]{:S(2)}, u32[]{:S(2)}) collective-permute-start(f32[2,512,128]{2,1,0:T(8,128)S(1)} %row_sums.3), channel_id=1, source_target_pairs={{0,1},{1,0},{2,3},{3,2},{4,5},{5,4},{6,7},{7,6},{8,9},{9,8},{10,11... | collective-permute-start | bytes 1572872 | tf_op jit(solution)/shard_map/ppermute | solution.py:258
  118.8 46.0 %copy-start.4 = (f32[512]{0:T(512)S(1)}, f32[512]{0:T(512)}, u32[]{:S(2)}) copy-start(f32[512]{0:T(512)} %param.8) | copy-start | bytes 6148

commit v6 on v5

--- a/solution.py
+++ b/solution.py
@@ -27,16 +27,17 @@
     bag, per = ids_ref.shape
     half = bag // 2
     ids = jnp.concatenate([ids_ref[:half], ids_ref[half:]], axis=1)
-    ids = jnp.concatenate([ids, jnp.zeros((out_ref.shape[1] - half, 2 * per), jnp.int32)], axis=0)
-    for k in range(out_ref.shape[0]):
-        out_ref[k] = ids
+    for j in range(half):
+        out_ref[:, :, j * 2 * per : (j + 1) * 2 * per] = jnp.broadcast_to(
+            ids[j : j + 1][None], (out_ref.shape[0], 1, 2 * per)
+        )
 
 
 def spread(ids, copies):
     bag, per = ids.shape
     return pl.pallas_call(
         spread_kernel,
-        out_shape=jax.ShapeDtypeStruct((copies, -(-bag // 16) * 8, 2 * per), jnp.int32),
+        out_shape=jax.ShapeDtypeStruct((copies, 1, bag * per), jnp.int32),
         in_specs=[WHOLE],
         out_specs=WHOLE,
         compiler_params=PARAMS,
@@ -52,7 +53,10 @@
     part = 32
 
     def two_blocks(i, _):
-        one, two = ids_ref[2 * i, : bag // 2], ids_ref[2 * i + 1, : bag // 2]
+        one, two = (
+            jnp.concatenate([ids_ref[2 * i + k, :, j * 2 * per : (j + 1) * 2 * per] for j in range(bag // 2)], axis=0)
+            for k in range(2)
+        )
         ids = jnp.concatenate(
             [
                 jnp.concatenate([one[:, :per], two[:, :per]], axis=1),
@@ -98,39 +102,27 @@
     )(places, ids)
 
 
-def pool_kernel(tile, places_ref, counts_ref, own_ref, own_c_ref, far_ref, far_c_ref, out_ref, halves):
+def pool_kernel(places_ref, counts_ref, own_ref, own_c_ref, far_ref, far_c_ref, out_ref, halves):
     rows, width = own_ref.shape
     for place, ref in ((4, own_ref), (5, own_c_ref), (6, far_ref), (7, far_c_ref)):
         high, low = split_halves(ref[...])
-        at = places_ref[place]
-        halves[at, :, :width] = high
-        halves[at, :, width:] = low
-
-    def some_samples(i, _):
-        some = pl.ds(pl.multiple_of(i * tile, tile), tile)
-        total = None
-        for p in range(4):
-            term = lax.dot_general(
-                counts_ref[p * rows : (p + 1) * rows, some],
-                halves[p],
-                (((0,), (0,)), ((), ())),
-                preferred_element_type=jnp.float32,
-            )
-            total = term if total is None else total + term
-        out_ref[some, :] = total[:, :width] + total[:, width:]
-        return 0
-
-    lax.fori_loop(0, counts_ref.shape[1] // tile, some_samples, 0)
-
-
-def pool(places, counts, tables, tile=256):
+        lines = pl.ds(pl.multiple_of(places_ref[place] * rows, rows), rows)
+        halves[lines, :width] = high
+        halves[lines, width:] = low
+    both = lax.dot_general(
+        counts_ref[...], halves[...], (((0,), (0,)), ((), ())), preferred_element_type=jnp.float32
+    )
+    out_ref[...] = both[:, :width] + both[:, width:]
+
+
+def pool(places, counts, tables):
     rows, width = tables[0].shape
     return pl.pallas_call(
-        functools.partial(pool_kernel, tile),
+        pool_kernel,
         out_shape=jax.ShapeDtypeStruct((counts.shape[1], width), jnp.float32),
         in_specs=[SCALARS] + [WHOLE] * 5,
         out_specs=WHOLE,
-        scratch_shapes=[pltpu.VMEM((4, rows, 2 * width), jnp.bfloat16)],
+        scratch_shapes=[pltpu.VMEM((4 * rows, 2 * width), jnp.bfloat16)],
         compiler_params=PARAMS,
         name="pool",
     )(places, counts, *tables)
@@ -237,20 +229,21 @@
 
 def adagrad(rows, sums, grads):
     count, width = rows.shape
-    block = pl.BlockSpec((LANES, width), lambda i: (i, 0))
-    line = pl.BlockSpec((1, 1, LANES), lambda i: (i, 0, 0))
+    lines = 2 * LANES
+    block = pl.BlockSpec((lines, width), lambda i: (i, 0))
+    line = pl.BlockSpec((1, 1, lines), lambda i: (i, 0, 0))
     new_rows, new_sums = pl.pallas_call(
         adagrad_kernel,
         out_shape=(
             jax.ShapeDtypeStruct(rows.shape, jnp.float32),
-            jax.ShapeDtypeStruct((count // LANES, 1, LANES), jnp.float32),
+            jax.ShapeDtypeStruct((count // lines, 1, lines), jnp.float32),
         ),
-        grid=(count // LANES,),
-        in_specs=[block, line, pl.BlockSpec((2, LANES, width // 2), lambda i: (0, i, 0))],
+        grid=(count // lines,),
+        in_specs=[block, line, pl.BlockSpec((2, lines, width // 2), lambda i: (0, i, 0))],
         out_specs=(block, line),
         compiler_params=PARAMS,
         name="adagrad",
-    )(rows, sums.reshape(-1, 1, LANES), grads)
+    )(rows, sums.reshape(-1, 1, lines), grads)
     return new_rows, new_sums.reshape(-1)
 
 
@@ -273,10 +266,9 @@
     places = [(h * (NZ * 2) + z * 2 + d) * rows for h in (0, 1) for d in (c, 1 - c)]
     places = jnp.stack(places + [2 * xh, 2 * xh + 1, 2 - 2 * xh, 3 - 2 * xh, xl]).astype(jnp.int32)
 
-    copies, sent = lax.optimization_barrier((spread(bag_ids.T, NZ), table))
-    ids = lax.all_to_all(copies, "z", 0, 0, tiled=True)
-    far = x_neighbour(sent)
-    own_c = other_core(sent)
+    ids = lax.all_to_all(spread(bag_ids.T, NZ), "z", 0, 0, tiled=True)
+    far = x_neighbour(table)
+    own_c = other_core(table)
     far, ids, places = lax.optimization_barrier((far, ids, places))
     tables = (table, own_c, far, other_core(far))
     mate_ids = xl_mate(ids)

time: 167 us -> 166 us (level)
  no operation moved by 1% of the time
where the time goes in v6:
time: 166 us; the launch traced here: 165 us
  blocking collectives  107 us (64%)
  starting transfers between devices  30.3 us (18%)
  Pallas kernels  16 us (10%)
  waiting for transfers between devices  9.79 us (6%)
    all_to_all x1, blocking collectives, body(): lax.all_to_all(partial.reshape(NZ, per, width), 'z', 0, 0, tiled=True)  35.2 us
    all_gather x1, blocking collectives, body(): gathered = lax.all_gather(halves, 'z', axis=0, tiled=False)  27 us
    all_to_all x1, blocking collectives, body(): lax.all_to_all(mine.reshape(16, rows // 8, width // 2), ('xh', 'y'), 0, 0...  24.3 us
    all_to_all x1, blocking collectives, body(): totals = lax.all_to_all(merge(parts, 16), ('xl', 'y'), 0, 0, tiled=True)  20.8 us
    all_to_all x1, starting transfers between devices, body(): ids = lax.all_to_all(spread(bag_ids.T, NZ), 'z', 0, 0, tiled=True)  15.2 us
    all_to_all x1, waiting for transfers between devices, body(): ids = lax.all_to_all(spread(bag_ids.T, NZ), 'z', 0, 0, tiled=True)  8.99 us
    pallas_call x2, Pallas kernels, count_rows(): pl.pallas_call(functools.partial(count_kernel, bag, per), out_shape=jax.S...  7.65 us
    ppermute x2, starting transfers between devices, xl_mate(): return lax.ppermute(x, 'xl', [(0, 1), (1, 0)])  5.81 us
  transfers between devices with their start and end apart: 7, of which 2 were waited for; matrix products, arithmetic and copies ran while one was open for 0% of the time, Pallas kernels for 7%

profile of v6, /device:TPU:10, one launch (start us, length us, event | category | flops | bytes accessed | tf_op | source)
XLA Modules:
  0.0 165.0 jit_solution(718356774046179806)
XLA Ops:
  0.6 0.0 copy-start
  0.6 3.5 %collective-permute-start = (f32[512,256]{1,0:T(8,128)}, f32[512,256]{1,0:T(8,128)S(1)}, u32[]{:S(2)}, u32[]{:S(2)}) collective-permute-start(f32[512,256]{1,0:T(8,128)} %rows_ref.1), channel_id=1, source_target_pairs={{0,408},{408,0},{24,384},{384,24},{1,409},{409,1},{25,385},{385,25... | collective-permute-start | bytes 1572872 | tf_op jit(solution)/shard_map/ppermute | solution.py:259
  4.2 0.7 copy-done.3
  4.9 0.7 spread.1
  5.6 15.2 %all-to-all-start = ((s32[12,1,1280]{2,1,0:T(1,128)}), s32[12,1,1280]{2,1,0:T(1,128)S(1)}, u32[]{:S(2)}, u32[]{:S(2)}) async-start(s32[12,1,1280]{2,1,0:T(1,128)} %spread.1), calls=%async_computation | async-start | bytes 122880 | tf_op jit(solution)/shard_map/all_to_all | solution.py:269
  20.8 1.9 %collective-permute-start.1 = (f32[512,256]{1,0:T(8,128)}, f32[512,256]{1,0:T(8,128)S(1)}, u32[]{:S(2)}, u32[]{:S(2)}) collective-permute-start(f32[512,256]{1,0:T(8,128)} %rows_ref.1), channel_id=1, source_target_pairs={{0,1},{1,0},{2,3},{3,2},{4,5},{5,4},{6,7},{7,6},{8,9},{9,8},{10,11... | collective-permute-start | bytes 1572872 | tf_op jit(solution)/shard_map/ppermute | solution.py:251
  22.7 0.1 stack.39.base_ref.places_ref
  22.8 9.0 %all-to-all-done.ids_ref = s32[12,1,1280]{2,1,0:T(1,128)S(1)} async-done(((s32[12,1,1280]{2,1,0:T(1,128)}), s32[12,1,1280]{2,1,0:T(1,128)S(1)}, u32[]{:S(2)}, u32[]{:S(2)}) %all-to-all-start) | async-done | bytes 61472 | tf_op jit(solution)/shard_map/all_to_all | solution.py:269
  31.8 0.0 collective-permute-done.far_ref
  31.8 1.9 %collective-permute-start.2 = (f32[512,256]{1,0:T(8,128)S(1)}, f32[512,256]{1,0:T(8,128)S(1)}, u32[]{:S(2)}, u32[]{:S(2)}) collective-permute-start(f32[512,256]{1,0:T(8,128)S(1)} %collective-permute-done.far_ref), channel_id=1, source_target_pairs={{0,1},{1,0},{2,3},{3,2},{4,5},{5,4},{6,7},{7,6},{8,9},{9,8},{10,11... | collective-permute-start | bytes 1572872 | tf_op jit(solution)/shard_map/ppermute | solution.py:251
  33.7 3.7 %collective-permute-start.3 = (s32[12,1,1280]{2,1,0:T(1,128)S(1)}, s32[12,1,1280]{2,1,0:T(1,128)S(1)}, u32[]{:S(2)}, u32[]{:S(2)}) collective-permute-start(s32[12,1,1280]{2,1,0:T(1,128)S(1)} %all-to-all-done.ids_ref), channel_id=1, source_target_pairs={{0,384},{384,0},{1,385},{385,1},{2,386},{386,2},{3,387},{387,3},{4... | collective-permute-start | bytes 184328 | tf_op jit(solution)/shard_map/ppermute | solution.py:255
  37.5 3.8 %count_rows.2.counts_ref.near_ref = bf16[2048,768]{1,0:T(8,128)(2,1)S(1)} custom-call(s32[9]{0:T(128)S(1)} %stack.39.base_ref.places_ref, s32[12,1,1280]{2,1,0:T(1,128)S(1)} %all-to-all-done.ids_ref), custom_call_target="tpu_custom_call" | custom-call | tf_op jit(solution)/shard_map/count_rows/pallas_call | solution.py:95
  41.3 0.0 copy-start.1
  41.3 0.0 copy-start.2
  41.3 0.0 copy-start.5
  41.3 0.0 collective-permute-done.2.far_c_ref
  41.3 2.9 %pool.1 = f32[768,256]{1,0:T(8,128)S(1)} custom-call(s32[9]{0:T(128)S(1)} %stack.39.base_ref.places_ref, bf16[2048,768]{1,0:T(8,128)(2,1)S(1)} %count_rows.2.counts_ref.near_ref, f32[512,256]{1,0:T(8,128)S(1)} %copy-done, f32[512,256]{1,0:T(8,128)S(1)} %collective-permute-done.1.own_c_ref, f32[512,256]{1,0:T(8,128)S(1)} %collective-permute-done.far_ref, ...), custom_call_target="tpu_custom_call" | custom-call | tf_op jit(solution)/shard_map/pool/pallas_call | solution.py:120
  44.2 35.2 %all_to_all.20.parts_ref = f32[12,64,256]{2,1,0:T(8,128)S(1)} all-to-all(f32[12,64,256]{2,1,0:T(8,128)S(1)} %bitcast.19), channel_id=1, replica_groups=mesh['xl'=2,'y'=8,'xh'=2,'z'=12,'c'=2] {'z'}, dimensions={0} | all-to-all | bytes 1572864 | tf_op jit(solution)/shard_map/all_to_all | solution.py:278
  79.5 1.4 cross.1
  80.9 2.1 %collective-permute-start.4 = (f32[64,128]{1,0:T(8,128)S(1)}, f32[64,128]{1,0:T(8,128)S(1)}, u32[]{:S(2)}, u32[]{:S(2)}) collective-permute-start(f32[64,128]{1,0:T(8,128)S(1)} %get-tuple-element.24), channel_id=1, source_target_pairs={{0,384},{384,0},{1,385},{385,1},{2,386},{386,2},{3,387},{387,3},{4... | collective-permute-start | bytes 98312 | tf_op jit(solution)/shard_map/ppermute | solution.py:255
  83.0 3.8 %count_rows.3.far_ref = bf16[2048,768]{1,0:T(8,128)(2,1)S(1)} custom-call(s32[9]{0:T(128)S(1)} %stack.39.base_ref.places_ref, s32[12,1,1280]{2,1,0:T(1,128)S(1)} %collective-permute-done.3.ids_ref), custom_call_target="tpu_custom_call" | custom-call | tf_op jit(solution)/shard_map/count_rows/pallas_call | solution.py:95
  86.9 27.0 %all-gather = f32[1536,128]{1,0:T(8,128)S(1)} all-gather(f32[128,128]{1,0:T(8,128)S(1)} %pad_maximum_fusion), channel_id=2, replica_groups=mesh['xl'=2,'y'=8,'xh'=2,'z'=12,'c'=2] {'z'}, dimensions={0}, use_global_device_ids=true | all-gather | bytes 851968 | tf_op jit(solution)/shard_map/all_gather | solution.py:284
  113.8 1.1 row_sums.3
  114.9 1.9 %collective-permute-start.5 = (f32[2,512,128]{2,1,0:T(8,128)S(1)}, f32[2,512,128]{2,1,0:T(8,128)S(1)}, u32[]{:S(2)}, u32[]{:S(2)}) collective-permute-start(f32[2,512,128]{2,1,0:T(8,128)S(1)} %row_sums.3), channel_id=1, source_target_pairs={{0,1},{1,0},{2,3},{3,2},{4,5},{5,4},{6,7},{7,6},{8,9},{9,8},{10,11... | collective-permute-start | bytes 1572872 | tf_op jit(solution)/shard_map/ppermute | solution.py:251
  116.8 1.1 row_sums.2
  117.9 0.0 copy-start.4
  117.9 0.8 collective-permute-done.5
  118.7 0.1 add.28
  118.8 24.3 %all_to_all.21.parts_ref = f32[16,64,128]{2,1,0:T(8,128)S(1)} all-to-all(f32[16,64,128]{2,1,0:T(8,128)S(1)} %bitcast.24), channel_id=1, replica_groups=mesh['xl'=2,'y'=8,'xh'=2,'z'=12,'c'=2] {'xh','y'}, dimensions={0} | all-to-all | bytes 1048576 | tf_op jit(solution)/shard_map/all_to_all | solution.py:287
  143.1 0.1 merge.1
  143.1 20.8 %all_to_all.22 = f32[16,64,128]{2,1,0:T(8,128)S(1)} all-to-all(f32[16,64,128]{2,1,0:T(8,128)S(1)} %merge.1), channel_id=1, replica_groups=mesh['xl'=2,'y'=8,'xh'=2,'z'=12,'c'=2] {'xl','y'}, dimensions={0} | all-to-all | bytes 1048576 | tf_op jit(solution)/shard_map/all_to_all | solution.py:288
  163.9 1.1 adagrad.1
  (10 shorter events, 0.0 us)
Async XLA Ops:
  0.6 40.7 %copy-start = (f32[512,256]{1,0:T(8,128)S(1)}, f32[512,256]{1,0:T(8,128)}, u32[]{:S(2)}) copy-start(f32[512,256]{1,0:T(8,128)} %rows_ref.1) | copy-start | bytes 1572868
  0.6 31.2 %collective-permute-start = (f32[512,256]{1,0:T(8,128)}, f32[512,256]{1,0:T(8,128)S(1)}, u32[]{:S(2)}, u32[]{:S(2)}) collective-permute-start(f32[512,256]{1,0:T(8,128)} %rows_ref.1), channel_id=1, source_target_pairs={{0,408},{408,0},{24,384},{384,24},{1,409},{409,1},{25,385},{385,25... | collective-permute-start | bytes 1572872 | tf_op jit(solution)/shard_map/ppermute | solution.py:259
  4.2 0.7 copy-start.3
  5.6 26.2 %all-to-all-start = ((s32[12,1,1280]{2,1,0:T(1,128)}), s32[12,1,1280]{2,1,0:T(1,128)S(1)}, u32[]{:S(2)}, u32[]{:S(2)}) async-start(s32[12,1,1280]{2,1,0:T(1,128)} %spread.1), calls=%async_computation | async-start | bytes 122880 | tf_op jit(solution)/shard_map/all_to_all | solution.py:269
  20.8 20.5 %collective-permute-start.1 = (f32[512,256]{1,0:T(8,128)}, f32[512,256]{1,0:T(8,128)S(1)}, u32[]{:S(2)}, u32[]{:S(2)}) collective-permute-start(f32[512,256]{1,0:T(8,128)} %rows_ref.1), channel_id=1, source_target_pairs={{0,1},{1,0},{2,3},{3,2},{4,5},{5,4},{6,7},{7,6},{8,9},{9,8},{10,11... | collective-permute-start | bytes 1572872 | tf_op jit(solution)/shard_map/ppermute | solution.py:251
  31.8 9.5 %collective-permute-start.2 = (f32[512,256]{1,0:T(8,128)S(1)}, f32[512,256]{1,0:T(8,128)S(1)}, u32[]{:S(2)}, u32[]{:S(2)}) collective-permute-start(f32[512,256]{1,0:T(8,128)S(1)} %collective-permute-done.far_ref), channel_id=1, source_target_pairs={{0,1},{1,0},{2,3},{3,2},{4,5},{5,4},{6,7},{7,6},{8,9},{9,8},{10,11... | collective-permute-start | bytes 1572872 | tf_op jit(solution)/shard_map/ppermute | solution.py:251
  33.7 10.5 %collective-permute-start.3 = (s32[12,1,1280]{2,1,0:T(1,128)S(1)}, s32[12,1,1280]{2,1,0:T(1,128)S(1)}, u32[]{:S(2)}, u32[]{:S(2)}) collective-permute-start(s32[12,1,1280]{2,1,0:T(1,128)S(1)} %all-to-all-done.ids_ref), channel_id=1, source_target_pairs={{0,384},{384,0},{1,385},{385,1},{2,386},{386,2},{3,387},{387,3},{4... | collective-permute-start | bytes 184328 | tf_op jit(solution)/shard_map/ppermute | solution.py:255
  41.3 38.2 %copy-start.1 = (f32[256,256]{1,0:T(8,128)S(1)}, f32[256,256]{1,0:T(8,128)}, u32[]{:S(2)}) copy-start(f32[256,256]{1,0:T(8,128)} %weight_ref.1) | copy-start | bytes 786436
  41.3 38.2 %copy-start.2 = (f32[64,256]{1,0:T(8,128)S(1)}, f32[64,256]{1,0:T(8,128)}, u32[]{:S(2)}) copy-start(f32[64,256]{1,0:T(8,128)} %upstream_ref.1) | copy-start | bytes 196612
  41.3 38.2 %copy-start.5 = (f32[256]{0:T(256)S(1)}, f32[256]{0:T(256)}, u32[]{:S(2)}) copy-start(f32[256]{0:T(256)} %param.10) | copy-start | bytes 3076
  80.9 5.9 %collective-permute-start.4 = (f32[64,128]{1,0:T(8,128)S(1)}, f32[64,128]{1,0:T(8,128)S(1)}, u32[]{:S(2)}, u32[]{:S(2)}) collective-permute-start(f32[64,128]{1,0:T(8,128)S(1)} %get-tuple-element.24), channel_id=1, source_target_pairs={{0,384},{384,0},{1,385},{385,1},{2,386},{386,2},{3,387},{387,3},{4... | collective-permute-start | bytes 98312 | tf_op jit(solution)/shard_map/ppermute | solution.py:255
  114.9 3.8 %collective-permute-start.5 = (f32[2,512,128]{2,1,0:T(8,128)S(1)}, f32[2,512,128]{2,1,0:T(8,128)S(1)}, u32[]{:S(2)}, u32[]{:S(2)}) collective-permute-start(f32[2,512,128]{2,1,0:T(8,128)S(1)} %row_sums.3), channel_id=1, source_target_pairs={{0,1},{1,0},{2,3},{3,2},{4,5},{5,4},{6,7},{7,6},{8,9},{9,8},{10,11... | collective-permute-start | bytes 1572872 | tf_op jit(solution)/shard_map/ppermute | solution.py:251
  117.9 46.0 %copy-start.4 = (f32[512]{0:T(512)S(1)}, f32[512]{0:T(512)}, u32[]{:S(2)}) copy-start(f32[512]{0:T(512)} %param.8) | copy-start | bytes 6148

commit v7 on v6

--- a/solution.py
+++ b/solution.py
@@ -12,7 +12,6 @@
 SIZES = (2, 8, 2, 12, 2)
 NZ = 12
 LANES = 128
-FIELDS, BITS = 6, 5
 PARAMS = pltpu.CompilerParams(vmem_limit_bytes=16 * 1024 * 1024)
 SCALARS = pl.BlockSpec(memory_space=pltpu.SMEM)
 WHOLE = pl.BlockSpec(memory_space=pltpu.VMEM)
@@ -45,16 +44,19 @@
     )(ids)
 
 
-def count_kernel(bag, per, base_ref, ids_ref, out_ref):
-    assert bag < 1 << BITS
+def count_kernel(bag, per, mate, places_ref, ids_ref, out_ref):
+    half = bag // 2
+    assert bag == 2 * half and half < 16
     rows = out_ref.shape[0] // 4
     pieces = 4 * rows // LANES
-    words = -(-pieces // FIELDS)
+    words = pieces // 8
     part = 32
+    low = 0x0F0F0F0F
+    line_of = jnp.where(places_ref[8] == mate, 0, ids_ref.shape[0] // 2)
 
     def two_blocks(i, _):
         one, two = (
-            jnp.concatenate([ids_ref[2 * i + k, :, j * 2 * per : (j + 1) * 2 * per] for j in range(bag // 2)], axis=0)
+            jnp.concatenate([ids_ref[line_of + 2 * i + k, :, j * 2 * per : (j + 1) * 2 * per] for j in range(bag // 2)], axis=0)
             for k in range(2)
         )
         ids = jnp.concatenate(
@@ -68,33 +70,39 @@
         line = ids & (LANES - 1)
         piece = jnp.full(ids.shape, -1, jnp.int32)
         for q in range(4):
-            local = ids - base_ref[q]
+            local = ids - places_ref[q]
             piece = jnp.where((local >= 0) & (local < rows), (q * rows + local) >> 7, piece)
         values = []
         for t in range(words):
-            field = piece - t * FIELDS
-            inside = (field >= 0) & (field < FIELDS) & (piece >= 0)
-            values.append(jnp.where(inside, jnp.int32(1) << jnp.where(inside, field, 0) * BITS, 0))
+            inside = (piece >= 8 * t) & (piece < 8 * (t + 1))
+            values.append(jnp.where(inside, jnp.int32(1) << (piece & 7) * 4, 0))
         for first in range(0, LANES, part):
             lines = lax.broadcasted_iota(jnp.int32, (part, LANES), 0) + first
-            sums = [jnp.zeros((part, LANES), jnp.int32) for _ in range(words)]
+            sums = [[jnp.zeros((part, LANES), jnp.int32) for _ in range(words)] for _ in range(2)]
             for j in range(bag):
                 hit = line[j : j + 1] == lines
+                some = sums[j // half]
                 for t in range(words):
-                    sums[t] = sums[t] + jnp.where(hit, values[t][j : j + 1], 0)
-            for p in range(pieces):
-                count = (sums[p // FIELDS] >> (BITS * (p % FIELDS))) & ((1 << BITS) - 1)
-                at = p * LANES + first
-                out_ref[at : at + part, columns] = count.astype(jnp.float32).astype(jnp.bfloat16)
+                    some[t] = some[t] + jnp.where(hit, values[t][j : j + 1], 0)
+            for t in range(words):
+                one, two = sums[0][t], sums[1][t]
+                even = (one & low) + (two & low)
+                odd = ((one >> 4) & low) + ((two >> 4) & low)
+                for f in range(8):
+                    count = (even, odd)[f % 2] >> (f // 2 * 8)
+                    if f < 6:
+                        count = count & 255
+                    at = (8 * t + f) * LANES + first
+                    out_ref[at : at + part, columns] = count.astype(jnp.float32).astype(jnp.bfloat16)
         return 0
 
-    lax.fori_loop(0, ids_ref.shape[0] // 2, two_blocks, 0)
-
-
-def count_rows(places, ids, bag, per, rows):
-    return pl.pallas_call(
-        functools.partial(count_kernel, bag, per),
-        out_shape=jax.ShapeDtypeStruct((4 * rows, ids.shape[0] * per), jnp.bfloat16),
+    lax.fori_loop(0, ids_ref.shape[0] // 4, two_blocks, 0)
+
+
+def count_rows(places, ids, bag, per, rows, mate):
+    return pl.pallas_call(
+        functools.partial(count_kernel, bag, per, mate),
+        out_shape=jax.ShapeDtypeStruct((4 * rows, ids.shape[0] // 2 * per), jnp.bfloat16),
         in_specs=[SCALARS, WHOLE],
         out_specs=WHOLE,
         compiler_params=PARAMS,
@@ -266,19 +274,17 @@
     places = [(h * (NZ * 2) + z * 2 + d) * rows for h in (0, 1) for d in (c, 1 - c)]
     places = jnp.stack(places + [2 * xh, 2 * xh + 1, 2 - 2 * xh, 3 - 2 * xh, xl]).astype(jnp.int32)
 
-    ids = lax.all_to_all(spread(bag_ids.T, NZ), "z", 0, 0, tiled=True)
+    ids = lax.all_to_all(spread(bag_ids.T, 2 * NZ), ("xl", "z"), 0, 0, tiled=True)
     far = x_neighbour(table)
     own_c = other_core(table)
     far, ids, places = lax.optimization_barrier((far, ids, places))
     tables = (table, own_c, far, other_core(far))
-    mate_ids = xl_mate(ids)
-    counts = count_rows(places, ids, bag, per, rows)
+    counts = count_rows(places, ids, bag, per, rows, 0)
     partial = pool(places, counts, tables)
-    partial, mate_ids = lax.optimization_barrier((partial, mate_ids))
     parts = lax.all_to_all(partial.reshape(NZ, per, width), "z", 0, 0, tiled=True)
     crossed, keep, give = cross(places, parts, cross_weight, cross_bias, upstream)
-    mate_ids, give = lax.optimization_barrier((mate_ids, give))
-    mate_counts = count_rows(places, mate_ids, bag, per, rows)
+    ids, give = lax.optimization_barrier((ids, give))
+    mate_counts = count_rows(places, ids, bag, per, rows, 1)
 
     halves = jnp.concatenate([keep, xl_mate(give)], axis=0)
     gathered = lax.all_gather(halves, "z", axis=0, tiled=False)

time: 166 us -> 164 us (0.988)
    ppermute x2 -> x1, starting transfers between devices: 5.81 us -> 3.43 us  [xl_mate(): return lax.ppermute(x, 'xl', [(0, 1), (1, 0)])]
    all_to_all x1, starting transfers between devices: 15.2 us -> 17 us  [body(): lax.all_to_all(spread(bag_ids.T, 2 * NZ), ('xl', 'z'), 0, 0, tiled=True)]
  transfers between devices with their start and end apart: 7 -> 6, of which waited for: 2 -> 2; matrix products, arithmetic and copies ran while one was open for 0% -> 0% of each run, Pallas kernels for 7% -> 5%
where the time goes in v7:
time: 164 us
  blocking collectives  107 us (65%)
  starting transfers between devices  29.7 us (18%)
  Pallas kernels  15.1 us (9%)
  waiting for transfers between devices  9.55 us (6%)
    all_to_all x1, blocking collectives, body(): lax.all_to_all(partial.reshape(NZ, per, width), 'z', 0, 0, tiled=True)  35.9 us
    all_gather x1, blocking collectives, body(): gathered = lax.all_gather(halves, 'z', axis=0, tiled=False)  26.8 us
    all_to_all x1, blocking collectives, body(): lax.all_to_all(mine.reshape(16, rows // 8, width // 2), ('xh', 'y'), 0, 0...  24 us
    all_to_all x1, blocking collectives, body(): totals = lax.all_to_all(merge(parts, 16), ('xl', 'y'), 0, 0, tiled=True)  20.7 us
    all_to_all x1, starting transfers between devices, body(): lax.all_to_all(spread(bag_ids.T, 2 * NZ), ('xl', 'z'), 0, 0, tiled=True)  17 us
    all_to_all x1, waiting for transfers between devices, body(): lax.all_to_all(spread(bag_ids.T, 2 * NZ), ('xl', 'z'), 0, 0, tiled=True)  8.76 us
    pallas_call x2, Pallas kernels, count_rows(): pl.pallas_call(functools.partial(count_kernel, bag, per, mate), out_shape...  6.72 us
    ppermute x3, starting transfers between devices, other_core(): return lax.ppermute(x, 'c', [(0, 1), (1, 0)])  5.75 us
  transfers between devices with their start and end apart: 6, of which 2 were waited for; matrix products, arithmetic and copies ran while one was open for 0% of the time, Pallas kernels for 5%

profile of v7, /device:TPU:10, one launch (start us, length us, event | category | flops | bytes accessed | tf_op | source)
XLA Modules:
  0.0 163.6 jit_solution(4116949687800543956)
XLA Ops:
  0.6 0.0 copy-start
  0.6 3.5 %collective-permute-start = (f32[512,256]{1,0:T(8,128)}, f32[512,256]{1,0:T(8,128)S(1)}, u32[]{:S(2)}, u32[]{:S(2)}) collective-permute-start(f32[512,256]{1,0:T(8,128)} %rows_ref.1), channel_id=1, source_target_pairs={{0,408},{408,0},{24,384},{384,24},{1,409},{409,1},{25,385},{385,25... | collective-permute-start | bytes 1572872 | tf_op jit(solution)/shard_map/ppermute | solution.py:267
  4.2 0.7 copy-done.3
  4.9 0.8 spread.1
  5.7 17.0 %all-to-all-start = ((s32[24,1,1280]{2,1,0:T(1,128)}), s32[24,1,1280]{2,1,0:T(1,128)S(1)}, u32[]{:S(2)}, u32[]{:S(2)}) async-start(s32[24,1,1280]{2,1,0:T(1,128)} %spread.1), calls=%async_computation | async-start | bytes 245760 | tf_op jit(solution)/shard_map/all_to_all | solution.py:277
  22.7 1.9 %collective-permute-start.1 = (f32[512,256]{1,0:T(8,128)}, f32[512,256]{1,0:T(8,128)S(1)}, u32[]{:S(2)}, u32[]{:S(2)}) collective-permute-start(f32[512,256]{1,0:T(8,128)} %rows_ref.1), channel_id=1, source_target_pairs={{0,1},{1,0},{2,3},{3,2},{4,5},{5,4},{6,7},{7,6},{8,9},{9,8},{10,11... | collective-permute-start | bytes 1572872 | tf_op jit(solution)/shard_map/ppermute | solution.py:259
  24.6 0.1 stack.39.places_ref
  24.7 8.8 %all-to-all-done.ids_ref = s32[24,1,1280]{2,1,0:T(1,128)S(1)} async-done(((s32[24,1,1280]{2,1,0:T(1,128)}), s32[24,1,1280]{2,1,0:T(1,128)S(1)}, u32[]{:S(2)}, u32[]{:S(2)}) %all-to-all-start) | async-done | bytes 122912 | tf_op jit(solution)/shard_map/all_to_all | solution.py:277
  33.5 0.0 collective-permute-done.far_ref
  33.5 1.9 %collective-permute-start.2 = (f32[512,256]{1,0:T(8,128)S(1)}, f32[512,256]{1,0:T(8,128)S(1)}, u32[]{:S(2)}, u32[]{:S(2)}) collective-permute-start(f32[512,256]{1,0:T(8,128)S(1)} %collective-permute-done.far_ref), channel_id=1, source_target_pairs={{0,1},{1,0},{2,3},{3,2},{4,5},{5,4},{6,7},{7,6},{8,9},{9,8},{10,11... | collective-permute-start | bytes 1572872 | tf_op jit(solution)/shard_map/ppermute | solution.py:259
  35.4 3.4 %count_rows.2.counts_ref.near_ref = bf16[2048,768]{1,0:T(8,128)(2,1)S(1)} custom-call(s32[9]{0:T(128)S(1)} %stack.39.places_ref, s32[24,1,1280]{2,1,0:T(1,128)S(1)} %all-to-all-done.ids_ref), custom_call_target="tpu_custom_call" | custom-call | tf_op jit(solution)/shard_map/count_rows/pallas_call | solution.py:103
  38.8 0.0 copy-start.1
  38.8 0.0 copy-start.2
  38.8 0.0 copy-start.5
  38.8 0.0 collective-permute-done.1.own_c_ref
  38.8 0.0 collective-permute-done.2.far_c_ref
  38.8 2.9 %pool.1 = f32[768,256]{1,0:T(8,128)S(1)} custom-call(s32[9]{0:T(128)S(1)} %stack.39.places_ref, bf16[2048,768]{1,0:T(8,128)(2,1)S(1)} %count_rows.2.counts_ref.near_ref, f32[512,256]{1,0:T(8,128)S(1)} %copy-done, f32[512,256]{1,0:T(8,128)S(1)} %collective-permute-done.1.own_c_ref, f32[512,256]{1,0:T(8,128)S(1)} %collective-permute-done.far_ref, ...), custom_call_target="tpu_custom_call" | custom-call | tf_op jit(solution)/shard_map/pool/pallas_call | solution.py:128
  41.7 35.9 %all_to_all.20.parts_ref = f32[12,64,256]{2,1,0:T(8,128)S(1)} all-to-all(f32[12,64,256]{2,1,0:T(8,128)S(1)} %bitcast.19), channel_id=1, replica_groups=mesh['xl'=2,'y'=8,'xh'=2,'z'=12,'c'=2] {'z'}, dimensions={0} | all-to-all | bytes 1572864 | tf_op jit(solution)/shard_map/all_to_all | solution.py:284
  77.6 1.4 cross.1
  79.0 3.4 %collective-permute-start.3 = (f32[64,128]{1,0:T(8,128)S(1)}, f32[64,128]{1,0:T(8,128)S(1)}, u32[]{:S(2)}, u32[]{:S(2)}) collective-permute-start(f32[64,128]{1,0:T(8,128)S(1)} %get-tuple-element.20), channel_id=1, source_target_pairs={{0,384},{384,0},{1,385},{385,1},{2,386},{386,2},{3,387},{387,3},{4... | collective-permute-start | bytes 98312 | tf_op jit(solution)/shard_map/ppermute | solution.py:263
  82.4 3.4 %count_rows.3.far_ref = bf16[2048,768]{1,0:T(8,128)(2,1)S(1)} custom-call(s32[9]{0:T(128)S(1)} %stack.39.places_ref, s32[24,1,1280]{2,1,0:T(1,128)S(1)} %all-to-all-done.ids_ref), custom_call_target="tpu_custom_call" | custom-call | tf_op jit(solution)/shard_map/count_rows/pallas_call | solution.py:103
  85.8 26.8 %all-gather = f32[1536,128]{1,0:T(8,128)S(1)} all-gather(f32[128,128]{1,0:T(8,128)S(1)} %pad_maximum_fusion), channel_id=2, replica_groups=mesh['xl'=2,'y'=8,'xh'=2,'z'=12,'c'=2] {'z'}, dimensions={0}, use_global_device_ids=true | all-gather | bytes 851968 | tf_op jit(solution)/shard_map/all_gather | solution.py:290
  112.7 1.1 row_sums.3
  113.7 1.9 %collective-permute-start.4 = (f32[2,512,128]{2,1,0:T(8,128)S(1)}, f32[2,512,128]{2,1,0:T(8,128)S(1)}, u32[]{:S(2)}, u32[]{:S(2)}) collective-permute-start(f32[2,512,128]{2,1,0:T(8,128)S(1)} %row_sums.3), channel_id=1, source_target_pairs={{0,1},{1,0},{2,3},{3,2},{4,5},{5,4},{6,7},{7,6},{8,9},{9,8},{10,11... | collective-permute-start | bytes 1572872 | tf_op jit(solution)/shard_map/ppermute | solution.py:259
  115.7 1.1 row_sums.2
  116.7 0.0 copy-start.4
  116.8 0.8 collective-permute-done.4
  117.5 0.1 add.28
  117.6 24.0 %all_to_all.21.parts_ref = f32[16,64,128]{2,1,0:T(8,128)S(1)} all-to-all(f32[16,64,128]{2,1,0:T(8,128)S(1)} %bitcast.24), channel_id=1, replica_groups=mesh['xl'=2,'y'=8,'xh'=2,'z'=12,'c'=2] {'xh','y'}, dimensions={0} | all-to-all | bytes 1048576 | tf_op jit(solution)/shard_map/all_to_all | solution.py:293
  141.6 0.1 merge.1
  141.7 20.7 %all_to_all.22 = f32[16,64,128]{2,1,0:T(8,128)S(1)} all-to-all(f32[16,64,128]{2,1,0:T(8,128)S(1)} %merge.1), channel_id=1, replica_groups=mesh['xl'=2,'y'=8,'xh'=2,'z'=12,'c'=2] {'xl','y'}, dimensions={0} | all-to-all | bytes 1048576 | tf_op jit(solution)/shard_map/all_to_all | solution.py:294
  162.5 1.1 adagrad.1
  (8 shorter events, 0.0 us)
Async XLA Ops:
  0.6 38.2 %copy-start = (f32[512,256]{1,0:T(8,128)S(1)}, f32[512,256]{1,0:T(8,128)}, u32[]{:S(2)}) copy-start(f32[512,256]{1,0:T(8,128)} %rows_ref.1) | copy-start | bytes 1572868
  0.6 32.8 %collective-permute-start = (f32[512,256]{1,0:T(8,128)}, f32[512,256]{1,0:T(8,128)S(1)}, u32[]{:S(2)}, u32[]{:S(2)}) collective-permute-start(f32[512,256]{1,0:T(8,128)} %rows_ref.1), channel_id=1, source_target_pairs={{0,408},{408,0},{24,384},{384,24},{1,409},{409,1},{25,385},{385,25... | collective-permute-start | bytes 1572872 | tf_op jit(solution)/shard_map/ppermute | solution.py:267
  4.2 0.7 copy-start.3
  5.7 27.8 %all-to-all-start = ((s32[24,1,1280]{2,1,0:T(1,128)}), s32[24,1,1280]{2,1,0:T(1,128)S(1)}, u32[]{:S(2)}, u32[]{:S(2)}) async-start(s32[24,1,1280]{2,1,0:T(1,128)} %spread.1), calls=%async_computation | async-start | bytes 245760 | tf_op jit(solution)/shard_map/all_to_all | solution.py:277
  22.7 16.1 %collective-permute-start.1 = (f32[512,256]{1,0:T(8,128)}, f32[512,256]{1,0:T(8,128)S(1)}, u32[]{:S(2)}, u32[]{:S(2)}) collective-permute-start(f32[512,256]{1,0:T(8,128)} %rows_ref.1), channel_id=1, source_target_pairs={{0,1},{1,0},{2,3},{3,2},{4,5},{5,4},{6,7},{7,6},{8,9},{9,8},{10,11... | collective-permute-start | bytes 1572872 | tf_op jit(solution)/shard_map/ppermute | solution.py:259
  33.5 5.3 %collective-permute-start.2 = (f32[512,256]{1,0:T(8,128)S(1)}, f32[512,256]{1,0:T(8,128)S(1)}, u32[]{:S(2)}, u32[]{:S(2)}) collective-permute-start(f32[512,256]{1,0:T(8,128)S(1)} %collective-permute-done.far_ref), channel_id=1, source_target_pairs={{0,1},{1,0},{2,3},{3,2},{4,5},{5,4},{6,7},{7,6},{8,9},{9,8},{10,11... | collective-permute-start | bytes 1572872 | tf_op jit(solution)/shard_map/ppermute | solution.py:259
  38.8 38.8 %copy-start.1 = (f32[256,256]{1,0:T(8,128)S(1)}, f32[256,256]{1,0:T(8,128)}, u32[]{:S(2)}) copy-start(f32[256,256]{1,0:T(8,128)} %weight_ref.1) | copy-start | bytes 786436
  38.8 38.8 %copy-start.2 = (f32[64,256]{1,0:T(8,128)S(1)}, f32[64,256]{1,0:T(8,128)}, u32[]{:S(2)}) copy-start(f32[64,256]{1,0:T(8,128)} %upstream_ref.1) | copy-start | bytes 196612
  38.8 38.8 %copy-start.5 = (f32[256]{0:T(256)S(1)}, f32[256]{0:T(256)}, u32[]{:S(2)}) copy-start(f32[256]{0:T(256)} %param.10) | copy-start | bytes 3076
  79.0 6.8 %collective-permute-start.3 = (f32[64,128]{1,0:T(8,128)S(1)}, f32[64,128]{1,0:T(8,128)S(1)}, u32[]{:S(2)}, u32[]{:S(2)}) collective-permute-start(f32[64,128]{1,0:T(8,128)S(1)} %get-tuple-element.20), channel_id=1, source_target_pairs={{0,384},{384,0},{1,385},{385,1},{2,386},{386,2},{3,387},{387,3},{4... | collective-permute-start | bytes 98312 | tf_op jit(solution)/shard_map/ppermute | solution.py:263
  113.7 3.8 %collective-permute-start.4 = (f32[2,512,128]{2,1,0:T(8,128)S(1)}, f32[2,512,128]{2,1,0:T(8,128)S(1)}, u32[]{:S(2)}, u32[]{:S(2)}) collective-permute-start(f32[2,512,128]{2,1,0:T(8,128)S(1)} %row_sums.3), channel_id=1, source_target_pairs={{0,1},{1,0},{2,3},{3,2},{4,5},{5,4},{6,7},{7,6},{8,9},{9,8},{10,11... | collective-permute-start | bytes 1572872 | tf_op jit(solution)/shard_map/ppermute | solution.py:259
  116.7 45.7 %copy-start.4 = (f32[512]{0:T(512)S(1)}, f32[512]{0:T(512)}, u32[]{:S(2)}) copy-start(f32[512]{0:T(512)} %param.8) | copy-start | bytes 6148

commit v8 on v7

--- a/solution.py
+++ b/solution.py
@@ -106,6 +106,7 @@
         in_specs=[SCALARS, WHOLE],
         out_specs=WHOLE,
         compiler_params=PARAMS,
+        cost_estimate=pl.CostEstimate(flops=2000000000, bytes_accessed=0, transcendentals=0),
         name="count_rows",
     )(places, ids)
 
@@ -277,7 +278,7 @@
     ids = lax.all_to_all(spread(bag_ids.T, 2 * NZ), ("xl", "z"), 0, 0, tiled=True)
     far = x_neighbour(table)
     own_c = other_core(table)
-    far, ids, places = lax.optimization_barrier((far, ids, places))
+    ids, places = lax.optimization_barrier((ids, places))
     tables = (table, own_c, far, other_core(far))
     counts = count_rows(places, ids, bag, per, rows, 0)
     partial = pool(places, counts, tables)

time: 164 us -> 161 us (0.982)
  waiting for transfers between devices: 9.55 us -> 7.12 us
    all_to_all x1, waiting for transfers between devices: 8.76 us -> 6.33 us  [body(): lax.all_to_all(spread(bag_ids.T, 2 * NZ), ('xl', 'z'), 0, 0, tiled=True)]
where the time goes in v8:
time: 161 us
  blocking collectives  107 us (66%)
  starting transfers between devices  29.3 us (18%)
  Pallas kernels  15.1 us (9%)
  waiting for transfers between devices  7.12 us (4%)
    all_to_all x1, blocking collectives, body(): lax.all_to_all(partial.reshape(NZ, per, width), 'z', 0, 0, tiled=True)  35.2 us
    all_gather x1, blocking collectives, body(): gathered = lax.all_gather(halves, 'z', axis=0, tiled=False)  26.2 us
    all_to_all x1, blocking collectives, body(): lax.all_to_all(mine.reshape(16, rows // 8, width // 2), ('xh', 'y'), 0, 0...  24.6 us
    all_to_all x1, blocking collectives, body(): totals = lax.all_to_all(merge(parts, 16), ('xl', 'y'), 0, 0, tiled=True)  21.3 us
    all_to_all x1, starting transfers between devices, body(): lax.all_to_all(spread(bag_ids.T, 2 * NZ), ('xl', 'z'), 0, 0, tiled=True)  17 us
    pallas_call x2, Pallas kernels, count_rows(): pl.pallas_call(functools.partial(count_kernel, bag, per, mate), out_shape...  6.72 us
    all_to_all x1, waiting for transfers between devices, body(): lax.all_to_all(spread(bag_ids.T, 2 * NZ), ('xl', 'z'), 0, 0, tiled=True)  6.33 us
    ppermute x3, starting transfers between devices, other_core(): return lax.ppermute(x, 'c', [(0, 1), (1, 0)])  6.25 us
  transfers between devices with their start and end apart: 6, of which 2 were waited for; matrix products, arithmetic and copies ran while one was open for 0% of the time, Pallas kernels for 5%

profile of v8, /device:TPU:10, one launch (start us, length us, event | category | flops | bytes accessed | tf_op | source)
XLA Modules:
  0.0 160.6 jit_solution(13317367947498861738)
XLA Ops:
  0.6 3.4 %collective-permute-start.1 = (f32[512,256]{1,0:T(8,128)}, f32[512,256]{1,0:T(8,128)S(1)}, u32[]{:S(2)}, u32[]{:S(2)}) collective-permute-start(f32[512,256]{1,0:T(8,128)} %rows_ref.1), channel_id=1, source_target_pairs={{0,408},{408,0},{24,384},{384,24},{1,409},{409,1},{25,385},{385,25... | collective-permute-start | bytes 1572872 | tf_op jit(solution)/shard_map/ppermute | solution.py:268
  4.0 0.7 copy-done.3
  4.7 0.8 spread.1
  5.5 17.0 %all-to-all-start = ((s32[24,1,1280]{2,1,0:T(1,128)}), s32[24,1,1280]{2,1,0:T(1,128)S(1)}, u32[]{:S(2)}, u32[]{:S(2)}) async-start(s32[24,1,1280]{2,1,0:T(1,128)} %spread.1), calls=%async_computation | async-start | bytes 245760 | tf_op jit(solution)/shard_map/all_to_all | solution.py:278
  22.5 1.9 %collective-permute-start = (f32[512,256]{1,0:T(8,128)}, f32[512,256]{1,0:T(8,128)S(1)}, u32[]{:S(2)}, u32[]{:S(2)}) collective-permute-start(f32[512,256]{1,0:T(8,128)} %rows_ref.1), channel_id=1, source_target_pairs={{0,1},{1,0},{2,3},{3,2},{4,5},{5,4},{6,7},{7,6},{8,9},{9,8},{10,11... | collective-permute-start | bytes 1572872 | tf_op jit(solution)/shard_map/ppermute | solution.py:260
  24.5 0.0 collective-permute-done.1.far_ref
  24.5 2.4 %collective-permute-start.2 = (f32[512,256]{1,0:T(8,128)S(1)}, f32[512,256]{1,0:T(8,128)S(1)}, u32[]{:S(2)}, u32[]{:S(2)}) collective-permute-start(f32[512,256]{1,0:T(8,128)S(1)} %collective-permute-done.1.far_ref), channel_id=1, source_target_pairs={{0,1},{1,0},{2,3},{3,2},{4,5},{5,4},{6,7},{7,6},{8,9},{9,8},{10,11... | collective-permute-start | bytes 1572872 | tf_op jit(solution)/shard_map/ppermute | solution.py:260
  26.9 0.1 stack.39.places_ref
  27.0 6.3 %all-to-all-done.ids_ref = s32[24,1,1280]{2,1,0:T(1,128)S(1)} async-done(((s32[24,1,1280]{2,1,0:T(1,128)}), s32[24,1,1280]{2,1,0:T(1,128)S(1)}, u32[]{:S(2)}, u32[]{:S(2)}) %all-to-all-start) | async-done | bytes 122912 | tf_op jit(solution)/shard_map/all_to_all | solution.py:278
  33.3 3.4 %count_rows.2.counts_ref.near_ref = bf16[2048,768]{1,0:T(8,128)(2,1)S(1)} custom-call(s32[9]{0:T(128)S(1)} %stack.39.places_ref, s32[24,1,1280]{2,1,0:T(1,128)S(1)} %all-to-all-done.ids_ref), custom_call_target="tpu_custom_call" | custom-call | flops 2000000000 | tf_op jit(solution)/shard_map/count_rows/pallas_call | solution.py:103
  36.7 0.0 copy-start.1
  36.7 0.0 copy-start.2
  36.7 0.0 copy-start.5
  36.7 0.0 collective-permute-done.own_c_ref
  36.7 0.0 collective-permute-done.2.far_c_ref
  36.8 2.9 %pool.1 = f32[768,256]{1,0:T(8,128)S(1)} custom-call(s32[9]{0:T(128)S(1)} %stack.39.places_ref, bf16[2048,768]{1,0:T(8,128)(2,1)S(1)} %count_rows.2.counts_ref.near_ref, f32[512,256]{1,0:T(8,128)S(1)} %copy-done, f32[512,256]{1,0:T(8,128)S(1)} %collective-permute-done.own_c_ref, f32[512,256]{1,0:T(8,128)S(1)} %collective-permute-done.1.far_ref, ...), custom_call_target="tpu_custom_call" | custom-call | tf_op jit(solution)/shard_map/pool/pallas_call | solution.py:129
  39.6 35.2 %all_to_all.20.parts_ref = f32[12,64,256]{2,1,0:T(8,128)S(1)} all-to-all(f32[12,64,256]{2,1,0:T(8,128)S(1)} %bitcast.19), channel_id=1, replica_groups=mesh['xl'=2,'y'=8,'xh'=2,'z'=12,'c'=2] {'z'}, dimensions={0} | all-to-all | bytes 1572864 | tf_op jit(solution)/shard_map/all_to_all | solution.py:285
  74.8 1.4 cross.1
  76.2 2.7 %collective-permute-start.3 = (f32[64,128]{1,0:T(8,128)S(1)}, f32[64,128]{1,0:T(8,128)S(1)}, u32[]{:S(2)}, u32[]{:S(2)}) collective-permute-start(f32[64,128]{1,0:T(8,128)S(1)} %get-tuple-element.18), channel_id=1, source_target_pairs={{0,384},{384,0},{1,385},{385,1},{2,386},{386,2},{3,387},{387,3},{4... | collective-permute-start | bytes 98312 | tf_op jit(solution)/shard_map/ppermute | solution.py:264
  78.9 3.4 %count_rows.3.far_ref = bf16[2048,768]{1,0:T(8,128)(2,1)S(1)} custom-call(s32[9]{0:T(128)S(1)} %stack.39.places_ref, s32[24,1,1280]{2,1,0:T(1,128)S(1)} %all-to-all-done.ids_ref), custom_call_target="tpu_custom_call" | custom-call | flops 2000000000 | tf_op jit(solution)/shard_map/count_rows/pallas_call | solution.py:103
  82.3 0.0 collective-permute-done.3
  82.3 26.2 %all-gather = f32[1536,128]{1,0:T(8,128)S(1)} all-gather(f32[128,128]{1,0:T(8,128)S(1)} %pad_maximum_fusion), channel_id=2, replica_groups=mesh['xl'=2,'y'=8,'xh'=2,'z'=12,'c'=2] {'z'}, dimensions={0}, use_global_device_ids=true | all-gather | bytes 851968 | tf_op jit(solution)/shard_map/all_gather | solution.py:291
  108.5 1.1 row_sums.3
  109.6 1.9 %collective-permute-start.4 = (f32[2,512,128]{2,1,0:T(8,128)S(1)}, f32[2,512,128]{2,1,0:T(8,128)S(1)}, u32[]{:S(2)}, u32[]{:S(2)}) collective-permute-start(f32[2,512,128]{2,1,0:T(8,128)S(1)} %row_sums.3), channel_id=1, source_target_pairs={{0,1},{1,0},{2,3},{3,2},{4,5},{5,4},{6,7},{7,6},{8,9},{9,8},{10,11... | collective-permute-start | bytes 1572872 | tf_op jit(solution)/shard_map/ppermute | solution.py:260
  111.5 1.1 row_sums.2
  112.6 0.0 copy-start.4
  112.6 0.8 collective-permute-done.4
  113.4 0.1 add.28
  113.5 24.6 %all_to_all.21.parts_ref = f32[16,64,128]{2,1,0:T(8,128)S(1)} all-to-all(f32[16,64,128]{2,1,0:T(8,128)S(1)} %bitcast.24), channel_id=1, replica_groups=mesh['xl'=2,'y'=8,'xh'=2,'z'=12,'c'=2] {'xh','y'}, dimensions={0} | all-to-all | bytes 1048576 | tf_op jit(solution)/shard_map/all_to_all | solution.py:294
  138.1 0.1 merge.1
  138.2 21.3 %all_to_all.22 = f32[16,64,128]{2,1,0:T(8,128)S(1)} all-to-all(f32[16,64,128]{2,1,0:T(8,128)S(1)} %merge.1), channel_id=1, replica_groups=mesh['xl'=2,'y'=8,'xh'=2,'z'=12,'c'=2] {'xl','y'}, dimensions={0} | all-to-all | bytes 1048576 | tf_op jit(solution)/shard_map/all_to_all | solution.py:295
  159.4 1.1 adagrad.1
  (8 shorter events, 0.0 us)
Async XLA Ops:
  0.6 23.8 %collective-permute-start.1 = (f32[512,256]{1,0:T(8,128)}, f32[512,256]{1,0:T(8,128)S(1)}, u32[]{:S(2)}, u32[]{:S(2)}) collective-permute-start(f32[512,256]{1,0:T(8,128)} %rows_ref.1), channel_id=1, source_target_pairs={{0,408},{408,0},{24,384},{384,24},{1,409},{409,1},{25,385},{385,25... | collective-permute-start | bytes 1572872 | tf_op jit(solution)/shard_map/ppermute | solution.py:268
  4.0 0.7 copy-start.3
  5.5 27.8 %all-to-all-start = ((s32[24,1,1280]{2,1,0:T(1,128)}), s32[24,1,1280]{2,1,0:T(1,128)S(1)}, u32[]{:S(2)}, u32[]{:S(2)}) async-start(s32[24,1,1280]{2,1,0:T(1,128)} %spread.1), calls=%async_computation | async-start | bytes 245760 | tf_op jit(solution)/shard_map/all_to_all | solution.py:278
  22.5 14.2 %collective-permute-start = (f32[512,256]{1,0:T(8,128)}, f32[512,256]{1,0:T(8,128)S(1)}, u32[]{:S(2)}, u32[]{:S(2)}) collective-permute-start(f32[512,256]{1,0:T(8,128)} %rows_ref.1), channel_id=1, source_target_pairs={{0,1},{1,0},{2,3},{3,2},{4,5},{5,4},{6,7},{7,6},{8,9},{9,8},{10,11... | collective-permute-start | bytes 1572872 | tf_op jit(solution)/shard_map/ppermute | solution.py:260
  24.5 12.3 %collective-permute-start.2 = (f32[512,256]{1,0:T(8,128)S(1)}, f32[512,256]{1,0:T(8,128)S(1)}, u32[]{:S(2)}, u32[]{:S(2)}) collective-permute-start(f32[512,256]{1,0:T(8,128)S(1)} %collective-permute-done.1.far_ref), channel_id=1, source_target_pairs={{0,1},{1,0},{2,3},{3,2},{4,5},{5,4},{6,7},{7,6},{8,9},{9,8},{10,11... | collective-permute-start | bytes 1572872 | tf_op jit(solution)/shard_map/ppermute | solution.py:260
  27.0 9.8 %copy-start = (f32[512,256]{1,0:T(8,128)S(1)}, f32[512,256]{1,0:T(8,128)}, u32[]{:S(2)}) copy-start(f32[512,256]{1,0:T(8,128)} %rows_ref.1) | copy-start | bytes 1572868
  36.7 38.1 %copy-start.1 = (f32[256,256]{1,0:T(8,128)S(1)}, f32[256,256]{1,0:T(8,128)}, u32[]{:S(2)}) copy-start(f32[256,256]{1,0:T(8,128)} %weight_ref.1) | copy-start | bytes 786436
  36.7 38.1 %copy-start.2 = (f32[64,256]{1,0:T(8,128)S(1)}, f32[64,256]{1,0:T(8,128)}, u32[]{:S(2)}) copy-start(f32[64,256]{1,0:T(8,128)} %upstream_ref.1) | copy-start | bytes 196612
  36.7 38.1 %copy-start.5 = (f32[256]{0:T(256)S(1)}, f32[256]{0:T(256)}, u32[]{:S(2)}) copy-start(f32[256]{0:T(256)} %param.10) | copy-start | bytes 3076
  76.2 6.0 %collective-permute-start.3 = (f32[64,128]{1,0:T(8,128)S(1)}, f32[64,128]{1,0:T(8,128)S(1)}, u32[]{:S(2)}, u32[]{:S(2)}) collective-permute-start(f32[64,128]{1,0:T(8,128)S(1)} %get-tuple-element.18), channel_id=1, source_target_pairs={{0,384},{384,0},{1,385},{385,1},{2,386},{386,2},{3,387},{387,3},{4... | collective-permute-start | bytes 98312 | tf_op jit(solution)/shard_map/ppermute | solution.py:264
  109.6 3.8 %collective-permute-start.4 = (f32[2,512,128]{2,1,0:T(8,128)S(1)}, f32[2,512,128]{2,1,0:T(8,128)S(1)}, u32[]{:S(2)}, u32[]{:S(2)}) collective-permute-start(f32[2,512,128]{2,1,0:T(8,128)S(1)} %row_sums.3), channel_id=1, source_target_pairs={{0,1},{1,0},{2,3},{3,2},{4,5},{5,4},{6,7},{7,6},{8,9},{9,8},{10,11... | collective-permute-start | bytes 1572872 | tf_op jit(solution)/shard_map/ppermute | solution.py:260
  112.6 46.8 %copy-start.4 = (f32[512]{0:T(512)S(1)}, f32[512]{0:T(512)}, u32[]{:S(2)}) copy-start(f32[512]{0:T(512)} %param.8) | copy-start | bytes 6148

commit v9 on v8

--- a/solution.py
+++ b/solution.py
@@ -138,13 +138,15 @@
 
 
 def dot3(a, b, dims):
-    a_high, a_low = split_halves(a)
+    rows = a.shape[0]
+    a_both = jnp.concatenate(split_halves(a), axis=0)
     b_high, b_low = split_halves(b)
 
     def dot(u, v):
         return lax.dot_general(u, v, (dims, ((), ())), preferred_element_type=jnp.float32)
 
-    return dot(a_high, b_high) + (dot(a_high, b_low) + dot(a_low, b_high))
+    by_high = dot(a_both, b_high)
+    return by_high[:rows] + (dot(a_both[:rows], b_low) + by_high[rows:])
 
 
 def cross_kernel(places_ref, parts_ref, weight_ref, bias_ref, upstream_ref, crossed_ref, keep_ref, give_ref):
@@ -174,7 +176,16 @@
     )(places, parts, weight, bias.reshape(1, -1), upstream)
 
 
-def row_kernel(core, near_ref, far_ref, back_ref, out_ref, halves):
+def row_sums_of(core, near_ref, mate_ref, halves, out_ref):
+    _, rows, width = out_ref.shape
+    for h in range(2):
+        chunk = slice((2 * h + core) * rows, (2 * h + core + 1) * rows)
+        both = jnp.dot(near_ref[chunk, :], halves[0], preferred_element_type=jnp.float32)
+        both = both + jnp.dot(mate_ref[chunk, :], halves[1], preferred_element_type=jnp.float32)
+        out_ref[h] = both[:, :width] + both[:, width:]
+
+
+def their_rows_kernel(near_ref, mate_ref, back_ref, out_ref, halves):
     blocks, per, width = back_ref.shape
     per = per // 2
     for b in range(blocks):
@@ -182,25 +193,33 @@
         for k in range(2):
             halves[k, b * per : (b + 1) * per, :width] = high[k * per : (k + 1) * per]
             halves[k, b * per : (b + 1) * per, width:] = low[k * per : (k + 1) * per]
-    rows = out_ref.shape[1]
-    for h in range(2):
-        chunk = slice((2 * h + core) * rows, (2 * h + core + 1) * rows)
-        both = jnp.dot(near_ref[chunk, :], halves[0], preferred_element_type=jnp.float32)
-        both = both + jnp.dot(far_ref[chunk, :], halves[1], preferred_element_type=jnp.float32)
-        out_ref[h] = both[:, :width] + both[:, width:]
-
-
-def row_sums(core, near, far, back, rows):
+    row_sums_of(1, near_ref, mate_ref, halves, out_ref)
+
+
+def their_rows(near, mate, back, rows):
     width = back.shape[2]
     return pl.pallas_call(
-        functools.partial(row_kernel, core),
-        out_shape=jax.ShapeDtypeStruct((2, rows, width), jnp.float32),
+        their_rows_kernel,
+        out_shape=(
+            jax.ShapeDtypeStruct((2, rows, width), jnp.float32),
+            jax.ShapeDtypeStruct((2, near.shape[1], 2 * width), jnp.bfloat16),
+        ),
         in_specs=[WHOLE] * 3,
-        out_specs=WHOLE,
-        scratch_shapes=[pltpu.VMEM((2, near.shape[1], 2 * width), jnp.bfloat16)],
-        compiler_params=PARAMS,
-        name="row_sums",
-    )(near, far, back)
+        out_specs=(WHOLE, WHOLE),
+        compiler_params=PARAMS,
+        name="their_rows",
+    )(near, mate, back)
+
+
+def own_rows(near, mate, halves, rows):
+    return pl.pallas_call(
+        functools.partial(row_sums_of, 0),
+        out_shape=jax.ShapeDtypeStruct((2, rows, halves.shape[2] // 2), jnp.float32),
+        in_specs=[WHOLE] * 3,
+        out_specs=WHOLE,
+        compiler_params=PARAMS,
+        name="own_rows",
+    )(near, mate, halves)
 
 
 def merge_kernel(parts_ref, out_ref):
@@ -287,10 +306,11 @@
     ids, give = lax.optimization_barrier((ids, give))
     mate_counts = count_rows(places, ids, bag, per, rows, 1)
 
-    halves = jnp.concatenate([keep, xl_mate(give)], axis=0)
-    gathered = lax.all_gather(halves, "z", axis=0, tiled=False)
-    theirs = other_core(row_sums(1, counts, mate_counts, gathered, rows))
-    mine = row_sums(0, counts, mate_counts, gathered, rows) + theirs
+    both = jnp.concatenate([keep, xl_mate(give)], axis=0)
+    gathered = lax.all_gather(both, "z", axis=0, tiled=False)
+    theirs, halves = their_rows(counts, mate_counts, gathered, rows)
+    theirs = other_core(theirs)
+    mine = own_rows(counts, mate_counts, halves, rows) + theirs
     parts = lax.all_to_all(mine.reshape(16, rows // 8, width // 2), ("xh", "y"), 0, 0, tiled=True)
     totals = lax.all_to_all(merge(parts, 16), ("xl", "y"), 0, 0, tiled=True)
     new_table, new_accum = adagrad(table, accum, totals.reshape(2, rows, width // 2))

time: 161 us -> 161 us (level)
  no operation moved by 1% of the time
where the time goes in v9:
time: 161 us; the launch traced here: 160 us
  blocking collectives  107 us (66%)
  starting transfers between devices  29.3 us (18%)
  Pallas kernels  15 us (9%)
  waiting for transfers between devices  7.22 us (4%)
    all_to_all x1, blocking collectives, body(): lax.all_to_all(partial.reshape(NZ, per, width), 'z', 0, 0, tiled=True)  35.2 us
    all_gather x1, blocking collectives, body(): gathered = lax.all_gather(both, 'z', axis=0, tiled=False)  26.2 us
    all_to_all x1, blocking collectives, body(): lax.all_to_all(mine.reshape(16, rows // 8, width // 2), ('xh', 'y'), 0, 0...  24.6 us
    all_to_all x1, blocking collectives, body(): totals = lax.all_to_all(merge(parts, 16), ('xl', 'y'), 0, 0, tiled=True)  21.3 us
    all_to_all x1, starting transfers between devices, body(): lax.all_to_all(spread(bag_ids.T, 2 * NZ), ('xl', 'z'), 0, 0, tiled=True)  17 us
    pallas_call x2, Pallas kernels, count_rows(): pl.pallas_call(functools.partial(count_kernel, bag, per, mate), out_shape...  6.72 us
    all_to_all x1, waiting for transfers between devices, body(): lax.all_to_all(spread(bag_ids.T, 2 * NZ), ('xl', 'z'), 0, 0, tiled=True)  6.33 us
    ppermute x3, starting transfers between devices, other_core(): return lax.ppermute(x, 'c', [(0, 1), (1, 0)])  6.25 us
  transfers between devices with their start and end apart: 6, of which 2 were waited for; matrix products, arithmetic and copies ran while one was open for 0% of the time, Pallas kernels for 5%

profile of v9, /device:TPU:10, one launch (start us, length us, event | category | flops | bytes accessed | tf_op | source)
XLA Modules:
  0.0 160.5 jit_solution(583279757922125131)
XLA Ops:
  0.6 3.4 %collective-permute-start.1 = (f32[512,256]{1,0:T(8,128)}, f32[512,256]{1,0:T(8,128)S(1)}, u32[]{:S(2)}, u32[]{:S(2)}) collective-permute-start(f32[512,256]{1,0:T(8,128)} %rows_ref.1), channel_id=1, source_target_pairs={{0,408},{408,0},{24,384},{384,24},{1,409},{409,1},{25,385},{385,25... | collective-permute-start | bytes 1572872 | tf_op jit(solution)/shard_map/ppermute | solution.py:287
  4.0 0.7 copy-done.3
  4.7 0.8 spread.1
  5.5 17.0 %all-to-all-start = ((s32[24,1,1280]{2,1,0:T(1,128)}), s32[24,1,1280]{2,1,0:T(1,128)S(1)}, u32[]{:S(2)}, u32[]{:S(2)}) async-start(s32[24,1,1280]{2,1,0:T(1,128)} %spread.1), calls=%async_computation | async-start | bytes 245760 | tf_op jit(solution)/shard_map/all_to_all | solution.py:297
  22.5 1.9 %collective-permute-start = (f32[512,256]{1,0:T(8,128)}, f32[512,256]{1,0:T(8,128)S(1)}, u32[]{:S(2)}, u32[]{:S(2)}) collective-permute-start(f32[512,256]{1,0:T(8,128)} %rows_ref.1), channel_id=1, source_target_pairs={{0,1},{1,0},{2,3},{3,2},{4,5},{5,4},{6,7},{7,6},{8,9},{9,8},{10,11... | collective-permute-start | bytes 1572872 | tf_op jit(solution)/shard_map/ppermute | solution.py:279
  24.5 0.0 collective-permute-done.1.far_ref
  24.5 2.4 %collective-permute-start.2 = (f32[512,256]{1,0:T(8,128)S(1)}, f32[512,256]{1,0:T(8,128)S(1)}, u32[]{:S(2)}, u32[]{:S(2)}) collective-permute-start(f32[512,256]{1,0:T(8,128)S(1)} %collective-permute-done.1.far_ref), channel_id=1, source_target_pairs={{0,1},{1,0},{2,3},{3,2},{4,5},{5,4},{6,7},{7,6},{8,9},{9,8},{10,11... | collective-permute-start | bytes 1572872 | tf_op jit(solution)/shard_map/ppermute | solution.py:279
  26.9 0.1 stack.39.places_ref
  27.0 6.3 %all-to-all-done.ids_ref = s32[24,1,1280]{2,1,0:T(1,128)S(1)} async-done(((s32[24,1,1280]{2,1,0:T(1,128)}), s32[24,1,1280]{2,1,0:T(1,128)S(1)}, u32[]{:S(2)}, u32[]{:S(2)}) %all-to-all-start) | async-done | bytes 122912 | tf_op jit(solution)/shard_map/all_to_all | solution.py:297
  33.3 3.4 %count_rows.2.counts_ref.near_ref = bf16[2048,768]{1,0:T(8,128)(2,1)S(1)} custom-call(s32[9]{0:T(128)S(1)} %stack.39.places_ref, s32[24,1,1280]{2,1,0:T(1,128)S(1)} %all-to-all-done.ids_ref), custom_call_target="tpu_custom_call" | custom-call | flops 2000000000 | tf_op jit(solution)/shard_map/count_rows/pallas_call | solution.py:103
  36.7 0.0 copy-start.1
  36.7 0.0 copy-start.2
  36.7 0.0 copy-start.5
  36.7 0.0 collective-permute-done.own_c_ref
  36.7 0.0 collective-permute-done.2.far_c_ref
  36.8 2.9 %pool.1 = f32[768,256]{1,0:T(8,128)S(1)} custom-call(s32[9]{0:T(128)S(1)} %stack.39.places_ref, bf16[2048,768]{1,0:T(8,128)(2,1)S(1)} %count_rows.2.counts_ref.near_ref, f32[512,256]{1,0:T(8,128)S(1)} %copy-done, f32[512,256]{1,0:T(8,128)S(1)} %collective-permute-done.own_c_ref, f32[512,256]{1,0:T(8,128)S(1)} %collective-permute-done.1.far_ref, ...), custom_call_target="tpu_custom_call" | custom-call | tf_op jit(solution)/shard_map/pool/pallas_call | solution.py:129
  39.6 35.2 %all_to_all.20.parts_ref = f32[12,64,256]{2,1,0:T(8,128)S(1)} all-to-all(f32[12,64,256]{2,1,0:T(8,128)S(1)} %bitcast.17), channel_id=1, replica_groups=mesh['xl'=2,'y'=8,'xh'=2,'z'=12,'c'=2] {'z'}, dimensions={0} | all-to-all | bytes 1572864 | tf_op jit(solution)/shard_map/all_to_all | solution.py:304
  74.8 1.4 cross.1
  76.2 2.7 %collective-permute-start.3 = (f32[64,128]{1,0:T(8,128)S(1)}, f32[64,128]{1,0:T(8,128)S(1)}, u32[]{:S(2)}, u32[]{:S(2)}) collective-permute-start(f32[64,128]{1,0:T(8,128)S(1)} %get-tuple-element.20), channel_id=1, source_target_pairs={{0,384},{384,0},{1,385},{385,1},{2,386},{386,2},{3,387},{387,3},{4... | collective-permute-start | bytes 98312 | tf_op jit(solution)/shard_map/ppermute | solution.py:283
  78.9 3.4 %count_rows.3.mate_ref = bf16[2048,768]{1,0:T(8,128)(2,1)S(1)} custom-call(s32[9]{0:T(128)S(1)} %stack.39.places_ref, s32[24,1,1280]{2,1,0:T(1,128)S(1)} %all-to-all-done.ids_ref), custom_call_target="tpu_custom_call" | custom-call | flops 2000000000 | tf_op jit(solution)/shard_map/count_rows/pallas_call | solution.py:103
  82.2 0.0 collective-permute-done.3
  82.3 26.2 %all-gather = f32[1536,128]{1,0:T(8,128)S(1)} all-gather(f32[128,128]{1,0:T(8,128)S(1)} %pad_maximum_fusion), channel_id=2, replica_groups=mesh['xl'=2,'y'=8,'xh'=2,'z'=12,'c'=2] {'z'}, dimensions={0}, use_global_device_ids=true | all-gather | bytes 851968 | tf_op jit(solution)/shard_map/all_gather | solution.py:310
  108.5 1.1 their_rows.1
  109.6 1.9 %collective-permute-start.4 = (f32[2,512,128]{2,1,0:T(8,128)S(1)}, f32[2,512,128]{2,1,0:T(8,128)S(1)}, u32[]{:S(2)}, u32[]{:S(2)}) collective-permute-start(f32[2,512,128]{2,1,0:T(8,128)S(1)} %get-tuple-element.22), channel_id=1, source_target_pairs={{0,1},{1,0},{2,3},{3,2},{4,5},{5,4},{6,7},{7,6},{8,9},{9,8},{10,11... | collective-permute-start | bytes 1572872 | tf_op jit(solution)/shard_map/ppermute | solution.py:279
  111.5 1.0 own_rows.1
  112.5 0.0 copy-start.4
  112.5 0.9 collective-permute-done.4
  113.4 0.1 add.28
  113.4 24.6 %all_to_all.21.parts_ref = f32[16,64,128]{2,1,0:T(8,128)S(1)} all-to-all(f32[16,64,128]{2,1,0:T(8,128)S(1)} %bitcast.23), channel_id=1, replica_groups=mesh['xl'=2,'y'=8,'xh'=2,'z'=12,'c'=2] {'xh','y'}, dimensions={0} | all-to-all | bytes 1048576 | tf_op jit(solution)/shard_map/all_to_all | solution.py:314
  138.1 0.1 merge.1
  138.1 21.3 %all_to_all.22 = f32[16,64,128]{2,1,0:T(8,128)S(1)} all-to-all(f32[16,64,128]{2,1,0:T(8,128)S(1)} %merge.1), channel_id=1, replica_groups=mesh['xl'=2,'y'=8,'xh'=2,'z'=12,'c'=2] {'xl','y'}, dimensions={0} | all-to-all | bytes 1048576 | tf_op jit(solution)/shard_map/all_to_all | solution.py:315
  159.4 1.1 adagrad.1
  (8 shorter events, 0.0 us)
Async XLA Ops:
  0.6 23.8 %collective-permute-start.1 = (f32[512,256]{1,0:T(8,128)}, f32[512,256]{1,0:T(8,128)S(1)}, u32[]{:S(2)}, u32[]{:S(2)}) collective-permute-start(f32[512,256]{1,0:T(8,128)} %rows_ref.1), channel_id=1, source_target_pairs={{0,408},{408,0},{24,384},{384,24},{1,409},{409,1},{25,385},{385,25... | collective-permute-start | bytes 1572872 | tf_op jit(solution)/shard_map/ppermute | solution.py:287
  4.0 0.7 copy-start.3
  5.5 27.8 %all-to-all-start = ((s32[24,1,1280]{2,1,0:T(1,128)}), s32[24,1,1280]{2,1,0:T(1,128)S(1)}, u32[]{:S(2)}, u32[]{:S(2)}) async-start(s32[24,1,1280]{2,1,0:T(1,128)} %spread.1), calls=%async_computation | async-start | bytes 245760 | tf_op jit(solution)/shard_map/all_to_all | solution.py:297
  22.5 14.2 %collective-permute-start = (f32[512,256]{1,0:T(8,128)}, f32[512,256]{1,0:T(8,128)S(1)}, u32[]{:S(2)}, u32[]{:S(2)}) collective-permute-start(f32[512,256]{1,0:T(8,128)} %rows_ref.1), channel_id=1, source_target_pairs={{0,1},{1,0},{2,3},{3,2},{4,5},{5,4},{6,7},{7,6},{8,9},{9,8},{10,11... | collective-permute-start | bytes 1572872 | tf_op jit(solution)/shard_map/ppermute | solution.py:279
  24.5 12.3 %collective-permute-start.2 = (f32[512,256]{1,0:T(8,128)S(1)}, f32[512,256]{1,0:T(8,128)S(1)}, u32[]{:S(2)}, u32[]{:S(2)}) collective-permute-start(f32[512,256]{1,0:T(8,128)S(1)} %collective-permute-done.1.far_ref), channel_id=1, source_target_pairs={{0,1},{1,0},{2,3},{3,2},{4,5},{5,4},{6,7},{7,6},{8,9},{9,8},{10,11... | collective-permute-start | bytes 1572872 | tf_op jit(solution)/shard_map/ppermute | solution.py:279
  27.0 9.8 %copy-start = (f32[512,256]{1,0:T(8,128)S(1)}, f32[512,256]{1,0:T(8,128)}, u32[]{:S(2)}) copy-start(f32[512,256]{1,0:T(8,128)} %rows_ref.1) | copy-start | bytes 1572868
  36.7 38.1 %copy-start.1 = (f32[256,256]{1,0:T(8,128)S(1)}, f32[256,256]{1,0:T(8,128)}, u32[]{:S(2)}) copy-start(f32[256,256]{1,0:T(8,128)} %weight_ref.1) | copy-start | bytes 786436
  36.7 38.1 %copy-start.2 = (f32[64,256]{1,0:T(8,128)S(1)}, f32[64,256]{1,0:T(8,128)}, u32[]{:S(2)}) copy-start(f32[64,256]{1,0:T(8,128)} %upstream_ref.1) | copy-start | bytes 196612
  36.7 38.1 %copy-start.5 = (f32[256]{0:T(256)S(1)}, f32[256]{0:T(256)}, u32[]{:S(2)}) copy-start(f32[256]{0:T(256)} %param.10) | copy-start | bytes 3076
  76.2 6.0 %collective-permute-start.3 = (f32[64,128]{1,0:T(8,128)S(1)}, f32[64,128]{1,0:T(8,128)S(1)}, u32[]{:S(2)}, u32[]{:S(2)}) collective-permute-start(f32[64,128]{1,0:T(8,128)S(1)} %get-tuple-element.20), channel_id=1, source_target_pairs={{0,384},{384,0},{1,385},{385,1},{2,386},{386,2},{3,387},{387,3},{4... | collective-permute-start | bytes 98312 | tf_op jit(solution)/shard_map/ppermute | solution.py:283
  109.6 3.8 %collective-permute-start.4 = (f32[2,512,128]{2,1,0:T(8,128)S(1)}, f32[2,512,128]{2,1,0:T(8,128)S(1)}, u32[]{:S(2)}, u32[]{:S(2)}) collective-permute-start(f32[2,512,128]{2,1,0:T(8,128)S(1)} %get-tuple-element.22), channel_id=1, source_target_pairs={{0,1},{1,0},{2,3},{3,2},{4,5},{5,4},{6,7},{7,6},{8,9},{9,8},{10,11... | collective-permute-start | bytes 1572872 | tf_op jit(solution)/shard_map/ppermute | solution.py:279
  112.5 46.9 %copy-start.4 = (f32[512]{0:T(512)S(1)}, f32[512]{0:T(512)}, u32[]{:S(2)}) copy-start(f32[512]{0:T(512)} %param.8) | copy-start | bytes 6148

commit v10 on v9

--- a/solution.py
+++ b/solution.py
@@ -242,36 +242,34 @@
 
 
 def adagrad_kernel(rows_ref, sums_ref, grads_ref, new_rows_ref, new_sums_ref):
-    lines, width = rows_ref.shape
+    width = rows_ref.shape[1]
     half = width // 2
-    at = (lines, lines)
+    at = (LANES, LANES)
     diagonal = lax.broadcasted_iota(jnp.int32, at, 0) == lax.broadcasted_iota(jnp.int32, at, 1)
-    sums = jnp.sum(jnp.where(diagonal, sums_ref[0], 0.0), axis=1, keepdims=True)
-    one, two = grads_ref[0], grads_ref[1]
-    fresh = sums + jnp.sum(one * one + two * two, axis=1, keepdims=True) / width
-    root = jnp.sqrt(fresh)
-    new_rows_ref[:, :half] = rows_ref[:, :half] - 0.5 * one / root
-    new_rows_ref[:, half:] = rows_ref[:, half:] - 0.5 * two / root
-    new_sums_ref[0] = jnp.sum(jnp.where(diagonal, fresh, 0.0), axis=0, keepdims=True)
+    for k in range(sums_ref.shape[0]):
+        lines = slice(k * LANES, (k + 1) * LANES)
+        sums = jnp.sum(jnp.where(diagonal, sums_ref[k], 0.0), axis=1, keepdims=True)
+        one, two = grads_ref[0, lines, :], grads_ref[1, lines, :]
+        fresh = sums + jnp.sum(one * one + two * two, axis=1, keepdims=True) / width
+        scale = 0.5 / jnp.sqrt(fresh)
+        new_rows_ref[lines, :half] = rows_ref[lines, :half] - one * scale
+        new_rows_ref[lines, half:] = rows_ref[lines, half:] - two * scale
+        new_sums_ref[k] = jnp.sum(jnp.where(diagonal, fresh, 0.0), axis=0, keepdims=True)
 
 
 def adagrad(rows, sums, grads):
-    count, width = rows.shape
-    lines = 2 * LANES
-    block = pl.BlockSpec((lines, width), lambda i: (i, 0))
-    line = pl.BlockSpec((1, 1, lines), lambda i: (i, 0, 0))
+    sums = sums.reshape(-1, 1, LANES)
     new_rows, new_sums = pl.pallas_call(
         adagrad_kernel,
         out_shape=(
             jax.ShapeDtypeStruct(rows.shape, jnp.float32),
-            jax.ShapeDtypeStruct((count // lines, 1, lines), jnp.float32),
+            jax.ShapeDtypeStruct(sums.shape, jnp.float32),
         ),
-        grid=(count // lines,),
-        in_specs=[block, line, pl.BlockSpec((2, lines, width // 2), lambda i: (0, i, 0))],
-        out_specs=(block, line),
+        in_specs=[WHOLE] * 3,
+        out_specs=(WHOLE, WHOLE),
         compiler_params=PARAMS,
         name="adagrad",
-    )(rows, sums.reshape(-1, 1, lines), grads)
+    )(rows, sums, grads)
     return new_rows, new_sums.reshape(-1)
 
 

time: 161 us -> 161 us (level)
  no operation moved by 1% of the time
where the time goes in v10:
time: 161 us; the launch traced here: 160 us
  blocking collectives  107 us (66%)
  starting transfers between devices  29.3 us (18%)
  Pallas kernels  14.9 us (9%)
  waiting for transfers between devices  7.22 us (4%)
    all_to_all x1, blocking collectives, body(): lax.all_to_all(partial.reshape(NZ, per, width), 'z', 0, 0, tiled=True)  35.2 us
    all_gather x1, blocking collectives, body(): gathered = lax.all_gather(both, 'z', axis=0, tiled=False)  26.2 us
    all_to_all x1, blocking collectives, body(): lax.all_to_all(mine.reshape(16, rows // 8, width // 2), ('xh', 'y'), 0, 0...  24.6 us
    all_to_all x1, blocking collectives, body(): totals = lax.all_to_all(merge(parts, 16), ('xl', 'y'), 0, 0, tiled=True)  21.3 us
    all_to_all x1, starting transfers between devices, body(): lax.all_to_all(spread(bag_ids.T, 2 * NZ), ('xl', 'z'), 0, 0, tiled=True)  17 us
    pallas_call x2, Pallas kernels, count_rows(): pl.pallas_call(functools.partial(count_kernel, bag, per, mate), out_shape...  6.72 us
    all_to_all x1, waiting for transfers between devices, body(): lax.all_to_all(spread(bag_ids.T, 2 * NZ), ('xl', 'z'), 0, 0, tiled=True)  6.33 us
    ppermute x3, starting transfers between devices, other_core(): return lax.ppermute(x, 'c', [(0, 1), (1, 0)])  6.25 us
  transfers between devices with their start and end apart: 6, of which 2 were waited for; matrix products, arithmetic and copies ran while one was open for 0% of the time, Pallas kernels for 5%

profile of v10, /device:TPU:10, one launch (start us, length us, event | category | flops | bytes accessed | tf_op | source)
XLA Modules:
  0.0 160.4 jit_solution(11588050919619498577)
XLA Ops:
  0.6 3.4 %collective-permute-start.1 = (f32[512,256]{1,0:T(8,128)}, f32[512,256]{1,0:T(8,128)S(1)}, u32[]{:S(2)}, u32[]{:S(2)}) collective-permute-start(f32[512,256]{1,0:T(8,128)} %rows_ref.1), channel_id=1, source_target_pairs={{0,408},{408,0},{24,384},{384,24},{1,409},{409,1},{25,385},{385,25... | collective-permute-start | bytes 1572872 | tf_op jit(solution)/shard_map/ppermute | solution.py:285
  4.0 0.7 copy-done.3
  4.7 0.8 spread.1
  5.5 17.0 %all-to-all-start = ((s32[24,1,1280]{2,1,0:T(1,128)}), s32[24,1,1280]{2,1,0:T(1,128)S(1)}, u32[]{:S(2)}, u32[]{:S(2)}) async-start(s32[24,1,1280]{2,1,0:T(1,128)} %spread.1), calls=%async_computation | async-start | bytes 245760 | tf_op jit(solution)/shard_map/all_to_all | solution.py:295
  22.5 1.9 %collective-permute-start = (f32[512,256]{1,0:T(8,128)}, f32[512,256]{1,0:T(8,128)S(1)}, u32[]{:S(2)}, u32[]{:S(2)}) collective-permute-start(f32[512,256]{1,0:T(8,128)} %rows_ref.1), channel_id=1, source_target_pairs={{0,1},{1,0},{2,3},{3,2},{4,5},{5,4},{6,7},{7,6},{8,9},{9,8},{10,11... | collective-permute-start | bytes 1572872 | tf_op jit(solution)/shard_map/ppermute | solution.py:277
  24.5 0.0 collective-permute-done.1.far_ref
  24.5 2.4 %collective-permute-start.2 = (f32[512,256]{1,0:T(8,128)S(1)}, f32[512,256]{1,0:T(8,128)S(1)}, u32[]{:S(2)}, u32[]{:S(2)}) collective-permute-start(f32[512,256]{1,0:T(8,128)S(1)} %collective-permute-done.1.far_ref), channel_id=1, source_target_pairs={{0,1},{1,0},{2,3},{3,2},{4,5},{5,4},{6,7},{7,6},{8,9},{9,8},{10,11... | collective-permute-start | bytes 1572872 | tf_op jit(solution)/shard_map/ppermute | solution.py:277
  26.9 0.1 stack.39.places_ref
  27.0 6.3 %all-to-all-done.ids_ref = s32[24,1,1280]{2,1,0:T(1,128)S(1)} async-done(((s32[24,1,1280]{2,1,0:T(1,128)}), s32[24,1,1280]{2,1,0:T(1,128)S(1)}, u32[]{:S(2)}, u32[]{:S(2)}) %all-to-all-start) | async-done | bytes 122912 | tf_op jit(solution)/shard_map/all_to_all | solution.py:295
  33.3 3.4 %count_rows.2.counts_ref.near_ref = bf16[2048,768]{1,0:T(8,128)(2,1)S(1)} custom-call(s32[9]{0:T(128)S(1)} %stack.39.places_ref, s32[24,1,1280]{2,1,0:T(1,128)S(1)} %all-to-all-done.ids_ref), custom_call_target="tpu_custom_call" | custom-call | flops 2000000000 | tf_op jit(solution)/shard_map/count_rows/pallas_call | solution.py:103
  36.7 0.0 copy-start.1
  36.7 0.0 copy-start.2
  36.7 0.0 copy-start.5
  36.7 0.0 collective-permute-done.own_c_ref
  36.7 0.0 collective-permute-done.2.far_c_ref
  36.8 2.9 %pool.1 = f32[768,256]{1,0:T(8,128)S(1)} custom-call(s32[9]{0:T(128)S(1)} %stack.39.places_ref, bf16[2048,768]{1,0:T(8,128)(2,1)S(1)} %count_rows.2.counts_ref.near_ref, f32[512,256]{1,0:T(8,128)S(1)} %copy-done, f32[512,256]{1,0:T(8,128)S(1)} %collective-permute-done.own_c_ref, f32[512,256]{1,0:T(8,128)S(1)} %collective-permute-done.1.far_ref, ...), custom_call_target="tpu_custom_call" | custom-call | tf_op jit(solution)/shard_map/pool/pallas_call | solution.py:129
  39.6 35.2 %all_to_all.20.parts_ref = f32[12,64,256]{2,1,0:T(8,128)S(1)} all-to-all(f32[12,64,256]{2,1,0:T(8,128)S(1)} %bitcast.17), channel_id=1, replica_groups=mesh['xl'=2,'y'=8,'xh'=2,'z'=12,'c'=2] {'z'}, dimensions={0} | all-to-all | bytes 1572864 | tf_op jit(solution)/shard_map/all_to_all | solution.py:302
  74.8 1.4 cross.1
  76.2 2.7 %collective-permute-start.3 = (f32[64,128]{1,0:T(8,128)S(1)}, f32[64,128]{1,0:T(8,128)S(1)}, u32[]{:S(2)}, u32[]{:S(2)}) collective-permute-start(f32[64,128]{1,0:T(8,128)S(1)} %get-tuple-element.20), channel_id=1, source_target_pairs={{0,384},{384,0},{1,385},{385,1},{2,386},{386,2},{3,387},{387,3},{4... | collective-permute-start | bytes 98312 | tf_op jit(solution)/shard_map/ppermute | solution.py:281
  78.9 3.4 %count_rows.3.mate_ref = bf16[2048,768]{1,0:T(8,128)(2,1)S(1)} custom-call(s32[9]{0:T(128)S(1)} %stack.39.places_ref, s32[24,1,1280]{2,1,0:T(1,128)S(1)} %all-to-all-done.ids_ref), custom_call_target="tpu_custom_call" | custom-call | flops 2000000000 | tf_op jit(solution)/shard_map/count_rows/pallas_call | solution.py:103
  82.2 0.0 collective-permute-done.3
  82.3 26.2 %all-gather = f32[1536,128]{1,0:T(8,128)S(1)} all-gather(f32[128,128]{1,0:T(8,128)S(1)} %pad_maximum_fusion), channel_id=2, replica_groups=mesh['xl'=2,'y'=8,'xh'=2,'z'=12,'c'=2] {'z'}, dimensions={0}, use_global_device_ids=true | all-gather | bytes 851968 | tf_op jit(solution)/shard_map/all_gather | solution.py:308
  108.5 1.1 their_rows.1
  109.6 1.9 %collective-permute-start.4 = (f32[2,512,128]{2,1,0:T(8,128)S(1)}, f32[2,512,128]{2,1,0:T(8,128)S(1)}, u32[]{:S(2)}, u32[]{:S(2)}) collective-permute-start(f32[2,512,128]{2,1,0:T(8,128)S(1)} %get-tuple-element.22), channel_id=1, source_target_pairs={{0,1},{1,0},{2,3},{3,2},{4,5},{5,4},{6,7},{7,6},{8,9},{9,8},{10,11... | collective-permute-start | bytes 1572872 | tf_op jit(solution)/shard_map/ppermute | solution.py:277
  111.5 1.0 own_rows.1
  112.5 0.0 copy-start.4
  112.5 0.9 collective-permute-done.4
  113.4 0.1 add.28
  113.4 24.6 %all_to_all.21.parts_ref = f32[16,64,128]{2,1,0:T(8,128)S(1)} all-to-all(f32[16,64,128]{2,1,0:T(8,128)S(1)} %bitcast.23), channel_id=1, replica_groups=mesh['xl'=2,'y'=8,'xh'=2,'z'=12,'c'=2] {'xh','y'}, dimensions={0} | all-to-all | bytes 1048576 | tf_op jit(solution)/shard_map/all_to_all | solution.py:312
  138.1 0.1 merge.1
  138.1 21.3 %all_to_all.22 = f32[16,64,128]{2,1,0:T(8,128)S(1)} all-to-all(f32[16,64,128]{2,1,0:T(8,128)S(1)} %merge.1), channel_id=1, replica_groups=mesh['xl'=2,'y'=8,'xh'=2,'z'=12,'c'=2] {'xl','y'}, dimensions={0} | all-to-all | bytes 1048576 | tf_op jit(solution)/shard_map/all_to_all | solution.py:313
  159.4 1.1 adagrad.1
  (8 shorter events, 0.0 us)
Async XLA Ops:
  0.6 23.8 %collective-permute-start.1 = (f32[512,256]{1,0:T(8,128)}, f32[512,256]{1,0:T(8,128)S(1)}, u32[]{:S(2)}, u32[]{:S(2)}) collective-permute-start(f32[512,256]{1,0:T(8,128)} %rows_ref.1), channel_id=1, source_target_pairs={{0,408},{408,0},{24,384},{384,24},{1,409},{409,1},{25,385},{385,25... | collective-permute-start | bytes 1572872 | tf_op jit(solution)/shard_map/ppermute | solution.py:285
  4.0 0.7 copy-start.3
  5.5 27.8 %all-to-all-start = ((s32[24,1,1280]{2,1,0:T(1,128)}), s32[24,1,1280]{2,1,0:T(1,128)S(1)}, u32[]{:S(2)}, u32[]{:S(2)}) async-start(s32[24,1,1280]{2,1,0:T(1,128)} %spread.1), calls=%async_computation | async-start | bytes 245760 | tf_op jit(solution)/shard_map/all_to_all | solution.py:295
  22.5 14.2 %collective-permute-start = (f32[512,256]{1,0:T(8,128)}, f32[512,256]{1,0:T(8,128)S(1)}, u32[]{:S(2)}, u32[]{:S(2)}) collective-permute-start(f32[512,256]{1,0:T(8,128)} %rows_ref.1), channel_id=1, source_target_pairs={{0,1},{1,0},{2,3},{3,2},{4,5},{5,4},{6,7},{7,6},{8,9},{9,8},{10,11... | collective-permute-start | bytes 1572872 | tf_op jit(solution)/shard_map/ppermute | solution.py:277
  24.5 12.3 %collective-permute-start.2 = (f32[512,256]{1,0:T(8,128)S(1)}, f32[512,256]{1,0:T(8,128)S(1)}, u32[]{:S(2)}, u32[]{:S(2)}) collective-permute-start(f32[512,256]{1,0:T(8,128)S(1)} %collective-permute-done.1.far_ref), channel_id=1, source_target_pairs={{0,1},{1,0},{2,3},{3,2},{4,5},{5,4},{6,7},{7,6},{8,9},{9,8},{10,11... | collective-permute-start | bytes 1572872 | tf_op jit(solution)/shard_map/ppermute | solution.py:277
  27.0 9.8 %copy-start = (f32[512,256]{1,0:T(8,128)S(1)}, f32[512,256]{1,0:T(8,128)}, u32[]{:S(2)}) copy-start(f32[512,256]{1,0:T(8,128)} %rows_ref.1) | copy-start | bytes 1572868
  36.7 38.1 %copy-start.1 = (f32[256,256]{1,0:T(8,128)S(1)}, f32[256,256]{1,0:T(8,128)}, u32[]{:S(2)}) copy-start(f32[256,256]{1,0:T(8,128)} %weight_ref.1) | copy-start | bytes 786436
  36.7 38.1 %copy-start.2 = (f32[64,256]{1,0:T(8,128)S(1)}, f32[64,256]{1,0:T(8,128)}, u32[]{:S(2)}) copy-start(f32[64,256]{1,0:T(8,128)} %upstream_ref.1) | copy-start | bytes 196612
  36.7 38.1 %copy-start.5 = (f32[256]{0:T(256)S(1)}, f32[256]{0:T(256)}, u32[]{:S(2)}) copy-start(f32[256]{0:T(256)} %param.10) | copy-start | bytes 3076
  76.2 6.0 %collective-permute-start.3 = (f32[64,128]{1,0:T(8,128)S(1)}, f32[64,128]{1,0:T(8,128)S(1)}, u32[]{:S(2)}, u32[]{:S(2)}) collective-permute-start(f32[64,128]{1,0:T(8,128)S(1)} %get-tuple-element.20), channel_id=1, source_target_pairs={{0,384},{384,0},{1,385},{385,1},{2,386},{386,2},{3,387},{387,3},{4... | collective-permute-start | bytes 98312 | tf_op jit(solution)/shard_map/ppermute | solution.py:281
  109.6 3.8 %collective-permute-start.4 = (f32[2,512,128]{2,1,0:T(8,128)S(1)}, f32[2,512,128]{2,1,0:T(8,128)S(1)}, u32[]{:S(2)}, u32[]{:S(2)}) collective-permute-start(f32[2,512,128]{2,1,0:T(8,128)S(1)} %get-tuple-element.22), channel_id=1, source_target_pairs={{0,1},{1,0},{2,3},{3,2},{4,5},{5,4},{6,7},{7,6},{8,9},{9,8},{10,11... | collective-permute-start | bytes 1572872 | tf_op jit(solution)/shard_map/ppermute | solution.py:277
  112.5 46.9 %copy-start.4 = (f32[512]{0:T(512)S(1)}, f32[512]{0:T(512)}, u32[]{:S(2)}) copy-start(f32[512]{0:T(512)} %param.8) | copy-start | bytes 6148
